TPU v7x, 256 devices: a whole 4x4x8 slice. The times are simulated.
256 devices in a mesh: batch: 8 (over z), ctx: 32 (over x, y, core).
Axes of the slice: x: 4, y: 4, z: 8, core: 2. Of those that a mesh axis runs over, the one named last changes fastest.
Arguments:
- latent_cache: bfloat16 [64, 32768, 576], P('batch', 'ctx'), parts along dimension 0, may hold values from -8 to 8
- queries: bfloat16 [64, 4, 64, 576], P('batch', None, 'ctx'), parts along dimension 0, may hold values from -60 to 60
- lengths: int32 [64], P('batch'), parts along dimension 0, may hold values from 8192 to 32768, as said below
- positions: int32 [64], P('batch'), parts along dimension 0, may hold values from 0 to 32767
- value_up: bfloat16 [64, 512, 128], P('ctx'), may hold values from -0.25 to 0.25
- out_proj: bfloat16 [8192, 7168], P('ctx'), may hold values from -0.25 to 0.25
Outputs:
- attended: bfloat16 [64, 4, 7168], P('batch', None, 'ctx'), parts along dimension 0
There are 8 independent parts, one for each index of `batch`. A program takes and returns all parts, laid end to end along the dimension named above; an argument that names none is the same for every part. Nothing has to cross between parts.
Inputs may be any that keep to these rules, and one draw needn't show every extreme that they name: `lengths`: one row of every part has the full length 32768.
All inputs are finite; a program needn't handle non-finite values.
Results may differ from a plain program's by a relative error of at most 0.018.
Values may be sent and summed in bfloat16 or wider, within the bound.
No kernel may reach another device: no remote copies, remote signals or barrier semaphores. Data moves between devices by JAX's collectives and lax.ppermute only.
A program may use at most 320 MiB of HBM per device.

v0:
```python
import math

import jax
import jax.numpy as jnp
from jax import lax
from jax.sharding import PartitionSpec as P

ROPE = 64
NOPE = 128


def rotate(queries, positions, latent_width):
    half_rope = (queries.shape[-1] - latent_width) // 2
    new_count = queries.shape[1]
    exponent = jnp.arange(half_rope, dtype=jnp.float32) * (-2.0 / (2 * half_rope))
    frequency = jnp.power(jnp.float32(50000.0), exponent)
    token_place = positions[:, None] + jnp.arange(new_count, dtype=jnp.int32)[None, :]
    angles = token_place.astype(jnp.float32)[:, :, None, None] * frequency
    cosine = jnp.cos(angles)
    sine_term = jnp.sin(angles)
    latent = queries[..., :latent_width].astype(jnp.float32)
    first_half = queries[..., latent_width : latent_width + half_rope].astype(jnp.float32)
    second_half = queries[..., latent_width + half_rope :].astype(jnp.float32)
    turned = jnp.concatenate(
        [
            latent,
            first_half * cosine - second_half * sine_term,
            second_half * cosine + first_half * sine_term,
        ],
        axis=-1,
    )
    return turned.astype(jnp.bfloat16)


def body(latent_cache, queries, lengths, positions, value_up, out_proj):
    row_count, context_dev, full_width = latent_cache.shape
    new_count = queries.shape[1]
    heads_dev = queries.shape[2]
    latent_width = value_up.shape[1]
    shard = lax.axis_index("ctx")
    shard_count = lax.axis_size("ctx")
    turned = rotate(queries, positions, latent_width)
    whole_query = lax.all_gather(turned, "ctx", axis=2, tiled=True)
    score_scale = 1.0 / math.sqrt(NOPE + ROPE)
    scores = (
        jnp.einsum("bqhc,btc->bqht", whole_query, latent_cache, preferred_element_type=jnp.float32)
        * score_scale
    )
    first_index = shard * context_dev
    token_index = first_index + jnp.arange(context_dev, dtype=jnp.int32)
    limit = lengths[:, None] - new_count + 1 + jnp.arange(new_count, dtype=jnp.int32)[None, :]
    visible = (token_index[None, None, :] < limit[:, :, None])[:, :, None, :]
    scores = jnp.where(visible, scores, -1e30)
    local_max = jnp.max(scores, axis=-1)
    weights = jnp.where(visible, jnp.exp(scores - local_max[..., None]), 0.0)
    local_sum = jnp.sum(weights, axis=-1)
    rounded = weights.astype(jnp.bfloat16)
    local_out = jnp.einsum(
        "bqht,btc->bqhc",
        rounded,
        latent_cache[:, :, :latent_width],
        preferred_element_type=jnp.float32,
    )
    top = lax.pmax(local_max, "ctx")
    factor = jnp.exp(local_max - top)
    total, summed = (
        lax.psum_scatter(factor * local_sum, "ctx", scatter_dimension=2, tiled=True),
        lax.psum_scatter(factor[..., None] * local_out, "ctx", scatter_dimension=2, tiled=True),
    )
    latent_heads = (summed / total[..., None]).astype(jnp.bfloat16)
    head_values = jnp.einsum(
        "bqhc,hcv->bqhv", latent_heads, value_up, preferred_element_type=jnp.float32
    ).astype(jnp.bfloat16)
    flat = head_values.reshape(row_count * new_count, heads_dev * value_up.shape[2])
    partial_terms = jnp.dot(flat, out_proj, preferred_element_type=jnp.float32)
    partial_terms = partial_terms.reshape(row_count, new_count, out_proj.shape[1])
    full_sum = lax.psum(partial_terms, "ctx")
    width_dev = out_proj.shape[1] // shard_count
    result = lax.dynamic_slice_in_dim(full_sum, shard * width_dev, width_dev, 2)
    return result.astype(jnp.bfloat16)


def solution(mesh):
    in_specs = (
        P("batch", "ctx", None),
        P("batch", None, "ctx", None),
        P("batch"),
        P("batch"),
        P("ctx", None, None),
        P("ctx", None),
    )
    out_specs = P("batch", None, "ctx")
    return jax.shard_map(body, mesh=mesh, in_specs=in_specs, out_specs=out_specs, check_vma=False)
```

profile of v0, /device:TPU:1, one launch (start us, length us, event | category | flops | bytes accessed | tf_op | source)
XLA Modules:
  0.0 488.4 jit_solution(7932486803855410408)
XLA Ops:
  6.6 0.9 fusion.34
  7.4 0.9 slice.12
  8.3 0.7 add_convert_fusion
  9.0 0.1 multiply_cosine_fusion
  9.2 0.7 pad_maximum_fusion
  9.9 0.0 all-gather.2.cloned.1.call-update
  9.9 0.0 reduce-scatter.2.cloned.1.call-start
  10.0 0.7 broadcast_add_fusion
  10.6 0.1 iota_add_fusion
  10.7 0.1 broadcast_compare_fusion
  10.8 53.0 %all-gather.2.cloned.1.call-done = bf16[8,4,64,576]{3,0,1,2:T(8,128)(2,1)} async-done(((bf16[8,4,2,576]{3,0,1,2:T(8,128)(2,1)}), bf16[8,4,64,576]{3,0,1,2:T(8,128)(2,1)}) %all-gather.2.cloned.1.call-update) | async-done | bytes 2359312 | tf_op jit(solution)/shard_map/all_gather | solution.py:43
  63.8 12.0 %fusion.5 = (f32[8,4,64]{2,1,0:T(4,128)S(1)}, f32[8,4,64,1024]{3,2,1,0:T(8,128)}) fusion(pred[8,4,1024]{2,1,0:T(4,128)(4,1)S(1)} %broadcast_compare_fusion, bf16[8,1024,576]{1,2,0:T(8,128)(2,1)} %param.6, bf16[8,4,64,576]{3,0,1,2:T(8,128)(2,1)} %all-gather.2.cloned.1.call-done), kind=kOutput, calls=%fused_computation.7 | convolution fusion | flops 2422208512 | bytes 20226048 | tf_op jit(solution)/shard_map/bqhc,btc->bqht/dot_general | solution.py:46
  75.8 121.1 %pmax.7 = f32[8,4,64]{2,1,0:T(4,128)S(1)} all-reduce(f32[8,4,64]{2,1,0:T(4,128)S(1)} %get-tuple-element.13), channel_id=1, replica_groups=mesh['batch'=8,'ctx'=32] {'ctx'}, use_global_device_ids=true, to_apply=%region_1.2 | all-reduce | flops 2048 | bytes 16384 | tf_op jit(solution)/shard_map/pmax | solution.py:64
  196.9 4.9 fusion.6
  201.8 10.6 %broadcast_multiply_fusion = f32[8,4,64,512]{3,2,1,0:T(8,128)} fusion(f32[8,4,64]{2,1,0:T(4,128)S(1)} %bitcast.39, bf16[8,1024,576]{1,2,0:T(8,128)(2,1)} %param.6, f32[8,4,64,1024]{3,2,1,0:T(8,128)} %get-tuple-element.14, f32[8,4,64]{2,1,0:T(4,128)S(1)} %get-tuple-element.13, pred[8,4,1024]{2,1,0:T(4,128)(4,1)S(1)} %broadcast_compare_fusion), kind=kOutput, calls=%fused_computation.18 | convolution fusion | flops 2159017984 | bytes 21020672 | tf_op jit(solution)/shard_map/bqht,btc->bqhc/dot_general | solution.py:58
  212.4 6.6 %copy.30 = f32[8,4,64,512]{3,0,1,2:T(8,128)} copy(f32[8,4,64,512]{3,2,1,0:T(8,128)} %broadcast_multiply_fusion) | data formatting | bytes 8388608 | tf_op jit(solution)/shard_map/mul | solution.py:68
  218.9 0.6 dynamic-slice
  220.2 0.1 copy.31
  220.3 124.2 %all-reduce = f32[8,4,64]{0,1,2:T(4,128)S(1)} all-reduce(f32[8,4,64]{0,1,2:T(4,128)S(1)} %copy.31), channel_id=3, replica_groups=mesh['batch'=8,'ctx'=32] {'ctx'}, use_global_device_ids=true, to_apply=%region_4.5.clone | all-reduce | flops 2048 | bytes 16384
  344.5 1.1 fusion.21
  345.6 2.8 fusion.14
  348.4 132.4 %all-reduce.2 = bf16[8,4,7168]{2,0,1:T(8,128)(2,1)S(1)} all-reduce(f32[8,4,7168]{2,0,1:T(8,128)S(1)} %fusion.14), channel_id=1, replica_groups=mesh['batch'=8,'ctx'=32] {'ctx'}, use_global_device_ids=true, to_apply=%region_5.6 | all-reduce | flops 229376 | bytes 1376256 | tf_op jit(solution)/shard_map/psum | solution.py:77
  480.9 0.1 dynamic-slice_convert_fusion
  480.9 0.6 copy.33
  (13 shorter events, 0.1 us)
Async XLA Ops:
  6.5 338.0 %copy-start = (bf16[2,512,128]{2,1,0:T(8,128)(2,1)S(1)}, bf16[2,512,128]{2,1,0:T(8,128)(2,1)}, u32[]{:S(2)}) copy-start(bf16[2,512,128]{2,1,0:T(8,128)(2,1)} %param.10) | copy-start | bytes 786436
  6.5 57.3 %all-gather.2.cloned.1.call-start = ((), (), s32[]{:S(2)}) async-start(), calls=%async_computation.1 | async-start | bytes 2703360 | tf_op jit(solution)/shard_map/all_gather | solution.py:43
  9.9 334.6 %reduce-scatter.2.cloned.1.call-start = ((), (), s32[]{:S(2)}) async-start(), calls=%async_computation.2 | async-start | bytes 4325376 | tf_op jit(solution)/shard_map/reduce_scatter | solution.py:68
  212.4 6.6 %copy-start.1 = (u32[256]{0:T(256)S(1)}, u32[256]{0:T(256)}, u32[]{:S(2)}) copy-start(u32[256]{0:T(256)} %constant.33) | copy-start | bytes 3076
Sparse Core Ops, SparseCore 0:
  10.0 53.7 all-gather.1
  219.1 89.4 reduce-scatter.1
where the time goes:
time: 493 us; the launch traced here: 488 us
  blocking collectives  378 us (77%)
  waiting for transfers between devices  53 us (11%)
  matrix products  26.5 us (5%)
  between operations  14.1 us (3%)
  local copies, waits for them, and re-layouts  9.77 us (2%)
  other arithmetic  7.27 us (1%)
    psum x1, blocking collectives, body(): full_sum = lax.psum(partial_terms, 'ctx')  132 us
    unnamed x1, blocking collectives  124 us
    pmax x1, blocking collectives, body(): top = lax.pmax(local_max, 'ctx')  121 us
    all_gather x1, waiting for transfers between devices, body(): whole_query = lax.all_gather(turned, 'ctx', axis=2, tiled=True)  53 us
    dot_general x1, matrix products, body(): jnp.einsum('bqhc,btc->bqht', whole_query, latent_cache, preferred_element...  12 us
    dot_general x1, matrix products, body(): jnp.einsum('bqht,btc->bqhc', rounded, latent_cache[:, :, :latent_width],...  10.6 us
  transfers between devices with their start and end apart: 2, of which 1 were waited for; matrix products, arithmetic and copies ran while one was open for 0% of the time, Pallas kernels for 0%

commit v1 on v0

v1 whole, which is shorter than its diff:
```python
import functools
import math

import jax
import jax.numpy as jnp
from jax import lax
from jax.experimental import pallas as pl
from jax.experimental.pallas import tpu as pltpu
from jax.sharding import PartitionSpec as P

ROPE = 64
NOPE = 128
LANES = 128
POWER = math.log2(math.e) / math.sqrt(NOPE + ROPE)
HIDDEN = -1e30
LEAST = -1e29


def angle_terms(positions, new_count, repeats):
    half_rope = ROPE // 2
    exponent = jnp.arange(half_rope, dtype=jnp.float32) * (-2.0 / ROPE)
    frequency = jnp.power(jnp.float32(50000.0), exponent)
    token_place = positions[:, None] + jnp.arange(new_count, dtype=jnp.int32)[None, :]
    angles = token_place.astype(jnp.float32)[:, :, None] * frequency
    cosine, sine = jnp.cos(angles), jnp.sin(angles)
    cosines = jnp.concatenate([cosine, cosine], axis=-1)
    sines = jnp.concatenate([-sine, sine], axis=-1)
    return jnp.tile(cosines, (1, repeats, 1)), jnp.tile(sines, (1, repeats, 1))


def split_stat(value, lane):
    high = value.astype(jnp.bfloat16).astype(jnp.float32)
    rest = value - high
    middle = rest.astype(jnp.bfloat16).astype(jnp.float32)
    low = rest - middle
    spot = lane % (LANES // 2)
    return jnp.where(spot == 0, high, jnp.where(spot == 1, middle, low))


def join_stat(tile, pair):
    at = pair * (LANES // 2)
    return tile[..., at : at + 1] + tile[..., at + 1 : at + 2] + tile[..., at + 2 : at + 3]


def attend_kernel(half_ref, first_ref, lengths_ref, cache_ref, query_ref, cos_ref, sin_ref, out_ref, *, new_count):
    pair = pl.program_id(0)
    peers, sixteen, full = query_ref.shape
    group = sixteen // 2
    latent = full - ROPE
    count = peers * group
    context = cache_ref.shape[1]
    column_groups = latent // LANES
    gathered = query_ref[...].astype(jnp.float32)
    place = first_ref[0] + lax.broadcasted_iota(jnp.int32, (count, context), 1)
    token = lax.broadcasted_iota(jnp.int32, (count, context), 0) % new_count
    outs, stats = [], []
    for row in range(2):
        query = gathered[:, row * group : (row + 1) * group, :]
        rope = query[:, :, latent:]
        swapped = jnp.concatenate([rope[:, :, ROPE // 2 :], rope[:, :, : ROPE // 2]], axis=-1)
        turned = rope * cos_ref[row][None] + swapped * sin_ref[row][None]
        query = jnp.concatenate([query[:, :, :latent], turned], axis=-1)
        query = query.reshape(count, full).astype(jnp.bfloat16)
        keys = cache_ref[row]
        scores = lax.dot_general(query, keys, (((1,), (1,)), ((), ())), preferred_element_type=jnp.float32)
        length = lengths_ref[half_ref[0] * 4 + pair * 2 + row]
        scores = jnp.where(place < length - new_count + 1 + token, scores, HIDDEN)
        top = jnp.maximum(jnp.max(scores, axis=-1, keepdims=True), LEAST)
        weights = jnp.exp2((scores - top) * POWER)
        total = jnp.sum(weights, axis=-1, keepdims=True)
        out = jnp.dot(weights.astype(jnp.bfloat16), keys[:, :latent], preferred_element_type=jnp.float32)
        seen = total > 0.0
        safe = jnp.where(seen, total, 1.0)
        out = out * (1.0 / safe)
        stat = jnp.where(seen, top * POWER + jnp.log2(safe), HIDDEN)
        outs.append(out.reshape(peers, group, latent))
        stats.append(jnp.broadcast_to(stat, (count, LANES)).reshape(peers, group, LANES))
    both = jnp.concatenate(outs, axis=1).astype(jnp.bfloat16)
    for g in range(column_groups):
        at = pl.multiple_of(g * 2 * sixteen + pair * sixteen, sixteen)
        out_ref[:, pl.ds(at, sixteen), :] = both[:, :, g * LANES : (g + 1) * LANES]
    stat = jnp.concatenate(stats, axis=1)
    lane = lax.broadcasted_iota(jnp.int32, stat.shape, 2)
    packed = split_stat(stat, lane).astype(jnp.bfloat16)
    at = column_groups * 2 * sixteen

    @pl.when(pair == 0)
    def _():
        out_ref[:, at : at + sixteen, :] = packed

    @pl.when(pair == 1)
    def _():
        out_ref[:, at : at + sixteen, :] = jnp.where(
            lane < LANES // 2, out_ref[:, at : at + sixteen, :].astype(jnp.float32), packed.astype(jnp.float32)
        ).astype(jnp.bfloat16)


def attend(half, first, lengths, cache, query, cosines, sines, new_count):
    peers, depth, full = query.shape
    sixteen = depth // 2
    context = cache.shape[1]
    group = sixteen // 2
    latent = full - ROPE
    rows_out = latent // LANES * depth + sixteen
    count = peers * group
    return pl.pallas_call(
        functools.partial(attend_kernel, new_count=new_count),
        out_shape=jax.ShapeDtypeStruct((peers, rows_out, LANES), jnp.bfloat16),
        grid_spec=pltpu.PrefetchScalarGridSpec(
            num_scalar_prefetch=3,
            grid=(2,),
            in_specs=[
                pl.BlockSpec((2, context, full), lambda p, half, *_: (half[0] * 2 + p, 0, 0)),
                pl.BlockSpec((peers, sixteen, full), lambda p, *_: (0, p, 0)),
                pl.BlockSpec((2, group, ROPE), lambda p, half, *_: (half[0] * 2 + p, 0, 0)),
                pl.BlockSpec((2, group, ROPE), lambda p, half, *_: (half[0] * 2 + p, 0, 0)),
            ],
            out_specs=pl.BlockSpec((peers, rows_out, LANES), lambda p, *_: (0, 0, 0)),
        ),
        compiler_params=pltpu.CompilerParams(vmem_limit_bytes=40 * 1024 * 1024),
        cost_estimate=pl.CostEstimate(
            flops=4 * count * context * (full + latent) * 2,
            bytes_accessed=4 * context * full * 2 + 4 * peers * rows_out * LANES,
            transcendentals=4 * count * context,
        ),
        name="attend",
    )(half, first, lengths, cache, query, cosines, sines)


def merge_kernel(left_ref, right_ref, out_ref):
    rows_out = out_ref.shape[1]
    sixteen = 16
    groups = (rows_out - sixteen) // (2 * sixteen)
    at = rows_out - sixteen
    left_stat = left_ref[:, at:, :].astype(jnp.float32)
    right_stat = right_ref[:, at:, :].astype(jnp.float32)
    lane = lax.broadcasted_iota(jnp.int32, left_stat.shape, 2)
    packed = []
    for pair in range(2):
        left, right = join_stat(left_stat, pair), join_stat(right_stat, pair)
        top = jnp.maximum(left, right)
        left_weight, right_weight = jnp.exp2(left - top), jnp.exp2(right - top)
        total = left_weight + right_weight
        packed.append(split_stat(jnp.broadcast_to(top + jnp.log2(total), left_stat.shape), lane))
        scale = 1.0 / total
        left_weight, right_weight = left_weight * scale, right_weight * scale
        for g in range(groups):
            rows = slice(g * 2 * sixteen + pair * sixteen, g * 2 * sixteen + pair * sixteen + sixteen)
            out_ref[:, rows, :] = (
                left_ref[:, rows, :].astype(jnp.float32) * left_weight
                + right_ref[:, rows, :].astype(jnp.float32) * right_weight
            ).astype(jnp.bfloat16)
    out_ref[:, at:, :] = jnp.where(lane < LANES // 2, packed[0], packed[1]).astype(jnp.bfloat16)


def merge(left, right):
    peers, rows_out, lanes = left.shape
    step = peers // 4
    spec = pl.BlockSpec((step, rows_out, lanes), lambda i: (i, 0, 0))
    return pl.pallas_call(
        merge_kernel,
        out_shape=jax.ShapeDtypeStruct(left.shape, left.dtype),
        grid=(4,),
        in_specs=[spec, spec],
        out_specs=spec,
        compiler_params=pltpu.CompilerParams(vmem_limit_bytes=16 * 1024 * 1024),
        name="merge",
    )(left, right)


def project_kernel(parts_ref, up_ref, proj_ref, out_ref, flat_ref, *, new_count):
    sixteen = 16
    peers, rows_out, lanes = parts_ref.shape
    at = rows_out - sixteen
    groups = at // (2 * sixteen)
    heads, _, width = up_ref.shape

    @pl.when(pl.program_id(0) == 0)
    def _():
        blocks = []
        for half in range(2):
            chosen = [2 * k + 1 - half for k in range(peers // 2)]
            stat_tiles = [parts_ref[k, at:, :].astype(jnp.float32) for k in chosen]
            for pair in range(2):
                stats = [join_stat(tile, pair) for tile in stat_tiles]
                top = functools.reduce(jnp.maximum, stats)
                weights = [jnp.exp2(stat - top) for stat in stats]
                scale = 1.0 / functools.reduce(jnp.add, weights)
                sums = []
                for g in range(groups):
                    start = g * 2 * sixteen + pair * sixteen
                    acc = None
                    for k, weight in zip(chosen, weights):
                        term = parts_ref[k, start : start + sixteen, :].astype(jnp.float32) * weight
                        acc = term if acc is None else acc + term
                    sums.append(acc * scale)
                blocks.append(jnp.concatenate(sums, axis=-1))
        latent = jnp.concatenate(blocks, axis=0).astype(jnp.bfloat16)
        count = latent.shape[0]
        out_row = lax.broadcasted_iota(jnp.int32, (count // heads, count), 0)
        in_row = lax.broadcasted_iota(jnp.int32, (count // heads, count), 1)
        base = (out_row // new_count) * (new_count * heads) + out_row % new_count
        for head in range(heads):
            pick = jnp.where(in_row == base + head * new_count, 1.0, 0.0).astype(jnp.bfloat16)
            own = jnp.dot(pick, latent, preferred_element_type=jnp.float32).astype(jnp.bfloat16)
            values = jnp.dot(own, up_ref[head], preferred_element_type=jnp.float32)
            flat_ref[:, head * width : (head + 1) * width] = values.astype(jnp.bfloat16)

    out_ref[...] = jnp.dot(flat_ref[...], proj_ref[...], preferred_element_type=jnp.float32).astype(jnp.bfloat16)


def project(parts, value_up, out_proj, new_count):
    peers, rows_out, lanes = parts.shape
    heads, latent, width = value_up.shape
    depth, columns = out_proj.shape
    tokens = 32
    steps = 4
    block = columns // steps
    return pl.pallas_call(
        functools.partial(project_kernel, new_count=new_count),
        out_shape=jax.ShapeDtypeStruct((tokens, columns), jnp.bfloat16),
        grid=(steps,),
        in_specs=[
            pl.BlockSpec((peers, rows_out, lanes), lambda i: (0, 0, 0)),
            pl.BlockSpec((heads, latent, width), lambda i: (0, 0, 0)),
            pl.BlockSpec((depth, block), lambda i: (0, i)),
        ],
        out_specs=pl.BlockSpec((tokens, block), lambda i: (0, i)),
        scratch_shapes=[pltpu.VMEM((tokens, depth), jnp.bfloat16)],
        compiler_params=pltpu.CompilerParams(vmem_limit_bytes=24 * 1024 * 1024),
        name="project",
    )(parts, value_up, out_proj)


def body(latent_cache, queries, lengths, positions, value_up, out_proj):
    row_count, context_dev, full = latent_cache.shape
    new_count, heads_dev = queries.shape[1], queries.shape[2]
    shard = lax.axis_index("ctx")
    peers = lax.axis_size("ctx")
    core = shard % 2
    partners = [(i, i ^ 1) for i in range(peers)]
    depth = row_count // 2 * new_count * heads_dev
    own = queries.transpose(0, 2, 1, 3).reshape(1, 2, depth, full)
    own = jnp.broadcast_to(own, (peers // 2, 2, depth, full)).reshape(peers, depth, full)
    here = lax.all_to_all(own, "ctx", 0, 0, tiled=True)
    there = lax.ppermute(here, "ctx", partners)
    cosines, sines = angle_terms(positions, new_count, heads_dev)
    first = (shard * context_dev).astype(jnp.int32).reshape(1)
    core = core.astype(jnp.int32).reshape(1)
    sent = attend(core, first, lengths, latent_cache, here, cosines, sines, new_count)
    came = lax.ppermute(sent, "ctx", partners)
    kept = attend(1 - core, first, lengths, latent_cache, there, cosines, sines, new_count)
    merged = merge(kept, came)
    parts = lax.all_to_all(merged, "ctx", 0, 0, tiled=True)
    terms = project(parts, value_up, out_proj, new_count)
    width = out_proj.shape[1] // peers
    terms = terms.reshape(row_count * new_count, peers, width).transpose(1, 0, 2)
    terms = lax.all_to_all(terms, "ctx", 0, 0, tiled=True)
    result = jnp.sum(terms.astype(jnp.float32), axis=0).astype(jnp.bfloat16)
    return result.reshape(row_count, new_count, width)


def solution(mesh):
    in_specs = (
        P("batch", "ctx", None),
        P("batch", None, "ctx", None),
        P("batch"),
        P("batch"),
        P("ctx", None, None),
        P("ctx", None),
    )
    out_specs = P("batch", None, "ctx")
    return jax.shard_map(body, mesh=mesh, in_specs=in_specs, out_specs=out_specs, check_vma=False)
```

time: 493 us -> 92.7 us (0.19)
  blocking collectives: 378 us -> 37.9 us
  waiting for transfers between devices: 53 us -> 5.32 us
  matrix products: 26.5 us -> 0 us
  Pallas kernels: 0 us -> 14.7 us
  local copies, waits for them, and re-layouts: 9.77 us -> 24.3 us
  between operations: 14.1 us -> 0.15 us
  starting transfers between devices: 0.04 us -> 9.1 us
  other arithmetic: 7.27 us -> 0.46 us
    psum x1 -> x0, blocking collectives: 132 us -> none  [body(): full_sum = lax.psum(partial_terms, 'ctx')]
    unnamed x1 -> x0, blocking collectives: 124 us -> none
    pmax x1 -> x0, blocking collectives: 121 us -> none  [body(): top = lax.pmax(local_max, 'ctx')]
    all_gather x1 -> x0, waiting for transfers between devices: 53 us -> none  [body(): whole_query = lax.all_gather(turned, 'ctx', axis=2, tiled=True)]
    all_to_all x0 -> x2, blocking collectives: none -> 37.9 us  [the longest x1 22.8 us: body(): parts = lax.all_to_all(merged, 'ctx', 0, 0, tiled=True)]
    dot_general x4 -> x0, matrix products: 26.5 us -> none  [the longest x1 12 us: body(): jnp.einsum('bqhc,btc->bqht', whole_query, latent_cache, preferred_element...]
    unnamed x7 -> x17, local copies, waits for them, and re-layouts: 0.62 us -> 20.4 us
    pallas_call x0 -> x4, Pallas kernels: none -> 14.7 us  [the longest x2 11.1 us: attend(): pl.pallas_call(functools.partial(attend_kernel, new_count=new_count), out...]
  transfers between devices with their start and end apart: 2 -> 3, of which waited for: 1 -> 1; matrix products, arithmetic and copies ran while one was open for 0% -> 16% of each run, Pallas kernels for 0% -> 12%
where the time goes in v1:
time: 92.7 us; the launch traced here: 92 us
  blocking collectives  37.9 us (41%)
  local copies, waits for them, and re-layouts  24.3 us (26%)
  Pallas kernels  14.7 us (16%)
  starting transfers between devices  9.1 us (10%)
  waiting for transfers between devices  5.32 us (6%)
    all_to_all x1, blocking collectives, body(): parts = lax.all_to_all(merged, 'ctx', 0, 0, tiled=True)  22.8 us
    unnamed x17, local copies, waits for them, and re-layouts  20.4 us
    all_to_all x1, blocking collectives, body(): terms = lax.all_to_all(terms, 'ctx', 0, 0, tiled=True)  15.2 us
    pallas_call x2, Pallas kernels, attend(): pl.pallas_call(functools.partial(attend_kernel, new_count=new_count), out...  11.1 us
    all_to_all x1, starting transfers between devices, body(): here = lax.all_to_all(own, 'ctx', 0, 0, tiled=True)  8.59 us
    all_to_all x1, waiting for transfers between devices, body(): here = lax.all_to_all(own, 'ctx', 0, 0, tiled=True)  5.32 us
    pallas_call x1, Pallas kernels, project(): pl.pallas_call(functools.partial(project_kernel, new_count=new_count), ou...  2.25 us
  transfers between devices with their start and end apart: 3, of which 1 were waited for; matrix products, arithmetic and copies ran while one was open for 16% of the time, Pallas kernels for 12%

profile of v1, /device:TPU:1, one launch (start us, length us, event | category | flops | bytes accessed | tf_op | source)
XLA Modules:
  0.0 92.0 jit_solution(16803867779128006827)
XLA Ops:
  0.0 0.9 copy.12
  1.0 1.2 %broadcast_in_dim.5 = bf16[16,2,32,576]{3,2,1,0:T(8,128)(2,1)} broadcast(bf16[2,32,576]{2,1,0:T(8,128)(2,1)S(1)} %broadcast_in_dim.4), dimensions={1,2,3} | broadcast | bytes 1253376 | tf_op jit(solution)/shard_map/broadcast_in_dim | solution.py:244
  2.2 8.6 %all-to-all-start = ((bf16[32,32,576]{2,1,0:T(8,128)(2,1)}), bf16[32,32,576]{2,1,0:T(8,128)(2,1)S(1)}, u32[]{:S(2)}, u32[]{:S(2)}) async-start(bf16[32,32,576]{2,1,0:T(8,128)(2,1)} %bitcast.3), calls=%async_computation | async-start | bytes 2621440 | tf_op jit(solution)/shard_map/all_to_all | solution.py:245
  10.8 0.0 copy-start.6
  10.8 14.1 %copy.13.cache_ref = bf16[8,1024,576]{2,1,0:T(8,128)(2,1)} copy(bf16[8,1024,576]{1,2,0:T(8,128)(2,1)} %param.6) | data formatting | bytes 18874368 | tf_op args[0]
  24.9 0.1 add_convert_fusion
  25.0 0.2 fusion
  25.2 0.1 pad_maximum_fusion
  25.3 5.3 %all-to-all-done.query_ref = bf16[32,32,576]{2,1,0:T(8,128)(2,1)S(1)} async-done(((bf16[32,32,576]{2,1,0:T(8,128)(2,1)}), bf16[32,32,576]{2,1,0:T(8,128)(2,1)S(1)}, u32[]{:S(2)}, u32[]{:S(2)}) %all-to-all-start) | async-done | bytes 1179680 | tf_op jit(solution)/shard_map/all_to_all | solution.py:245
  30.6 0.4 collective-permute-start
  31.0 4.0 %copy-done = bf16[8,1024,576]{2,1,0:T(8,128)(2,1)S(1)} copy-done((bf16[8,1024,576]{2,1,0:T(8,128)(2,1)S(1)}, bf16[8,1024,576]{2,1,0:T(8,128)(2,1)}, u32[]{:S(2)}) %copy-start) | copy-done | bytes 9437208
  35.0 6.0 %attend.3 = bf16[32,144,128]{2,1,0:T(8,128)(2,1)} custom-call(s32[1]{0:T(128)} %bitcast.half_ref, s32[1]{0:T(128)} %bitcast.1.first_ref, s32[8]{0:T(128)S(1)} %copy-done.6, bf16[8,1024,576]{2,1,0:T(8,128)(2,1)S(1)} %copy-done, bf16[32,32,576]{2,1,0:T(8,128)(2,1)S(1)} %all-to-all-done.query_ref, f32[8,8,64]{2,1,0:T(8,128)S(1)} %bitcast.9, ...), custom_call_target="tpu_custom_call" | custom-call | flops 2281701376 | bytes 7077888 | tf_op jit(solution)/shard_map/attend/pallas_call | solution.py:106
  41.0 0.1 collective-permute-start.1
  41.2 1.1 %copy-done.3 = bf16[32,32,576]{2,1,0:T(8,128)(2,1)} copy-done((bf16[32,32,576]{2,1,0:T(8,128)(2,1)}, bf16[32,32,576]{2,1,0:T(8,128)(2,1)S(1)}, u32[]{:S(2)}) %copy-start.3) | copy-done | bytes 1179672
  42.2 1.3 %copy-done.4 = bf16[32,32,576]{2,1,0:T(8,128)(2,1)S(1)} copy-done((bf16[32,32,576]{2,1,0:T(8,128)(2,1)S(1)}, bf16[32,32,576]{2,1,0:T(8,128)(2,1)}, u32[]{:S(2)}) %copy-start.4) | copy-done | bytes 1179672
  43.6 5.0 %attend.2.left_ref = bf16[32,144,128]{2,1,0:T(8,128)(2,1)S(1)} custom-call(s32[1]{0:T(128)S(6)} %sub.3.half_ref, s32[1]{0:T(128)} %bitcast.1.first_ref, s32[8]{0:T(128)S(1)} %copy-done.6, bf16[8,1024,576]{2,1,0:T(8,128)(2,1)S(1)} %copy-done.1, bf16[32,32,576]{2,1,0:T(8,128)(2,1)S(1)} %copy-done.4, f32[8,8,64]{2,1,0:T(8,128)S(1)} %bitcast.10, ...), custom_call_target="tpu_custom_call" | custom-call | flops 2281701376 | bytes 7077888 | tf_op jit(solution)/shard_map/attend/pallas_call | solution.py:106
  48.6 1.4 %merge.1 = bf16[32,144,128]{2,1,0:T(8,128)(2,1)S(1)} custom-call(bf16[32,144,128]{2,1,0:T(8,128)(2,1)S(1)} %attend.2.left_ref, bf16[32,144,128]{2,1,0:T(8,128)(2,1)S(1)} %collective-permute-done.1.right_ref), custom_call_target="tpu_custom_call" | custom-call | tf_op jit(solution)/shard_map/merge/pallas_call | solution.py:160
  50.0 22.8 %all_to_all.15.parts_ref = bf16[32,144,128]{2,1,0:T(8,128)(2,1)S(1)} all-to-all(bf16[32,144,128]{2,1,0:T(8,128)(2,1)S(1)} %merge.1), channel_id=1, replica_groups=mesh['batch'=8,'ctx'=32] {'ctx'}, dimensions={0} | all-to-all | bytes 2359296 | tf_op jit(solution)/shard_map/all_to_all | solution.py:254
  72.8 2.2 %project.1 = bf16[32,7168]{1,0:T(8,128)(2,1)S(1)} custom-call(bf16[32,144,128]{2,1,0:T(8,128)(2,1)S(1)} %all_to_all.15.parts_ref, bf16[2,512,128]{2,1,0:T(8,128)(2,1)S(1)} %copy-done.5, bf16[256,7168]{1,0:T(8,128)(2,1)S(1)} %copy-done.2), custom_call_target="tpu_custom_call" | custom-call | tf_op jit(solution)/shard_map/project/pallas_call | solution.py:219
  75.0 0.8 reshape.55
  75.8 0.3 copy.17
  76.1 15.2 %all_to_all.16 = bf16[32,32,224]{2,1,0:T(8,128)(2,1)S(1)} all-to-all(bf16[32,32,224]{2,1,0:T(8,128)(2,1)S(1)} %bitcast.13), channel_id=1, replica_groups=mesh['batch'=8,'ctx'=32] {'ctx'}, dimensions={0} | all-to-all | bytes 917504 | tf_op jit(solution)/shard_map/all_to_all | solution.py:258
  91.3 0.1 reduce_sum.12
  91.4 0.6 reshape.56
  (18 shorter events, 0.1 us)
Async XLA Ops:
  2.2 28.4 %all-to-all-start = ((bf16[32,32,576]{2,1,0:T(8,128)(2,1)}), bf16[32,32,576]{2,1,0:T(8,128)(2,1)S(1)}, u32[]{:S(2)}, u32[]{:S(2)}) async-start(bf16[32,32,576]{2,1,0:T(8,128)(2,1)} %bitcast.3), calls=%async_computation | async-start | bytes 2621440 | tf_op jit(solution)/shard_map/all_to_all | solution.py:245
  10.8 14.1 %copy-start.7 = (s32[8]{0:T(128)S(1)}, s32[8]{0:T(128)}, u32[]{:S(2)}) copy-start(s32[8]{0:T(128)} %param.9) | copy-start | bytes 100
  10.8 20.2 %copy-start.6 = (s32[8]{0:T(128)S(1)}, s32[8]{0:T(128)}, u32[]{:S(2)}) copy-start(s32[8]{0:T(128)} %lengths_ref.3) | copy-start | bytes 100
  30.6 10.6 %collective-permute-start = (bf16[32,32,576]{2,1,0:T(8,128)(2,1)S(1)}, bf16[32,32,576]{2,1,0:T(8,128)(2,1)S(1)}, u32[]{:S(2)}, u32[]{:S(2)}) collective-permute-start(bf16[32,32,576]{2,1,0:T(8,128)(2,1)S(1)} %all-to-all-done.query_ref), channel_id=1, source_target_pairs={{0,1},{1,0},{2,3},{3,2},{4,5},{5,4},{6,7},{7,6},{8,9},{9,8},{10,11... | collective-permute-start | bytes 3538952 | tf_op jit(solution)/shard_map/ppermute | solution.py:246
  31.0 4.0 %copy-start = (bf16[8,1024,576]{2,1,0:T(8,128)(2,1)S(1)}, bf16[8,1024,576]{2,1,0:T(8,128)(2,1)}, u32[]{:S(2)}) copy-start(bf16[8,1024,576]{2,1,0:T(8,128)(2,1)} %copy.13.cache_ref) | copy-start | bytes 28311556
  35.0 7.2 %copy-start.1 = (bf16[8,1024,576]{2,1,0:T(8,128)(2,1)S(1)}, bf16[8,1024,576]{2,1,0:T(8,128)(2,1)}, u32[]{:S(2)}) copy-start(bf16[8,1024,576]{2,1,0:T(8,128)(2,1)} %copy.13.cache_ref) | copy-start | bytes 28311556
  41.0 7.6 %collective-permute-start.1 = (bf16[32,144,128]{2,1,0:T(8,128)(2,1)}, bf16[32,144,128]{2,1,0:T(8,128)(2,1)S(1)}, u32[]{:S(2)}, u32[]{:S(2)}) collective-permute-start(bf16[32,144,128]{2,1,0:T(8,128)(2,1)} %attend.3), channel_id=1, source_target_pairs={{0,1},{1,0},{2,3},{3,2},{4,5},{5,4},{6,7},{7,6},{8,9},{9,8},{10,11... | collective-permute-start | bytes 3538952 | tf_op jit(solution)/shard_map/ppermute | solution.py:251
  41.2 1.1 %copy-start.3 = (bf16[32,32,576]{2,1,0:T(8,128)(2,1)}, bf16[32,32,576]{2,1,0:T(8,128)(2,1)S(1)}, u32[]{:S(2)}) copy-start(bf16[32,32,576]{2,1,0:T(8,128)(2,1)S(1)} %collective-permute-done.query_ref) | copy-start | bytes 3538948
  42.2 1.3 %copy-start.4 = (bf16[32,32,576]{2,1,0:T(8,128)(2,1)S(1)}, bf16[32,32,576]{2,1,0:T(8,128)(2,1)}, u32[]{:S(2)}) copy-start(bf16[32,32,576]{2,1,0:T(8,128)(2,1)} %copy-done.3) | copy-start | bytes 3538948
  48.6 24.2 %copy-start.2 = (bf16[256,7168]{1,0:T(8,128)(2,1)S(1)}, bf16[256,7168]{1,0:T(8,128)(2,1)}, u32[]{:S(2)}) copy-start(bf16[256,7168]{1,0:T(8,128)(2,1)} %proj_ref.1) | copy-start | bytes 11010052
  50.0 22.8 %copy-start.5 = (bf16[2,512,128]{2,1,0:T(8,128)(2,1)S(1)}, bf16[2,512,128]{2,1,0:T(8,128)(2,1)}, u32[]{:S(2)}) copy-start(bf16[2,512,128]{2,1,0:T(8,128)(2,1)} %up_ref.1) | copy-start | bytes 786436

commit v2 on v1

v2 whole, which is shorter than its diff:
```python
import functools
import math

import jax
import jax.numpy as jnp
from jax import lax
from jax.experimental import pallas as pl
from jax.experimental.pallas import tpu as pltpu
from jax.sharding import PartitionSpec as P

ROPE = 64
NOPE = 128
LANES = 128
POWER = math.log2(math.e) / math.sqrt(NOPE + ROPE)
HIDDEN = -1e30
VMEM_LIMIT = 24 * 1024 * 1024
LEAST = -1e29


def angle_terms(positions, new_count, repeats):
    half_rope = ROPE // 2
    exponent = jnp.arange(half_rope, dtype=jnp.float32) * (-2.0 / ROPE)
    frequency = jnp.power(jnp.float32(50000.0), exponent)
    token_place = positions[:, None] + jnp.arange(new_count, dtype=jnp.int32)[None, :]
    angles = token_place.astype(jnp.float32)[:, :, None] * frequency
    cosine, sine = jnp.cos(angles), jnp.sin(angles)
    cosines = jnp.concatenate([cosine, cosine], axis=-1)
    sines = jnp.concatenate([-sine, sine], axis=-1)
    return jnp.tile(cosines, (1, repeats, 1)), jnp.tile(sines, (1, repeats, 1))


def split_stat(value, lane):
    high = value.astype(jnp.bfloat16).astype(jnp.float32)
    rest = value - high
    middle = rest.astype(jnp.bfloat16).astype(jnp.float32)
    low = rest - middle
    spot = lane % (LANES // 2)
    return jnp.where(spot == 0, high, jnp.where(spot == 1, middle, low))


def join_stat(tile, pair):
    at = pair * (LANES // 2)
    return tile[..., at : at + 1] + tile[..., at + 1 : at + 2] + tile[..., at + 2 : at + 3]


def attend_kernel(scalars_ref, lengths_ref, own_ref, came_ref, query_ref, cos_ref, sin_ref, out_ref, kept_ref, *, new_count):
    row = pl.program_id(0)
    peers, sixteen, full = query_ref.shape
    group = sixteen // 2
    latent = full - ROPE
    count = peers * group
    context = own_ref.shape[2]
    column_groups = latent // LANES
    odd = lax.rem(row, 2) == 1
    gathered = query_ref[...].astype(jnp.float32)
    query = jnp.where(odd, gathered[:, group:, :], gathered[:, :group, :])
    rope = query[:, :, latent:]
    swapped = jnp.concatenate([rope[:, :, ROPE // 2 :], rope[:, :, : ROPE // 2]], axis=-1)
    turned = rope * cos_ref[0][None] + swapped * sin_ref[0][None]
    query = jnp.concatenate([query[:, :, :latent], turned], axis=-1)
    query = query.reshape(count, full).astype(jnp.bfloat16)
    limit = lengths_ref[scalars_ref[0] * 4 + row] - new_count + 1
    token = lax.broadcasted_iota(jnp.int32, (count, 1), 0) % new_count
    terms = []
    for block, first in ((own_ref, scalars_ref[1]), (came_ref, scalars_ref[2])):
        keys = block[0]
        scores = jnp.dot(query, keys, preferred_element_type=jnp.float32)
        place = lax.broadcasted_iota(jnp.int32, (count, context), 1)
        scores = jnp.where(place < limit - first + token, scores, HIDDEN)
        top = jnp.maximum(jnp.max(scores, axis=-1, keepdims=True), LEAST)
        weights = jnp.exp2((scores - top) * POWER)
        total = jnp.sum(weights, axis=-1, keepdims=True)
        out = lax.dot_general(
            weights.astype(jnp.bfloat16),
            keys[:latent],
            (((1,), (1,)), ((), ())),
            preferred_element_type=jnp.float32,
        )
        terms.append((top, total, out))
    (top_a, total_a, out_a), (top_b, total_b, out_b) = terms
    top = jnp.maximum(top_a, top_b)
    scale_a, scale_b = jnp.exp2((top_a - top) * POWER), jnp.exp2((top_b - top) * POWER)
    total = total_a * scale_a + total_b * scale_b
    seen = total > 0.0
    safe = jnp.where(seen, total, 1.0)
    inverse = 1.0 / safe
    out = out_a * (scale_a * inverse) + out_b * (scale_b * inverse)
    stat = jnp.where(seen, top * POWER + jnp.log2(safe), HIDDEN)
    out = out.reshape(peers, group, latent)
    stat = jnp.broadcast_to(stat, (count, LANES)).reshape(peers, group, LANES)

    @pl.when(jnp.logical_not(odd))
    def _():
        kept_ref[:, :, :latent] = out
        kept_ref[:, :, latent:] = stat

    @pl.when(odd)
    def _():
        pair = row // 2
        both = jnp.concatenate([kept_ref[:, :, :latent], out], axis=1).astype(jnp.bfloat16)
        for g in range(column_groups):
            at = pl.multiple_of(g * 2 * sixteen + pair * sixteen, sixteen)
            out_ref[:, pl.ds(at, sixteen), :] = both[:, :, g * LANES : (g + 1) * LANES]
        stats = jnp.concatenate([kept_ref[:, :, latent:], stat], axis=1)
        lane = lax.broadcasted_iota(jnp.int32, stats.shape, 2)
        packed = split_stat(stats, lane)
        at = column_groups * 2 * sixteen

        @pl.when(pair == 0)
        def _():
            out_ref[:, at : at + sixteen, :] = packed.astype(jnp.bfloat16)

        @pl.when(pair == 1)
        def _():
            before = out_ref[:, at : at + sixteen, :].astype(jnp.float32)
            out_ref[:, at : at + sixteen, :] = jnp.where(lane < LANES // 2, before, packed).astype(jnp.bfloat16)


def attend(scalars, lengths, own, came, query, cosines, sines, new_count):
    peers, depth, full = query.shape
    sixteen = depth // 2
    context = own.shape[2]
    group = sixteen // 2
    latent = full - ROPE
    rows_out = latent // LANES * depth + sixteen
    count = peers * group
    return pl.pallas_call(
        functools.partial(attend_kernel, new_count=new_count),
        out_shape=jax.ShapeDtypeStruct((peers, rows_out, LANES), jnp.bfloat16),
        grid_spec=pltpu.PrefetchScalarGridSpec(
            num_scalar_prefetch=2,
            grid=(4,),
            in_specs=[
                pl.BlockSpec((1, full, context), lambda r, scalars, _: (scalars[0] * 4 + r, 0, 0)),
                pl.BlockSpec((1, full, context), lambda r, *_: (r, 0, 0)),
                pl.BlockSpec((peers, sixteen, full), lambda r, *_: (0, r // 2, 0)),
                pl.BlockSpec((1, group, ROPE), lambda r, scalars, _: (scalars[0] * 4 + r, 0, 0)),
                pl.BlockSpec((1, group, ROPE), lambda r, scalars, _: (scalars[0] * 4 + r, 0, 0)),
            ],
            out_specs=pl.BlockSpec((peers, rows_out, LANES), lambda r, *_: (0, 0, 0)),
            scratch_shapes=[pltpu.VMEM((peers, group, latent + LANES), jnp.float32)],
        ),
        compiler_params=pltpu.CompilerParams(vmem_limit_bytes=VMEM_LIMIT),
        cost_estimate=pl.CostEstimate(
            flops=4 * count * context * (full + latent) * 4,
            bytes_accessed=8 * context * full * 2 + 4 * peers * rows_out * LANES,
            transcendentals=8 * count * context,
        ),
        name="attend",
    )(scalars, lengths, own, came, query, cosines, sines)


def project_kernel(parts_ref, up_ref, proj_ref, out_ref, flat_ref, *, new_count):
    sixteen = 16
    peers, rows_out, lanes = parts_ref.shape
    at = rows_out - sixteen
    groups = at // (2 * sixteen)
    heads, _, width = up_ref.shape

    @pl.when(pl.program_id(0) == 0)
    def _():
        blocks = []
        for half in range(2):
            chosen = [2 * k + half for k in range(peers // 2)]
            stat_tiles = [parts_ref[k, at:, :].astype(jnp.float32) for k in chosen]
            for pair in range(2):
                stats = [join_stat(tile, pair) for tile in stat_tiles]
                top = functools.reduce(jnp.maximum, stats)
                weights = [jnp.exp2(stat - top) for stat in stats]
                scale = 1.0 / functools.reduce(jnp.add, weights)
                sums = []
                for g in range(groups):
                    start = g * 2 * sixteen + pair * sixteen
                    acc = None
                    for k, weight in zip(chosen, weights):
                        term = parts_ref[k, start : start + sixteen, :].astype(jnp.float32) * weight
                        acc = term if acc is None else acc + term
                    sums.append(acc * scale)
                blocks.append(jnp.concatenate(sums, axis=-1))
        latent = jnp.concatenate(blocks, axis=0).astype(jnp.bfloat16)
        count = latent.shape[0]
        out_row = lax.broadcasted_iota(jnp.int32, (count // heads, count), 0)
        in_row = lax.broadcasted_iota(jnp.int32, (count // heads, count), 1)
        base = (out_row // new_count) * (new_count * heads) + out_row % new_count
        for head in range(heads):
            pick = jnp.where(in_row == base + head * new_count, 1.0, 0.0).astype(jnp.bfloat16)
            own = jnp.dot(pick, latent, preferred_element_type=jnp.float32).astype(jnp.bfloat16)
            values = jnp.dot(own, up_ref[head], preferred_element_type=jnp.float32)
            flat_ref[:, head * width : (head + 1) * width] = values.astype(jnp.bfloat16)

    terms = jnp.dot(flat_ref[...], proj_ref[...], preferred_element_type=jnp.float32)
    width = out_ref.shape[2]
    for k in range(out_ref.shape[0]):
        out_ref[k] = terms[:, k * width : (k + 1) * width].astype(jnp.bfloat16)


def project(parts, value_up, out_proj, new_count):
    peers, rows_out, lanes = parts.shape
    heads, latent, width = value_up.shape
    depth, columns = out_proj.shape
    tokens = (rows_out - 16) // (latent // lanes) * 2 // heads
    steps = 4
    block = columns // steps
    return pl.pallas_call(
        functools.partial(project_kernel, new_count=new_count),
        out_shape=jax.ShapeDtypeStruct((peers, tokens, columns // peers), jnp.bfloat16),
        grid=(steps,),
        in_specs=[
            pl.BlockSpec((peers, rows_out, lanes), lambda i: (0, 0, 0)),
            pl.BlockSpec((heads, latent, width), lambda i: (0, 0, 0)),
            pl.BlockSpec((depth, block), lambda i: (0, i)),
        ],
        out_specs=pl.BlockSpec((peers // steps, tokens, columns // peers), lambda i: (i, 0, 0)),
        scratch_shapes=[pltpu.VMEM((tokens, depth), jnp.bfloat16)],
        compiler_params=pltpu.CompilerParams(vmem_limit_bytes=16 * 1024 * 1024),
        name="project",
    )(parts, value_up, out_proj)


def total_kernel(terms_ref, out_ref):
    total = jnp.sum(terms_ref[...].astype(jnp.float32), axis=0).astype(jnp.bfloat16)
    new_count = out_ref.shape[1]
    for row in range(out_ref.shape[0]):
        out_ref[row] = total[row * new_count : (row + 1) * new_count]


def total(terms, rows, new_count):
    return pl.pallas_call(
        total_kernel,
        out_shape=jax.ShapeDtypeStruct((rows, new_count, terms.shape[2]), jnp.bfloat16),
        compiler_params=pltpu.CompilerParams(vmem_limit_bytes=8 * 1024 * 1024),
        name="total",
    )(terms)


def body(latent_cache, queries, lengths, positions, value_up, out_proj):
    row_count, context_dev, full = latent_cache.shape
    new_count, heads_dev = queries.shape[1], queries.shape[2]
    shard = lax.axis_index("ctx")
    peers = lax.axis_size("ctx")
    core = shard % 2
    partners = [(i, i ^ 1) for i in range(peers)]
    depth = row_count // 2 * new_count * heads_dev
    own = queries.transpose(0, 2, 1, 3).reshape(1, 2, depth, full)
    own = jnp.broadcast_to(own, (peers // 2, 2, depth, full)).reshape(peers, depth, full)
    here = lax.all_to_all(own, "ctx", 0, 0, tiled=True)
    cache = jnp.swapaxes(latent_cache, 1, 2)
    half = row_count // 2
    lost = lax.dynamic_slice_in_dim(cache, (1 - core) * half, half, 0)
    came = lax.ppermute(lost, "ctx", partners)
    cosines, sines = angle_terms(positions, new_count, heads_dev)
    scalars = jnp.stack([core, shard * context_dev, (shard ^ 1) * context_dev]).astype(jnp.int32)
    mine = attend(scalars, lengths, cache, came, here, cosines, sines, new_count)
    parts = lax.all_to_all(mine, "ctx", 0, 0, tiled=True)
    terms = project(parts, value_up, out_proj, new_count)
    terms = lax.all_to_all(terms, "ctx", 0, 0, tiled=True)
    return total(terms, row_count, new_count)


def solution(mesh):
    in_specs = (
        P("batch", "ctx", None),
        P("batch", None, "ctx", None),
        P("batch"),
        P("batch"),
        P("ctx", None, None),
        P("ctx", None),
    )
    out_specs = P("batch", None, "ctx")
    return jax.shard_map(body, mesh=mesh, in_specs=in_specs, out_specs=out_specs, check_vma=False)
```

time: 92.7 us -> 90.7 us (0.978)
  local copies, waits for them, and re-layouts: 24.3 us -> 10.1 us
  waiting for transfers between devices: 5.32 us -> 19.3 us
    unnamed x17 -> x12, local copies, waits for them, and re-layouts: 20.4 us -> 3.69 us
    all_to_all x1, waiting for transfers between devices: 5.32 us -> 19.3 us  [body(): here = lax.all_to_all(own, 'ctx', 0, 0, tiled=True)]
    dynamic_slice x0 -> x1, local copies, waits for them, and re-layouts: none -> 5.02 us  [body(): lost = lax.dynamic_slice_in_dim(cache, (1 - core) * half, half, 0)]
    all_to_all x1, starting transfers between devices: 8.59 us -> 5.47 us  [body(): here = lax.all_to_all(own, 'ctx', 0, 0, tiled=True)]
    ppermute x2 -> x1, starting transfers between devices: 0.51 us -> 3.23 us  [body(): came = lax.ppermute(lost, 'ctx', partners)]
    reshape x3 -> x0, local copies, waits for them, and re-layouts: 1.67 us -> none  [the longest x2 1.05 us: body(): terms.reshape(row_count * new_count, peers, width).transpose(1, 0, 2)]
    pallas_call x2 -> x1, Pallas kernels: 11.1 us -> 10.7 us  [attend(): pl.pallas_call(functools.partial(attend_kernel, new_count=new_count), out...]
  transfers between devices with their start and end apart: 3 -> 2, of which waited for: 1 -> 1; matrix products, arithmetic and copies ran while one was open for 16% -> 2% of each run, Pallas kernels for 12% -> 0%
where the time goes in v2:
time: 90.7 us; the launch traced here: 90.5 us
  blocking collectives  37.8 us (42%)
  waiting for transfers between devices  19.3 us (21%)
  Pallas kernels  14 us (15%)
  local copies, waits for them, and re-layouts  10.1 us (11%)
  starting transfers between devices  8.7 us (10%)
    all_to_all x1, blocking collectives, body(): parts = lax.all_to_all(mine, 'ctx', 0, 0, tiled=True)  22.6 us
    all_to_all x1, waiting for transfers between devices, body(): here = lax.all_to_all(own, 'ctx', 0, 0, tiled=True)  19.3 us
    all_to_all x1, blocking collectives, body(): terms = lax.all_to_all(terms, 'ctx', 0, 0, tiled=True)  15.2 us
    pallas_call x1, Pallas kernels, attend(): pl.pallas_call(functools.partial(attend_kernel, new_count=new_count), out...  10.7 us
    all_to_all x1, starting transfers between devices, body(): here = lax.all_to_all(own, 'ctx', 0, 0, tiled=True)  5.47 us
    dynamic_slice x1, local copies, waits for them, and re-layouts, body(): lost = lax.dynamic_slice_in_dim(cache, (1 - core) * half, half, 0)  5.02 us
    unnamed x12, local copies, waits for them, and re-layouts  3.69 us
    ppermute x1, starting transfers between devices, body(): came = lax.ppermute(lost, 'ctx', partners)  3.23 us
  transfers between devices with their start and end apart: 2, of which 1 were waited for; matrix products, arithmetic and copies ran while one was open for 2% of the time, Pallas kernels for 0%

profile of v2, /device:TPU:1, one launch (start us, length us, event | category | flops | bytes accessed | tf_op | source)
XLA Modules:
  0.0 90.5 jit_solution(949003552867112057)
XLA Ops:
  0.0 0.0 copy-start.5
  0.0 0.0 copy-start.3
  0.0 5.0 %dynamic-slice_bitcast_fusion = bf16[4,576,1024]{2,1,0:T(8,128)(2,1)} fusion(bf16[8,1024,576]{1,2,0:T(8,128)(2,1)} %param.6, s32[]{:T(128)S(6)} %select_n.11), kind=kLoop, calls=%fused_computation | loop fusion | bytes 9437188 | tf_op jit(solution)/shard_map/dynamic_slice | solution.py:249
  5.0 3.2 %collective-permute-start = (bf16[4,576,1024]{2,1,0:T(8,128)(2,1)}, bf16[4,576,1024]{2,1,0:T(8,128)(2,1)}, u32[]{:S(2)}, u32[]{:S(2)}) collective-permute-start(bf16[4,576,1024]{2,1,0:T(8,128)(2,1)} %dynamic-slice_bitcast_fusion), channel_id=1, source_target_pairs={{0,1},{1,0},{2,3},{3,2},{4,5},{5,4},{6,7},{7,6},{8,9},{9,8},{10,11... | collective-permute-start | bytes 14155784 | tf_op jit(solution)/shard_map/ppermute | solution.py:250
  8.3 0.0 copy-done.4
  8.3 1.3 %broadcast_in_dim.5 = bf16[16,2,32,576]{3,2,1,0:T(8,128)(2,1)} broadcast(bf16[2,32,576]{2,1,0:T(8,128)(2,1)S(1)} %broadcast_in_dim.4), dimensions={1,2,3} | broadcast | bytes 1253376 | tf_op jit(solution)/shard_map/broadcast_in_dim | solution.py:245
  9.6 5.5 %all-to-all-start = ((bf16[32,32,576]{2,1,0:T(8,128)(2,1)}), bf16[32,32,576]{2,1,0:T(8,128)(2,1)S(1)}, u32[]{:S(2)}, u32[]{:S(2)}) async-start(bf16[32,32,576]{2,1,0:T(8,128)(2,1)} %bitcast.6), calls=%async_computation | async-start | bytes 2621440 | tf_op jit(solution)/shard_map/all_to_all | solution.py:246
  15.1 0.1 pad_add_fusion.scalars_ref
  15.2 0.0 copy-done.5
  15.2 0.1 add_convert_fusion
  15.3 0.2 fusion
  15.5 0.1 pad_maximum_fusion
  15.5 19.3 %all-to-all-done.query_ref = bf16[32,32,576]{2,1,0:T(8,128)(2,1)S(1)} async-done(((bf16[32,32,576]{2,1,0:T(8,128)(2,1)}), bf16[32,32,576]{2,1,0:T(8,128)(2,1)S(1)}, u32[]{:S(2)}, u32[]{:S(2)}) %all-to-all-start) | async-done | bytes 1179680 | tf_op jit(solution)/shard_map/all_to_all | solution.py:246
  34.9 0.0 collective-permute-done.came_ref
  34.9 0.0 copy-done.3
  34.9 0.0 copy-start.1
  34.9 3.7 %copy-done.1 = bf16[8,1024,576]{1,2,0:T(8,128)(2,1)S(1)} copy-done((bf16[8,1024,576]{1,2,0:T(8,128)(2,1)S(1)}, bf16[8,1024,576]{1,2,0:T(8,128)(2,1)}, u32[]{:S(2)}) %copy-start.1) | copy-done | bytes 9437208
  38.6 10.7 %attend.1 = bf16[32,144,128]{2,1,0:T(8,128)(2,1)S(1)} custom-call(s32[3]{0:T(128)S(1)} %pad_add_fusion.scalars_ref, s32[8]{0:T(128)S(1)} %copy-done.3, bf16[8,576,1024]{2,1,0:T(8,128)(2,1)S(1)} %bitcast.10, bf16[4,576,1024]{2,1,0:T(8,128)(2,1)} %collective-permute-done.came_ref, bf16[32,32,576]{2,1,0:T(8,128)(2,1)S(1)} %all-to-all-done.query_ref, ...), custom_call_target="tpu_custom_call" | custom-call | flops 4563402752 | bytes 11796480 | tf_op jit(solution)/shard_map/attend/pallas_call | solution.py:127
  49.3 22.6 %all_to_all.15.parts_ref = bf16[32,144,128]{2,1,0:T(8,128)(2,1)S(1)} all-to-all(bf16[32,144,128]{2,1,0:T(8,128)(2,1)S(1)} %attend.1), channel_id=1, replica_groups=mesh['batch'=8,'ctx'=32] {'ctx'}, dimensions={0} | all-to-all | bytes 2359296 | tf_op jit(solution)/shard_map/all_to_all | solution.py:254
  72.0 0.0 copy-done
  72.0 0.0 copy-done.2
  72.0 2.6 %project.1 = bf16[32,32,224]{2,1,0:T(8,128)(2,1)S(1)} custom-call(bf16[32,144,128]{2,1,0:T(8,128)(2,1)S(1)} %all_to_all.15.parts_ref, bf16[2,512,128]{2,1,0:T(8,128)(2,1)S(1)} %copy-done.2, bf16[256,7168]{1,0:T(8,128)(2,1)S(1)} %copy-done), custom_call_target="tpu_custom_call" | custom-call | tf_op jit(solution)/shard_map/project/pallas_call | solution.py:204
  74.6 15.2 %all_to_all.16.terms_ref = bf16[32,32,224]{2,1,0:T(8,128)(2,1)S(1)} all-to-all(bf16[32,32,224]{2,1,0:T(8,128)(2,1)S(1)} %project.1), channel_id=1, replica_groups=mesh['batch'=8,'ctx'=32] {'ctx'}, dimensions={0} | all-to-all | bytes 917504 | tf_op jit(solution)/shard_map/all_to_all | solution.py:256
  89.8 0.7 total.1
  (8 shorter events, 0.1 us)
Async XLA Ops:
  0.0 8.3 %copy-start.4 = (bf16[8,4,2,576]{3,2,1,0:T(2,128)(2,1)S(1)}, bf16[8,4,2,576]{3,2,1,0:T(2,128)(2,1)}, u32[]{:S(2)}) copy-start(bf16[8,4,2,576]{3,2,1,0:T(2,128)(2,1)} %param.7) | copy-start | bytes 221188
  0.0 15.2 %copy-start.5 = (s32[8]{0:T(128)S(1)}, s32[8]{0:T(128)}, u32[]{:S(2)}) copy-start(s32[8]{0:T(128)} %param.9) | copy-start | bytes 100
  0.0 34.9 %copy-start.3 = (s32[8]{0:T(128)S(1)}, s32[8]{0:T(128)}, u32[]{:S(2)}) copy-start(s32[8]{0:T(128)} %lengths_ref.1) | copy-start | bytes 100
  5.0 29.8 %collective-permute-start = (bf16[4,576,1024]{2,1,0:T(8,128)(2,1)}, bf16[4,576,1024]{2,1,0:T(8,128)(2,1)}, u32[]{:S(2)}, u32[]{:S(2)}) collective-permute-start(bf16[4,576,1024]{2,1,0:T(8,128)(2,1)} %dynamic-slice_bitcast_fusion), channel_id=1, source_target_pairs={{0,1},{1,0},{2,3},{3,2},{4,5},{5,4},{6,7},{7,6},{8,9},{9,8},{10,11... | collective-permute-start | bytes 14155784 | tf_op jit(solution)/shard_map/ppermute | solution.py:250
  9.6 25.3 %all-to-all-start = ((bf16[32,32,576]{2,1,0:T(8,128)(2,1)}), bf16[32,32,576]{2,1,0:T(8,128)(2,1)S(1)}, u32[]{:S(2)}, u32[]{:S(2)}) async-start(bf16[32,32,576]{2,1,0:T(8,128)(2,1)} %bitcast.6), calls=%async_computation | async-start | bytes 2621440 | tf_op jit(solution)/shard_map/all_to_all | solution.py:246
  34.9 3.7 %copy-start.1 = (bf16[8,1024,576]{1,2,0:T(8,128)(2,1)S(1)}, bf16[8,1024,576]{1,2,0:T(8,128)(2,1)}, u32[]{:S(2)}) copy-start(bf16[8,1024,576]{1,2,0:T(8,128)(2,1)} %param.6) | copy-start | bytes 28311556
  38.6 33.4 %copy-start = (bf16[256,7168]{1,0:T(8,128)(2,1)S(1)}, bf16[256,7168]{1,0:T(8,128)(2,1)}, u32[]{:S(2)}) copy-start(bf16[256,7168]{1,0:T(8,128)(2,1)} %proj_ref.1) | copy-start | bytes 11010052
  38.6 33.4 %copy-start.2 = (bf16[2,512,128]{2,1,0:T(8,128)(2,1)S(1)}, bf16[2,512,128]{2,1,0:T(8,128)(2,1)}, u32[]{:S(2)}) copy-start(bf16[2,512,128]{2,1,0:T(8,128)(2,1)} %up_ref.1) | copy-start | bytes 786436

commit v3 on v2

--- a/solution.py
+++ b/solution.py
@@ -43,108 +43,114 @@
     return tile[..., at : at + 1] + tile[..., at + 1 : at + 2] + tile[..., at + 2 : at + 3]
 
 
-def attend_kernel(scalars_ref, lengths_ref, own_ref, came_ref, query_ref, cos_ref, sin_ref, out_ref, kept_ref, *, new_count):
-    row = pl.program_id(0)
-    peers, sixteen, full = query_ref.shape
-    group = sixteen // 2
+def attend_kernel(scalars_ref, lengths_ref, own_ref, came_ref, query_ref, cos_ref, sin_ref, out_ref, keys_ref, arrived, *, new_count):
+    peers, depth, full = query_ref.shape
+    rows = keys_ref.shape[0] // 2
+    group = depth // rows
     latent = full - ROPE
     count = peers * group
-    context = own_ref.shape[2]
+    context = keys_ref.shape[2]
     column_groups = latent // LANES
-    odd = lax.rem(row, 2) == 1
-    gathered = query_ref[...].astype(jnp.float32)
-    query = jnp.where(odd, gathered[:, group:, :], gathered[:, :group, :])
-    rope = query[:, :, latent:]
-    swapped = jnp.concatenate([rope[:, :, ROPE // 2 :], rope[:, :, : ROPE // 2]], axis=-1)
-    turned = rope * cos_ref[0][None] + swapped * sin_ref[0][None]
-    query = jnp.concatenate([query[:, :, :latent], turned], axis=-1)
-    query = query.reshape(count, full).astype(jnp.bfloat16)
-    limit = lengths_ref[scalars_ref[0] * 4 + row] - new_count + 1
+    base = scalars_ref[0] * rows
+    copies = []
+    for row in range(rows):
+        for side, ref in enumerate((own_ref, came_ref)):
+            slot = row * 2 + side
+            copies.append(pltpu.make_async_copy(ref.at[base + row], keys_ref.at[slot], arrived.at[slot]))
+    for copy in copies:
+        copy.start()
     token = lax.broadcasted_iota(jnp.int32, (count, 1), 0) % new_count
-    terms = []
-    for block, first in ((own_ref, scalars_ref[1]), (came_ref, scalars_ref[2])):
-        keys = block[0]
-        scores = jnp.dot(query, keys, preferred_element_type=jnp.float32)
+    queries = []
+    for row in range(rows):
+        query = query_ref[:, row // 2 * 2 * group : (row // 2 + 1) * 2 * group, :].astype(jnp.float32)
+        query = query[:, row % 2 * group : (row % 2 + 1) * group, :]
+        rope = query[:, :, latent:]
+        swapped = jnp.concatenate([rope[:, :, ROPE // 2 :], rope[:, :, : ROPE // 2]], axis=-1)
+        turned = rope * cos_ref[base + row][None] + swapped * sin_ref[base + row][None]
+        query = jnp.concatenate([query[:, :, :latent], turned], axis=-1)
+        queries.append(query.reshape(count, full).astype(jnp.bfloat16))
+
+    def scores_of(slot):
+        copies[slot].wait()
+        return jnp.dot(queries[slot // 2], keys_ref[slot], preferred_element_type=jnp.float32)
+
+    def terms_of(slot, scores):
+        row, side = slot // 2, slot % 2
+        limit = lengths_ref[base + row] - new_count + 1 - scalars_ref[1 + side]
         place = lax.broadcasted_iota(jnp.int32, (count, context), 1)
-        scores = jnp.where(place < limit - first + token, scores, HIDDEN)
+        scores = jnp.where(place < limit + token, scores, HIDDEN)
         top = jnp.maximum(jnp.max(scores, axis=-1, keepdims=True), LEAST)
         weights = jnp.exp2((scores - top) * POWER)
         total = jnp.sum(weights, axis=-1, keepdims=True)
         out = lax.dot_general(
             weights.astype(jnp.bfloat16),
-            keys[:latent],
+            keys_ref[slot, :latent],
             (((1,), (1,)), ((), ())),
             preferred_element_type=jnp.float32,
         )
-        terms.append((top, total, out))
-    (top_a, total_a, out_a), (top_b, total_b, out_b) = terms
-    top = jnp.maximum(top_a, top_b)
-    scale_a, scale_b = jnp.exp2((top_a - top) * POWER), jnp.exp2((top_b - top) * POWER)
-    total = total_a * scale_a + total_b * scale_b
-    seen = total > 0.0
-    safe = jnp.where(seen, total, 1.0)
-    inverse = 1.0 / safe
-    out = out_a * (scale_a * inverse) + out_b * (scale_b * inverse)
-    stat = jnp.where(seen, top * POWER + jnp.log2(safe), HIDDEN)
-    out = out.reshape(peers, group, latent)
-    stat = jnp.broadcast_to(stat, (count, LANES)).reshape(peers, group, LANES)
-
-    @pl.when(jnp.logical_not(odd))
-    def _():
-        kept_ref[:, :, :latent] = out
-        kept_ref[:, :, latent:] = stat
-
-    @pl.when(odd)
-    def _():
-        pair = row // 2
-        both = jnp.concatenate([kept_ref[:, :, :latent], out], axis=1).astype(jnp.bfloat16)
-        for g in range(column_groups):
-            at = pl.multiple_of(g * 2 * sixteen + pair * sixteen, sixteen)
-            out_ref[:, pl.ds(at, sixteen), :] = both[:, :, g * LANES : (g + 1) * LANES]
-        stats = jnp.concatenate([kept_ref[:, :, latent:], stat], axis=1)
-        lane = lax.broadcasted_iota(jnp.int32, stats.shape, 2)
-        packed = split_stat(stats, lane)
-        at = column_groups * 2 * sixteen
-
-        @pl.when(pair == 0)
-        def _():
-            out_ref[:, at : at + sixteen, :] = packed.astype(jnp.bfloat16)
-
-        @pl.when(pair == 1)
-        def _():
-            before = out_ref[:, at : at + sixteen, :].astype(jnp.float32)
-            out_ref[:, at : at + sixteen, :] = jnp.where(lane < LANES // 2, before, packed).astype(jnp.bfloat16)
+        return top, total, out
+
+    def close(row, first, second):
+        (top_a, total_a, out_a), (top_b, total_b, out_b) = first, second
+        top = jnp.maximum(top_a, top_b)
+        scale_a, scale_b = jnp.exp2((top_a - top) * POWER), jnp.exp2((top_b - top) * POWER)
+        total = total_a * scale_a + total_b * scale_b
+        seen = total > 0.0
+        safe = jnp.where(seen, total, 1.0)
+        inverse = 1.0 / safe
+        out = out_a * (scale_a * inverse) + out_b * (scale_b * inverse)
+        stat = jnp.where(seen, top * POWER + jnp.log2(safe), HIDDEN)
+        return out.reshape(peers, group, latent), jnp.broadcast_to(stat, (count, LANES)).reshape(peers, group, LANES)
+
+    sixteen = 2 * group
+    at = column_groups * depth
+    slots = 2 * rows
+    ahead = scores_of(0)
+    terms, closed, packed = [], [], []
+    for slot in range(slots):
+        scores = ahead
+        if slot + 1 < slots:
+            ahead = scores_of(slot + 1)
+        terms.append(terms_of(slot, scores))
+        if slot % 2 == 1:
+            closed.append(close(slot // 2, *terms[-2:]))
+        if slot % 4 == 3:
+            pair = slot // 4
+            (out_a, stat_a), (out_b, stat_b) = closed[-2:]
+            both = jnp.concatenate([out_a, out_b], axis=1).astype(jnp.bfloat16)
+            for g in range(column_groups):
+                start = g * depth + pair * sixteen
+                out_ref[:, start : start + sixteen, :] = both[:, :, g * LANES : (g + 1) * LANES]
+            stats = jnp.concatenate([stat_a, stat_b], axis=1)
+            lane = lax.broadcasted_iota(jnp.int32, stats.shape, 2)
+            packed.append(split_stat(stats, lane))
+    lane = lax.broadcasted_iota(jnp.int32, packed[0].shape, 2)
+    out_ref[:, at : at + sixteen, :] = jnp.where(lane < LANES // 2, packed[0], packed[1]).astype(jnp.bfloat16)
 
 
 def attend(scalars, lengths, own, came, query, cosines, sines, new_count):
     peers, depth, full = query.shape
-    sixteen = depth // 2
+    rows = own.shape[0] // 2
     context = own.shape[2]
-    group = sixteen // 2
     latent = full - ROPE
-    rows_out = latent // LANES * depth + sixteen
-    count = peers * group
+    rows_out = latent // LANES * depth + depth // rows * 2
+    count = peers * depth // rows
+    smem, vmem, anywhere = (pl.BlockSpec(memory_space=s) for s in (pltpu.SMEM, pltpu.VMEM, pl.ANY))
+    own = pltpu.with_memory_space_constraint(own, pltpu.HBM)
     return pl.pallas_call(
         functools.partial(attend_kernel, new_count=new_count),
-        out_shape=jax.ShapeDtypeStruct((peers, rows_out, LANES), jnp.bfloat16),
-        grid_spec=pltpu.PrefetchScalarGridSpec(
-            num_scalar_prefetch=2,
-            grid=(4,),
-            in_specs=[
-                pl.BlockSpec((1, full, context), lambda r, scalars, _: (scalars[0] * 4 + r, 0, 0)),
-                pl.BlockSpec((1, full, context), lambda r, *_: (r, 0, 0)),
-                pl.BlockSpec((peers, sixteen, full), lambda r, *_: (0, r // 2, 0)),
-                pl.BlockSpec((1, group, ROPE), lambda r, scalars, _: (scalars[0] * 4 + r, 0, 0)),
-                pl.BlockSpec((1, group, ROPE), lambda r, scalars, _: (scalars[0] * 4 + r, 0, 0)),
-            ],
-            out_specs=pl.BlockSpec((peers, rows_out, LANES), lambda r, *_: (0, 0, 0)),
-            scratch_shapes=[pltpu.VMEM((peers, group, latent + LANES), jnp.float32)],
-        ),
+        out_shape=pltpu.VMEM((peers, rows_out, LANES), jnp.bfloat16),
+        in_specs=[smem, smem, anywhere, anywhere, vmem, vmem, vmem],
+        out_specs=vmem,
+        scratch_shapes=[
+            pltpu.VMEM((2 * rows, full, context), jnp.bfloat16),
+            pltpu.SemaphoreType.DMA((2 * rows,)),
+        ],
         compiler_params=pltpu.CompilerParams(vmem_limit_bytes=VMEM_LIMIT),
         cost_estimate=pl.CostEstimate(
-            flops=4 * count * context * (full + latent) * 4,
-            bytes_accessed=8 * context * full * 2 + 4 * peers * rows_out * LANES,
-            transcendentals=8 * count * context,
+            flops=4 * count * context * (full + latent) * rows,
+            bytes_accessed=2 * rows * context * full * 2 + 2 * peers * rows_out * LANES,
+            transcendentals=2 * rows * count * context,
         ),
         name="attend",
     )(scalars, lengths, own, came, query, cosines, sines)
@@ -245,9 +251,7 @@
     own = jnp.broadcast_to(own, (peers // 2, 2, depth, full)).reshape(peers, depth, full)
     here = lax.all_to_all(own, "ctx", 0, 0, tiled=True)
     cache = jnp.swapaxes(latent_cache, 1, 2)
-    half = row_count // 2
-    lost = lax.dynamic_slice_in_dim(cache, (1 - core) * half, half, 0)
-    came = lax.ppermute(lost, "ctx", partners)
+    came = lax.ppermute(cache, "ctx", partners)
     cosines, sines = angle_terms(positions, new_count, heads_dev)
     scalars = jnp.stack([core, shard * context_dev, (shard ^ 1) * context_dev]).astype(jnp.int32)
     mine = attend(scalars, lengths, cache, came, here, cosines, sines, new_count)

time: 90.7 us -> 82.7 us (0.912)
  local copies, waits for them, and re-layouts: 10.1 us -> 2.23 us
    dynamic_slice x1 -> x0, local copies, waits for them, and re-layouts: 5.02 us -> none  [body(): lost = lax.dynamic_slice_in_dim(cache, (1 - core) * half, half, 0)]
    unnamed x12 -> x8, local copies, waits for them, and re-layouts: 3.69 us -> 0.02 us
  transfers between devices with their start and end apart: 2 -> 2, of which waited for: 1 -> 1; matrix products, arithmetic and copies ran while one was open for 2% -> 3% of each run, Pallas kernels for 0% -> 0%
where the time goes in v3:
time: 82.7 us; the launch traced here: 82.5 us
  blocking collectives  37.9 us (46%)
  waiting for transfers between devices  19.3 us (23%)
  Pallas kernels  13.6 us (16%)
  starting transfers between devices  8.84 us (11%)
  local copies, waits for them, and re-layouts  2.23 us (3%)
    all_to_all x1, blocking collectives, body(): parts = lax.all_to_all(mine, 'ctx', 0, 0, tiled=True)  22.8 us
    all_to_all x1, waiting for transfers between devices, body(): here = lax.all_to_all(own, 'ctx', 0, 0, tiled=True)  19.3 us
    all_to_all x1, blocking collectives, body(): terms = lax.all_to_all(terms, 'ctx', 0, 0, tiled=True)  15.2 us
    pallas_call x1, Pallas kernels, attend(): pl.pallas_call(functools.partial(attend_kernel, new_count=new_count), out...  10.3 us
    all_to_all x1, starting transfers between devices, body(): here = lax.all_to_all(own, 'ctx', 0, 0, tiled=True)  5.6 us
    ppermute x1, starting transfers between devices, body(): came = lax.ppermute(cache, 'ctx', partners)  3.24 us
    pallas_call x1, Pallas kernels, project(): pl.pallas_call(functools.partial(project_kernel, new_count=new_count), ou...  2.58 us
  transfers between devices with their start and end apart: 2, of which 1 were waited for; matrix products, arithmetic and copies ran while one was open for 3% of the time, Pallas kernels for 0%

profile of v3, /device:TPU:1, one launch (start us, length us, event | category | flops | bytes accessed | tf_op | source)
XLA Modules:
  0.0 82.5 jit_solution(9572960740356121408)
XLA Ops:
  0.0 3.2 %collective-permute-start = (bf16[8,576,1024]{2,1,0:T(8,128)(2,1)}, bf16[8,576,1024]{2,1,0:T(8,128)(2,1)}, u32[]{:S(2)}, u32[]{:S(2)}) collective-permute-start(bf16[8,576,1024]{2,1,0:T(8,128)(2,1)} %bitcast.10), channel_id=1, source_target_pairs={{0,1},{1,0},{2,3},{3,2},{4,5},{5,4},{6,7},{7,6},{8,9},{9,8},{10,11... | collective-permute-start | bytes 28311560 | tf_op jit(solution)/shard_map/ppermute | solution.py:254
  3.2 0.9 %copy.7 = bf16[8,2,4,576]{3,2,1,0:T(4,128)(2,1)S(1)} copy(bf16[8,2,4,576]{3,1,2,0:T(2,128)(2,1)} %bitcast.12) | data formatting | bytes 147456 | tf_op jit(solution)/shard_map/transpose | solution.py:250
  4.2 1.2 %broadcast_in_dim.5 = bf16[16,2,32,576]{3,2,1,0:T(8,128)(2,1)} broadcast(bf16[2,32,576]{2,1,0:T(8,128)(2,1)S(1)} %broadcast_in_dim.4), dimensions={1,2,3} | broadcast | bytes 1253376 | tf_op jit(solution)/shard_map/broadcast_in_dim | solution.py:251
  5.4 0.0 copy-start.3
  5.5 0.0 copy-start.2
  5.5 5.6 %all-to-all-start = ((bf16[32,32,576]{2,1,0:T(8,128)(2,1)}), bf16[32,32,576]{2,1,0:T(8,128)(2,1)S(1)}, u32[]{:S(2)}, u32[]{:S(2)}) async-start(bf16[32,32,576]{2,1,0:T(8,128)(2,1)} %bitcast.5), calls=%async_computation | async-start | bytes 2621440 | tf_op jit(solution)/shard_map/all_to_all | solution.py:252
  11.1 0.1 pad_add_fusion.scalars_ref
  11.2 0.0 copy-done.3
  11.2 0.1 add_convert_fusion
  11.2 0.2 fusion
  11.4 0.1 pad_maximum_fusion
  11.5 19.3 %all-to-all-done.query_ref = bf16[32,32,576]{2,1,0:T(8,128)(2,1)S(1)} async-done(((bf16[32,32,576]{2,1,0:T(8,128)(2,1)}), bf16[32,32,576]{2,1,0:T(8,128)(2,1)S(1)}, u32[]{:S(2)}, u32[]{:S(2)}) %all-to-all-start) | async-done | bytes 1179680 | tf_op jit(solution)/shard_map/all_to_all | solution.py:252
  30.9 0.0 collective-permute-done.came_ref
  30.9 0.0 copy-done.2
  30.9 0.0 copy-start
  30.9 10.3 %attend.1 = bf16[32,144,128]{2,1,0:T(8,128)(2,1)S(1)} custom-call(s32[3]{0:T(128)S(1)} %pad_add_fusion.scalars_ref, s32[8]{0:T(128)S(1)} %copy-done.2, bf16[8,576,1024]{2,1,0:T(8,128)(2,1)} %bitcast.11, bf16[8,576,1024]{2,1,0:T(8,128)(2,1)} %collective-permute-done.came_ref, bf16[32,32,576]{2,1,0:T(8,128)(2,1)S(1)} %all-to-all-done.query_ref, ...), custom_call_target="tpu_custom_call" | custom-call | flops 4563402752 | bytes 10616832 | tf_op jit(solution)/shard_map/attend/pallas_call | solution.py:140
  41.2 0.0 copy-start.1
  41.2 22.8 %all_to_all.15.parts_ref = bf16[32,144,128]{2,1,0:T(8,128)(2,1)S(1)} all-to-all(bf16[32,144,128]{2,1,0:T(8,128)(2,1)S(1)} %attend.1), channel_id=1, replica_groups=mesh['batch'=8,'ctx'=32] {'ctx'}, dimensions={0} | all-to-all | bytes 2359296 | tf_op jit(solution)/shard_map/all_to_all | solution.py:258
  64.0 0.0 copy-done
  64.0 0.0 copy-done.1
  64.0 2.6 %project.1 = bf16[32,32,224]{2,1,0:T(8,128)(2,1)S(1)} custom-call(bf16[32,144,128]{2,1,0:T(8,128)(2,1)S(1)} %all_to_all.15.parts_ref, bf16[2,512,128]{2,1,0:T(8,128)(2,1)S(1)} %copy-done.1, bf16[256,7168]{1,0:T(8,128)(2,1)S(1)} %copy-done), custom_call_target="tpu_custom_call" | custom-call | tf_op jit(solution)/shard_map/project/pallas_call | solution.py:210
  66.5 15.2 %all_to_all.16.terms_ref = bf16[32,32,224]{2,1,0:T(8,128)(2,1)S(1)} all-to-all(bf16[32,32,224]{2,1,0:T(8,128)(2,1)S(1)} %project.1), channel_id=1, replica_groups=mesh['batch'=8,'ctx'=32] {'ctx'}, dimensions={0} | all-to-all | bytes 917504 | tf_op jit(solution)/shard_map/all_to_all | solution.py:260
  81.7 0.7 total.1
  (4 shorter events, 0.1 us)
Async XLA Ops:
  0.0 30.9 %collective-permute-start = (bf16[8,576,1024]{2,1,0:T(8,128)(2,1)}, bf16[8,576,1024]{2,1,0:T(8,128)(2,1)}, u32[]{:S(2)}, u32[]{:S(2)}) collective-permute-start(bf16[8,576,1024]{2,1,0:T(8,128)(2,1)} %bitcast.10), channel_id=1, source_target_pairs={{0,1},{1,0},{2,3},{3,2},{4,5},{5,4},{6,7},{7,6},{8,9},{9,8},{10,11... | collective-permute-start | bytes 28311560 | tf_op jit(solution)/shard_map/ppermute | solution.py:254
  5.4 5.7 %copy-start.3 = (s32[8]{0:T(128)S(1)}, s32[8]{0:T(128)}, u32[]{:S(2)}) copy-start(s32[8]{0:T(128)} %param.9) | copy-start | bytes 100
  5.5 25.4 %copy-start.2 = (s32[8]{0:T(128)S(1)}, s32[8]{0:T(128)}, u32[]{:S(2)}) copy-start(s32[8]{0:T(128)} %lengths_ref.1) | copy-start | bytes 100
  5.5 25.4 %all-to-all-start = ((bf16[32,32,576]{2,1,0:T(8,128)(2,1)}), bf16[32,32,576]{2,1,0:T(8,128)(2,1)S(1)}, u32[]{:S(2)}, u32[]{:S(2)}) async-start(bf16[32,32,576]{2,1,0:T(8,128)(2,1)} %bitcast.5), calls=%async_computation | async-start | bytes 2621440 | tf_op jit(solution)/shard_map/all_to_all | solution.py:252
  30.9 33.1 %copy-start = (bf16[256,7168]{1,0:T(8,128)(2,1)S(1)}, bf16[256,7168]{1,0:T(8,128)(2,1)}, u32[]{:S(2)}) copy-start(bf16[256,7168]{1,0:T(8,128)(2,1)} %proj_ref.1) | copy-start | bytes 11010052
  41.2 22.8 %copy-start.1 = (bf16[2,512,128]{2,1,0:T(8,128)(2,1)S(1)}, bf16[2,512,128]{2,1,0:T(8,128)(2,1)}, u32[]{:S(2)}) copy-start(bf16[2,512,128]{2,1,0:T(8,128)(2,1)} %up_ref.1) | copy-start | bytes 786436

commit v4 on v3

v4 whole, which is shorter than its diff:
```python
import functools
import math

import jax
import jax.numpy as jnp
from jax import lax
from jax.experimental import pallas as pl
from jax.experimental.pallas import tpu as pltpu
from jax.sharding import Mesh
from jax.sharding import PartitionSpec as P

ROPE = 64
NOPE = 128
LANES = 128
POWER = math.log2(math.e) / math.sqrt(NOPE + ROPE)
HIDDEN = -1e30
VMEM_LIMIT = 24 * 1024 * 1024
LEAST = -1e29


def angle_terms(positions, new_count, repeats):
    half_rope = ROPE // 2
    exponent = jnp.arange(half_rope, dtype=jnp.float32) * (-2.0 / ROPE)
    frequency = jnp.power(jnp.float32(50000.0), exponent)
    token_place = positions[:, None] + jnp.arange(new_count, dtype=jnp.int32)[None, :]
    angles = token_place.astype(jnp.float32)[:, :, None] * frequency
    cosine, sine = jnp.cos(angles), jnp.sin(angles)
    cosines = jnp.concatenate([cosine, cosine], axis=-1)
    sines = jnp.concatenate([-sine, sine], axis=-1)
    return jnp.repeat(cosines, repeats, axis=1), jnp.repeat(sines, repeats, axis=1)


def split_stat(value, lane):
    high = value.astype(jnp.bfloat16).astype(jnp.float32)
    rest = value - high
    middle = rest.astype(jnp.bfloat16).astype(jnp.float32)
    low = rest - middle
    spot = lane % (LANES // 2)
    return jnp.where(spot == 0, high, jnp.where(spot == 1, middle, low))


def join_stat(tile, pair):
    at = pair * (LANES // 2)
    return tile[..., at : at + 1] + tile[..., at + 1 : at + 2] + tile[..., at + 2 : at + 3]


def spread_kernel(query_ref, out_ref, flat_ref):
    rows, new_count, heads, _ = query_ref.shape
    for row in range(rows):
        for token in range(new_count):
            at = (row * new_count + token) * heads
            flat_ref[at : at + heads, :] = query_ref[row, token].astype(jnp.float32)
    flat = flat_ref[...].astype(jnp.bfloat16)
    depth = out_ref.shape[1]
    for peer in range(out_ref.shape[0]):
        at = peer % 2 * depth
        out_ref[peer] = flat[at : at + depth]


def spread(queries, peers):
    rows, new_count, heads, full = queries.shape
    count = rows * new_count * heads
    vmem = pl.BlockSpec(memory_space=pltpu.VMEM)
    return pl.pallas_call(
        spread_kernel,
        out_shape=pltpu.VMEM((peers, count // 2, full), jnp.bfloat16),
        in_specs=[vmem],
        out_specs=vmem,
        scratch_shapes=[pltpu.VMEM((count, full), jnp.float32)],
        compiler_params=pltpu.CompilerParams(vmem_limit_bytes=8 * 1024 * 1024),
        name="spread",
    )(queries)


def attend_kernel(scalars_ref, lengths_ref, own_ref, came_ref, query_ref, cos_ref, sin_ref, out_ref, keys_ref, arrived, *, new_count):
    peers, depth, full = query_ref.shape
    slots, wide, context = keys_ref.shape
    rows = slots // 2
    group = depth // rows
    latent = full - ROPE
    count = peers * group
    column_groups = latent // LANES
    base = scalars_ref[0] * rows
    copies = []
    for row in range(rows):
        for side, ref in enumerate((own_ref, came_ref)):
            slot = row * 2 + side
            copies.append(pltpu.make_async_copy(ref.at[base + row], keys_ref.at[slot, pl.ds(0, full)], arrived.at[slot]))
    for copy in copies:
        copy.start()
    spare = wide - full
    heads = group // new_count
    column = lax.broadcasted_iota(jnp.int32, (peers, group, spare), 2)
    member = lax.broadcasted_iota(jnp.int32, (peers, group, spare), 1)
    flags = jnp.where(column == member // heads, 1.0, 0.0)
    place = lax.broadcasted_iota(jnp.int32, (spare, context), 1)
    token = lax.broadcasted_iota(jnp.int32, (spare, context), 0)
    for slot in range(slots):
        limit = lengths_ref[base + slot // 2] - new_count + 1 - scalars_ref[1 + slot % 2]
        hidden = (token < new_count) & (place >= limit + token)
        keys_ref[slot, full:, :] = jnp.where(hidden, HIDDEN, 0.0).astype(jnp.bfloat16)
    queries = []
    for row in range(rows):
        query = query_ref[:, row // 2 * 2 * group : (row // 2 + 1) * 2 * group, :].astype(jnp.float32)
        query = query[:, row % 2 * group : (row % 2 + 1) * group, :]
        rope = query[:, :, latent:]
        swapped = jnp.concatenate([rope[:, :, ROPE // 2 :], rope[:, :, : ROPE // 2]], axis=-1)
        turned = rope * cos_ref[base + row][None] + swapped * sin_ref[base + row][None]
        query = jnp.concatenate([query[:, :, :latent], turned, flags], axis=-1)
        queries.append(query.reshape(count, wide).astype(jnp.bfloat16))

    def score(slot):
        copies[slot].wait()
        scores = jnp.dot(queries[slot // 2], keys_ref[slot], preferred_element_type=jnp.float32)
        return scores, jnp.maximum(jnp.max(scores, axis=-1, keepdims=True), LEAST)

    def close(first, second):
        (top_a, total_a, out_a), (top_b, total_b, out_b) = first, second
        top = jnp.maximum(top_a, top_b)
        scale_a, scale_b = jnp.exp2((top_a - top) * POWER), jnp.exp2((top_b - top) * POWER)
        total = total_a * scale_a + total_b * scale_b
        seen = total > 0.0
        safe = jnp.where(seen, total, 1.0)
        inverse = 1.0 / safe
        out = out_a * (scale_a * inverse) + out_b * (scale_b * inverse)
        stat = jnp.where(seen, top * POWER + jnp.log2(safe), HIDDEN)
        return out.reshape(peers, group, latent), jnp.broadcast_to(stat, (count, LANES)).reshape(peers, group, LANES)

    sixteen = 2 * group
    at = column_groups * depth
    terms, closed, packed = [], [], []
    ahead = score(0)
    for slot in range(slots):
        scores, top = ahead
        if slot + 1 < slots:
            ahead = score(slot + 1)
        weights = jnp.exp2((scores - top) * POWER)
        total = jnp.sum(weights, axis=-1, keepdims=True)
        out = lax.dot_general(
            weights.astype(jnp.bfloat16),
            keys_ref[slot, :latent],
            (((1,), (1,)), ((), ())),
            preferred_element_type=jnp.float32,
        )
        terms.append((top, total, out))
        if slot % 2 == 1:
            closed.append(close(*terms[-2:]))
        if slot % 4 == 3:
            pair = slot // 4
            (out_a, stat_a), (out_b, stat_b) = closed[-2:]
            both = jnp.concatenate([out_a, out_b], axis=1).astype(jnp.bfloat16)
            for g in range(column_groups):
                start = g * depth + pair * sixteen
                out_ref[:, start : start + sixteen, :] = both[:, :, g * LANES : (g + 1) * LANES]
            stats = jnp.concatenate([stat_a, stat_b], axis=1)
            lane = lax.broadcasted_iota(jnp.int32, stats.shape, 2)
            packed.append(split_stat(stats, lane))
    lane = lax.broadcasted_iota(jnp.int32, packed[0].shape, 2)
    out_ref[:, at : at + sixteen, :] = jnp.where(lane < LANES // 2, packed[0], packed[1]).astype(jnp.bfloat16)


def attend(scalars, lengths, own, came, query, cosines, sines, new_count):
    peers, depth, full = query.shape
    rows = own.shape[0] // 2
    context = own.shape[2]
    latent = full - ROPE
    rows_out = latent // LANES * depth + depth // rows * 2
    count = peers * depth // rows
    smem, vmem, anywhere = (pl.BlockSpec(memory_space=s) for s in (pltpu.SMEM, pltpu.VMEM, pl.ANY))
    own = pltpu.with_memory_space_constraint(own, pltpu.HBM)
    return pl.pallas_call(
        functools.partial(attend_kernel, new_count=new_count),
        out_shape=pltpu.VMEM((peers, rows_out, LANES), jnp.bfloat16),
        in_specs=[smem, smem, anywhere, anywhere, vmem, vmem, vmem],
        out_specs=vmem,
        scratch_shapes=[
            pltpu.VMEM((2 * rows, -(-full // LANES) * LANES, context), jnp.bfloat16),
            pltpu.SemaphoreType.DMA((2 * rows,)),
        ],
        compiler_params=pltpu.CompilerParams(vmem_limit_bytes=VMEM_LIMIT),
        cost_estimate=pl.CostEstimate(
            flops=4 * count * context * (full + latent) * rows,
            bytes_accessed=2 * rows * context * full * 2 + 2 * peers * rows_out * LANES,
            transcendentals=2 * rows * count * context,
        ),
        name="attend",
    )(scalars, lengths, own, came, query, cosines, sines)


def project_kernel(core_ref, parts_ref, own_up_ref, came_up_ref, own_proj_ref, came_proj_ref, out_ref):
    sixteen = 16
    peers, rows_out, _ = parts_ref.shape
    at = rows_out - sixteen
    groups = at // (2 * sixteen)
    flats = []
    for side, up_ref in enumerate((own_up_ref, came_up_ref)):
        heads = up_ref.shape[0]
        member = core_ref[0] if side == 0 else 1 - core_ref[0]
        blocks = []
        stat_tiles = [parts_ref[2 * k + member, at:, :].astype(jnp.float32) for k in range(peers // 2)]
        for pair in range(2):
            stats = [join_stat(tile, pair) for tile in stat_tiles]
            top = functools.reduce(jnp.maximum, stats)
            weights = [jnp.exp2(stat - top) for stat in stats]
            scale = 1.0 / functools.reduce(jnp.add, weights)
            sums = []
            for g in range(groups):
                start = g * 2 * sixteen + pair * sixteen
                terms = [
                    parts_ref[2 * k + member, start : start + sixteen, :].astype(jnp.float32) * weight
                    for k, weight in enumerate(weights)
                ]
                sums.append(functools.reduce(jnp.add, terms) * scale)
            blocks.append(jnp.concatenate(sums, axis=-1))
        latent = jnp.concatenate(blocks, axis=0).astype(jnp.bfloat16)
        count = latent.shape[0]
        out_row = lax.broadcasted_iota(jnp.int32, (count // heads, count), 0)
        in_row = lax.broadcasted_iota(jnp.int32, (count // heads, count), 1)
        values = []
        for head in range(heads):
            pick = jnp.where(in_row == out_row * heads + head, 1.0, 0.0).astype(jnp.bfloat16)
            chosen = jnp.dot(pick, latent, preferred_element_type=jnp.float32).astype(jnp.bfloat16)
            values.append(jnp.dot(chosen, up_ref[head], preferred_element_type=jnp.float32).astype(jnp.bfloat16))
        flats.append(jnp.concatenate(values, axis=-1))
    width = out_ref.shape[2]
    step = 4
    for first in range(0, out_ref.shape[0], step):
        columns = slice(first * width, (first + step) * width)
        terms = jnp.dot(flats[0], own_proj_ref[:, columns], preferred_element_type=jnp.float32)
        terms += jnp.dot(flats[1], came_proj_ref[:, columns], preferred_element_type=jnp.float32)
        for k in range(step):
            out_ref[first + k] = terms[:, k * width : (k + 1) * width].astype(jnp.bfloat16)


def project(core, parts, own_up, came_up, own_proj, came_proj):
    peers, rows_out, lanes = parts.shape
    heads, latent, _ = own_up.shape
    columns = own_proj.shape[1]
    tokens = (rows_out - 16) // (latent // lanes) // heads
    smem, vmem = (pl.BlockSpec(memory_space=space) for space in (pltpu.SMEM, pltpu.VMEM))
    return pl.pallas_call(
        project_kernel,
        out_shape=pltpu.VMEM((peers, tokens, columns // peers), jnp.bfloat16),
        in_specs=[smem] + [vmem] * 5,
        out_specs=vmem,
        compiler_params=pltpu.CompilerParams(vmem_limit_bytes=16 * 1024 * 1024),
        name="project",
    )(core, parts, own_up, came_up, own_proj, came_proj)


def total_kernel(terms_ref, out_ref):
    rows, new_count, _ = out_ref.shape
    half = rows // 2
    for core in range(2):
        terms = [terms_ref[k].astype(jnp.float32) for k in range(core, terms_ref.shape[0], 2)]
        result = functools.reduce(jnp.add, terms).astype(jnp.bfloat16)
        for row in range(half):
            out_ref[core * half + row] = result[row * new_count : (row + 1) * new_count]


def total(terms, rows, new_count):
    vmem = pl.BlockSpec(memory_space=pltpu.VMEM)
    return pl.pallas_call(
        total_kernel,
        out_shape=jax.ShapeDtypeStruct((rows, new_count, terms.shape[2]), jnp.bfloat16),
        in_specs=[vmem],
        out_specs=vmem,
        compiler_params=pltpu.CompilerParams(vmem_limit_bytes=8 * 1024 * 1024),
        name="total",
    )(terms)


def body(latent_cache, queries, lengths, positions, value_up, out_proj):
    row_count, context_dev, full = latent_cache.shape
    new_count, heads_dev = queries.shape[1], queries.shape[2]
    core = lax.axis_index("core")
    shard = lax.axis_index("chip") * 2 + core
    peers = lax.axis_size("chip") * 2
    both = ("chip", "core")
    swap = [(0, 1), (1, 0)]
    cache = jnp.swapaxes(latent_cache, 1, 2)
    came = lax.ppermute(cache, "core", swap)
    query = lax.all_to_all(spread(queries, peers), both, 0, 0, tiled=True)
    cosines, sines = angle_terms(positions, new_count, heads_dev)
    scalars = jnp.stack([core, shard * context_dev, (shard ^ 1) * context_dev]).astype(jnp.int32)
    mine = attend(scalars, lengths, cache, came, query, cosines, sines, new_count)
    query, value_up, out_proj = lax.optimization_barrier((query, value_up, out_proj))
    came_up = lax.ppermute(value_up, "core", swap)
    came_proj = lax.ppermute(out_proj, "core", swap)
    parts = lax.all_to_all(mine, "chip", 0, 0, tiled=True)
    terms = project(scalars[:1], parts, value_up, came_up, out_proj, came_proj)
    terms = lax.all_to_all(terms, both, 0, 0, tiled=True)
    return total(terms, row_count, new_count)


def solution(mesh):
    batch, ctx = mesh.devices.shape
    mesh = Mesh(mesh.devices.reshape(batch, ctx // 2, 2), ("batch", "chip", "core"))
    ctx = ("chip", "core")
    in_specs = (
        P("batch", ctx, None),
        P("batch", None, ctx, None),
        P("batch"),
        P("batch"),
        P(ctx, None, None),
        P(ctx, None),
    )
    out_specs = P("batch", None, ctx)
    return jax.shard_map(body, mesh=mesh, in_specs=in_specs, out_specs=out_specs, check_vma=False)
```

time: 82.7 us -> 83.8 us (1.013)
  Pallas kernels: 13.6 us -> 16.8 us
  blocking collectives: 37.9 us -> 39.6 us
  local copies, waits for them, and re-layouts: 2.23 us -> 0.93 us
  starting transfers between devices: 8.84 us -> 7.55 us
  waiting for transfers between devices: 19.3 us -> 18.1 us
    pallas_call x1 -> x2, Pallas kernels: 2.58 us -> 5.36 us  [the longest x1 5.2 us: project(): pl.pallas_call(project_kernel, out_shape=pltpu.VMEM((peers, tokens, colum...]
    all_to_all x1, waiting for transfers between devices: 19.3 us -> 16.9 us  [body(): parts = lax.all_to_all(mine, 'chip', 0, 0, tiled=True)]
    all_to_all x1, starting transfers between devices: 5.6 us -> 3.71 us  [body(): parts = lax.all_to_all(mine, 'chip', 0, 0, tiled=True)]
    all_to_all x2, blocking collectives: 37.9 us -> 39.6 us  [the longest x1 25.5 us: body(): query = lax.all_to_all(spread(queries, peers), both, 0, 0, tiled=True)]
    broadcast_in_dim x2, local copies, waits for them, and re-layouts: 1.28 us -> 0.03 us  [the longest x1 0.01 us: angle_terms(): jnp.repeat(cosines, repeats, axis=1)]
    ppermute x1 -> x3, waiting for transfers between devices: 0.01 us -> 1.22 us  [the longest x1 1.22 us: body(): came_up = lax.ppermute(value_up, 'core', swap)]
    transpose x1 -> x0, local copies, waits for them, and re-layouts: 0.92 us -> none  [body(): own = queries.transpose(0, 2, 1, 3).reshape(1, 2, depth, full)]
    unnamed x8, local copies, waits for them, and re-layouts: 0.02 us -> 0.9 us
  transfers between devices with their start and end apart: 2 -> 4, of which waited for: 1 -> 2; matrix products, arithmetic and copies ran while one was open for 3% -> 1% of each run, Pallas kernels for 0% -> 13%
where the time goes in v4:
time: 83.8 us; the launch traced here: 83.5 us
  blocking collectives  39.6 us (47%)
  waiting for transfers between devices  18.1 us (22%)
  Pallas kernels  16.8 us (20%)
  starting transfers between devices  7.55 us (9%)
  local copies, waits for them, and re-layouts  0.93 us (1%)
    all_to_all x1, blocking collectives, body(): query = lax.all_to_all(spread(queries, peers), both, 0, 0, tiled=True)  25.5 us
    all_to_all x1, waiting for transfers between devices, body(): parts = lax.all_to_all(mine, 'chip', 0, 0, tiled=True)  16.9 us
    all_to_all x1, blocking collectives, body(): terms = lax.all_to_all(terms, both, 0, 0, tiled=True)  14.1 us
    pallas_call x1, Pallas kernels, attend(): pl.pallas_call(functools.partial(attend_kernel, new_count=new_count), out...  10.8 us
    pallas_call x1, Pallas kernels, project(): pl.pallas_call(project_kernel, out_shape=pltpu.VMEM((peers, tokens, colum...  5.2 us
    all_to_all x1, starting transfers between devices, body(): parts = lax.all_to_all(mine, 'chip', 0, 0, tiled=True)  3.71 us
    ppermute x1, starting transfers between devices, body(): came = lax.ppermute(cache, 'core', swap)  3.24 us
  transfers between devices with their start and end apart: 4, of which 2 were waited for; matrix products, arithmetic and copies ran while one was open for 1% of the time, Pallas kernels for 13%

profile of v4, /device:TPU:1, one launch (start us, length us, event | category | flops | bytes accessed | tf_op | source)
XLA Modules:
  0.0 83.5 jit_solution(7020513278580681463)
XLA Ops:
  0.0 0.0 copy-start.3
  0.0 3.2 %collective-permute-start = (bf16[8,576,1024]{2,1,0:T(8,128)(2,1)}, bf16[8,576,1024]{2,1,0:T(8,128)(2,1)}, u32[]{:S(2)}, u32[]{:S(2)}) collective-permute-start(bf16[8,576,1024]{2,1,0:T(8,128)(2,1)} %bitcast.8), channel_id=1, source_target_pairs={{0,1},{1,0},{2,3},{3,2},{4,5},{5,4},{6,7},{7,6},{8,9},{9,8},{10,11... | collective-permute-start | bytes 28311560 | tf_op jit(solution)/shard_map/ppermute | solution.py:282
  3.2 0.9 %copy-done.1 = bf16[8,4,2,576]{3,2,1,0:T(2,128)(2,1)S(1)} copy-done((bf16[8,4,2,576]{3,2,1,0:T(2,128)(2,1)S(1)}, bf16[8,4,2,576]{3,2,1,0:T(2,128)(2,1)}, u32[]{:S(2)}) %copy-start.1) | copy-done | bytes 73752
  4.1 0.2 spread.1
  4.3 25.5 %all_to_all.15.query_ref = bf16[32,32,576]{2,1,0:T(8,128)(2,1)S(1)} all-to-all(bf16[32,32,576]{2,1,0:T(8,128)(2,1)S(1)} %spread.1), channel_id=1, replica_groups=mesh['batch'=8,'chip'=16,'core'=2] {'chip','core'}, dimensions={0} | all-to-all | bytes 2359296 | tf_op jit(solution)/shard_map/all_to_all | solution.py:283
  29.8 0.2 collective-permute-start.2
  30.0 0.1 pad_add_fusion.scalars_ref
  30.1 0.0 copy-done.3
  30.1 0.1 add_convert_fusion
  30.1 0.2 fusion
  30.3 0.1 pad_maximum_fusion
  30.4 0.0 collective-permute-done.came_ref
  30.5 0.0 copy-done.2
  30.5 0.0 copy-start
  30.5 10.8 %attend.1 = bf16[32,144,128]{2,1,0:T(8,128)(2,1)} custom-call(s32[3]{0:T(128)S(1)} %pad_add_fusion.scalars_ref, s32[8]{0:T(128)S(1)} %copy-done.2, bf16[8,576,1024]{2,1,0:T(8,128)(2,1)} %bitcast.9, bf16[8,576,1024]{2,1,0:T(8,128)(2,1)} %collective-permute-done.came_ref, bf16[32,32,576]{2,1,0:T(8,128)(2,1)S(1)} %all_to_all.15.query_ref, ...), custom_call_target="tpu_custom_call" | custom-call | flops 4563402752 | bytes 10616832 | tf_op jit(solution)/shard_map/attend/pallas_call | solution.py:171
  41.3 3.7 %all-to-all-start.1 = ((bf16[32,144,128]{2,1,0:T(8,128)(2,1)}), bf16[32,144,128]{2,1,0:T(8,128)(2,1)S(1)}, u32[]{:S(2)}, u32[]{:S(2)}) async-start(bf16[32,144,128]{2,1,0:T(8,128)(2,1)} %attend.1), calls=%async_computation.1 | async-start | bytes 2359296 | tf_op jit(solution)/shard_map/all_to_all | solution.py:290
  45.0 0.0 copy-done
  45.0 0.4 collective-permute-start.1
  45.4 1.2 %collective-permute-done.1.came_up_ref = bf16[2,512,128]{2,1,0:T(8,128)(2,1)S(1)} collective-permute-done((bf16[2,512,128]{2,1,0:T(8,128)(2,1)S(1)}, bf16[2,512,128]{2,1,0:T(8,128)(2,1)S(1)}, u32[]{:S(2)}, u32[]{:S(2)}) %collective-permute-start.1) | collective-permute-done | bytes 262176 | tf_op jit(solution)/shard_map/ppermute | solution.py:288
  46.6 0.0 collective-permute-done.2.came_proj_ref
  46.6 16.9 %all-to-all-done.1.parts_ref = bf16[32,144,128]{2,1,0:T(8,128)(2,1)S(1)} async-done(((bf16[32,144,128]{2,1,0:T(8,128)(2,1)}), bf16[32,144,128]{2,1,0:T(8,128)(2,1)S(1)}, u32[]{:S(2)}, u32[]{:S(2)}) %all-to-all-start.1) | async-done | bytes 1179680 | tf_op jit(solution)/shard_map/all_to_all | solution.py:290
  63.5 5.2 %project.1 = bf16[32,16,224]{2,1,0:T(8,128)(2,1)S(1)} custom-call(s32[1]{0:T(128)} %bitcast.core_ref, bf16[32,144,128]{2,1,0:T(8,128)(2,1)S(1)} %all-to-all-done.1.parts_ref, bf16[2,512,128]{2,1,0:T(8,128)(2,1)S(1)} %copy-done, bf16[2,512,128]{2,1,0:T(8,128)(2,1)S(1)} %collective-permute-done.1.came_up_ref, bf16[256,7168]{1,0:T(8,128)(2,1)} %own_proj_ref, ...), custom_call_target="tpu_custom_call" | custom-call | tf_op jit(solution)/shard_map/project/pallas_call | solution.py:241
  68.7 14.1 %all_to_all.16.terms_ref = bf16[32,16,224]{2,1,0:T(8,128)(2,1)S(1)} all-to-all(bf16[32,16,224]{2,1,0:T(8,128)(2,1)S(1)} %project.1), channel_id=1, replica_groups=mesh['batch'=8,'chip'=16,'core'=2] {'chip','core'}, dimensions={0} | all-to-all | bytes 458752 | tf_op jit(solution)/shard_map/all_to_all | solution.py:292
  82.8 0.7 total.1
  (5 shorter events, 0.0 us)
Async XLA Ops:
  0.0 30.1 %copy-start.3 = (s32[8]{0:T(128)S(1)}, s32[8]{0:T(128)}, u32[]{:S(2)}) copy-start(s32[8]{0:T(128)} %param.9) | copy-start | bytes 100
  0.0 30.5 %copy-start.2 = (s32[8]{0:T(128)S(1)}, s32[8]{0:T(128)}, u32[]{:S(2)}) copy-start(s32[8]{0:T(128)} %lengths_ref.1) | copy-start | bytes 100
  0.0 30.4 %collective-permute-start = (bf16[8,576,1024]{2,1,0:T(8,128)(2,1)}, bf16[8,576,1024]{2,1,0:T(8,128)(2,1)}, u32[]{:S(2)}, u32[]{:S(2)}) collective-permute-start(bf16[8,576,1024]{2,1,0:T(8,128)(2,1)} %bitcast.8), channel_id=1, source_target_pairs={{0,1},{1,0},{2,3},{3,2},{4,5},{5,4},{6,7},{7,6},{8,9},{9,8},{10,11... | collective-permute-start | bytes 28311560 | tf_op jit(solution)/shard_map/ppermute | solution.py:282
  3.2 0.9 %copy-start.1 = (bf16[8,4,2,576]{3,2,1,0:T(2,128)(2,1)S(1)}, bf16[8,4,2,576]{3,2,1,0:T(2,128)(2,1)}, u32[]{:S(2)}) copy-start(bf16[8,4,2,576]{3,2,1,0:T(2,128)(2,1)} %query_ref.1) | copy-start | bytes 221188
  29.8 16.8 %collective-permute-start.2 = (bf16[256,7168]{1,0:T(8,128)(2,1)}, bf16[256,7168]{1,0:T(8,128)(2,1)}, u32[]{:S(2)}, u32[]{:S(2)}) collective-permute-start(bf16[256,7168]{1,0:T(8,128)(2,1)} %own_proj_ref), channel_id=1, source_target_pairs={{0,1},{1,0},{2,3},{3,2},{4,5},{5,4},{6,7},{7,6},{8,9},{9,8},{10,11... | collective-permute-start | bytes 11010056 | tf_op jit(solution)/shard_map/ppermute | solution.py:289
  30.5 14.5 %copy-start = (bf16[2,512,128]{2,1,0:T(8,128)(2,1)S(1)}, bf16[2,512,128]{2,1,0:T(8,128)(2,1)}, u32[]{:S(2)}) copy-start(bf16[2,512,128]{2,1,0:T(8,128)(2,1)} %own_up_ref) | copy-start | bytes 786436
  41.3 22.3 %all-to-all-start.1 = ((bf16[32,144,128]{2,1,0:T(8,128)(2,1)}), bf16[32,144,128]{2,1,0:T(8,128)(2,1)S(1)}, u32[]{:S(2)}, u32[]{:S(2)}) async-start(bf16[32,144,128]{2,1,0:T(8,128)(2,1)} %attend.1), calls=%async_computation.1 | async-start | bytes 2359296 | tf_op jit(solution)/shard_map/all_to_all | solution.py:290
  45.0 1.6 %collective-permute-start.1 = (bf16[2,512,128]{2,1,0:T(8,128)(2,1)S(1)}, bf16[2,512,128]{2,1,0:T(8,128)(2,1)S(1)}, u32[]{:S(2)}, u32[]{:S(2)}) collective-permute-start(bf16[2,512,128]{2,1,0:T(8,128)(2,1)S(1)} %copy-done), channel_id=1, source_target_pairs={{0,1},{1,0},{2,3},{3,2},{4,5},{5,4},{6,7},{7,6},{8,9},{9,8},{10,11... | collective-permute-start | bytes 786440 | tf_op jit(solution)/shard_map/ppermute | solution.py:288

commit v5 on v4

--- a/solution.py
+++ b/solution.py
@@ -187,17 +187,16 @@
     )(scalars, lengths, own, came, query, cosines, sines)
 
 
-def project_kernel(core_ref, parts_ref, own_up_ref, came_up_ref, own_proj_ref, came_proj_ref, out_ref):
+def project_kernel(parts_ref, up_ref, proj_ref, out_ref):
     sixteen = 16
     peers, rows_out, _ = parts_ref.shape
     at = rows_out - sixteen
     groups = at // (2 * sixteen)
-    flats = []
-    for side, up_ref in enumerate((own_up_ref, came_up_ref)):
-        heads = up_ref.shape[0]
-        member = core_ref[0] if side == 0 else 1 - core_ref[0]
-        blocks = []
-        stat_tiles = [parts_ref[2 * k + member, at:, :].astype(jnp.float32) for k in range(peers // 2)]
+    heads = up_ref.shape[0]
+    blocks = []
+    for half in range(2):
+        chosen = range(half, peers, 2)
+        stat_tiles = [parts_ref[k, at:, :].astype(jnp.float32) for k in chosen]
         for pair in range(2):
             stats = [join_stat(tile, pair) for tile in stat_tiles]
             top = functools.reduce(jnp.maximum, stats)
@@ -207,55 +206,52 @@
             for g in range(groups):
                 start = g * 2 * sixteen + pair * sixteen
                 terms = [
-                    parts_ref[2 * k + member, start : start + sixteen, :].astype(jnp.float32) * weight
-                    for k, weight in enumerate(weights)
+                    parts_ref[k, start : start + sixteen, :].astype(jnp.float32) * weight
+                    for k, weight in zip(chosen, weights)
                 ]
                 sums.append(functools.reduce(jnp.add, terms) * scale)
             blocks.append(jnp.concatenate(sums, axis=-1))
-        latent = jnp.concatenate(blocks, axis=0).astype(jnp.bfloat16)
-        count = latent.shape[0]
-        out_row = lax.broadcasted_iota(jnp.int32, (count // heads, count), 0)
-        in_row = lax.broadcasted_iota(jnp.int32, (count // heads, count), 1)
-        values = []
-        for head in range(heads):
-            pick = jnp.where(in_row == out_row * heads + head, 1.0, 0.0).astype(jnp.bfloat16)
-            chosen = jnp.dot(pick, latent, preferred_element_type=jnp.float32).astype(jnp.bfloat16)
-            values.append(jnp.dot(chosen, up_ref[head], preferred_element_type=jnp.float32).astype(jnp.bfloat16))
-        flats.append(jnp.concatenate(values, axis=-1))
+    latent = jnp.concatenate(blocks, axis=0).astype(jnp.bfloat16)
+    count = latent.shape[0]
+    out_row = lax.broadcasted_iota(jnp.int32, (count // heads, count), 0)
+    in_row = lax.broadcasted_iota(jnp.int32, (count // heads, count), 1)
+    values = []
+    for head in range(heads):
+        pick = jnp.where(in_row == out_row * heads + head, 1.0, 0.0).astype(jnp.bfloat16)
+        own = jnp.dot(pick, latent, preferred_element_type=jnp.float32).astype(jnp.bfloat16)
+        values.append(jnp.dot(own, up_ref[head], preferred_element_type=jnp.float32).astype(jnp.bfloat16))
+    flat = jnp.concatenate(values, axis=-1)
     width = out_ref.shape[2]
     step = 4
     for first in range(0, out_ref.shape[0], step):
         columns = slice(first * width, (first + step) * width)
-        terms = jnp.dot(flats[0], own_proj_ref[:, columns], preferred_element_type=jnp.float32)
-        terms += jnp.dot(flats[1], came_proj_ref[:, columns], preferred_element_type=jnp.float32)
+        terms = jnp.dot(flat, proj_ref[:, columns], preferred_element_type=jnp.float32)
         for k in range(step):
             out_ref[first + k] = terms[:, k * width : (k + 1) * width].astype(jnp.bfloat16)
 
 
-def project(core, parts, own_up, came_up, own_proj, came_proj):
+def project(parts, value_up, out_proj):
     peers, rows_out, lanes = parts.shape
-    heads, latent, _ = own_up.shape
-    columns = own_proj.shape[1]
-    tokens = (rows_out - 16) // (latent // lanes) // heads
-    smem, vmem = (pl.BlockSpec(memory_space=space) for space in (pltpu.SMEM, pltpu.VMEM))
+    heads, latent, _ = value_up.shape
+    columns = out_proj.shape[1]
+    tokens = (rows_out - 16) // (latent // lanes) * 2 // heads
+    vmem = pl.BlockSpec(memory_space=pltpu.VMEM)
     return pl.pallas_call(
         project_kernel,
         out_shape=pltpu.VMEM((peers, tokens, columns // peers), jnp.bfloat16),
-        in_specs=[smem] + [vmem] * 5,
+        in_specs=[vmem] * 3,
         out_specs=vmem,
         compiler_params=pltpu.CompilerParams(vmem_limit_bytes=16 * 1024 * 1024),
         name="project",
-    )(core, parts, own_up, came_up, own_proj, came_proj)
+    )(parts, value_up, out_proj)
 
 
 def total_kernel(terms_ref, out_ref):
     rows, new_count, _ = out_ref.shape
-    half = rows // 2
-    for core in range(2):
-        terms = [terms_ref[k].astype(jnp.float32) for k in range(core, terms_ref.shape[0], 2)]
-        result = functools.reduce(jnp.add, terms).astype(jnp.bfloat16)
-        for row in range(half):
-            out_ref[core * half + row] = result[row * new_count : (row + 1) * new_count]
+    terms = [terms_ref[k].astype(jnp.float32) for k in range(terms_ref.shape[0])]
+    result = functools.reduce(jnp.add, terms).astype(jnp.bfloat16)
+    for row in range(rows):
+        out_ref[row] = result[row * new_count : (row + 1) * new_count]
 
 
 def total(terms, rows, new_count):
@@ -284,11 +280,8 @@
     cosines, sines = angle_terms(positions, new_count, heads_dev)
     scalars = jnp.stack([core, shard * context_dev, (shard ^ 1) * context_dev]).astype(jnp.int32)
     mine = attend(scalars, lengths, cache, came, query, cosines, sines, new_count)
-    query, value_up, out_proj = lax.optimization_barrier((query, value_up, out_proj))
-    came_up = lax.ppermute(value_up, "core", swap)
-    came_proj = lax.ppermute(out_proj, "core", swap)
-    parts = lax.all_to_all(mine, "chip", 0, 0, tiled=True)
-    terms = project(scalars[:1], parts, value_up, came_up, out_proj, came_proj)
+    parts = lax.all_to_all(mine, both, 0, 0, tiled=True)
+    terms = project(parts, value_up, out_proj)
     terms = lax.all_to_all(terms, both, 0, 0, tiled=True)
     return total(terms, row_count, new_count)
 

time: 83.8 us -> 81.4 us (0.971)
  Pallas kernels: 16.8 us -> 13.5 us
  blocking collectives: 39.6 us -> 37.9 us
  starting transfers between devices: 7.55 us -> 8.84 us
  waiting for transfers between devices: 18.1 us -> 19.3 us
    pallas_call x1, Pallas kernels: 5.2 us -> 1.52 us  [project(): pl.pallas_call(project_kernel, out_shape=pltpu.VMEM((peers, tokens, colum...]
    all_to_all x1, blocking collectives: 25.5 us -> 22.7 us  [body(): parts = lax.all_to_all(mine, both, 0, 0, tiled=True)]
    all_to_all x1, waiting for transfers between devices: 16.9 us -> 19.3 us  [body(): query = lax.all_to_all(spread(queries, peers), both, 0, 0, tiled=True)]
    all_to_all x1, starting transfers between devices: 3.71 us -> 5.6 us  [body(): query = lax.all_to_all(spread(queries, peers), both, 0, 0, tiled=True)]
    ppermute x2 -> x0, waiting for transfers between devices: 1.22 us -> none  [the longest x1 1.22 us: body(): came_up = lax.ppermute(value_up, 'core', swap)]
    all_to_all x1, blocking collectives: 14.1 us -> 15.2 us  [body(): terms = lax.all_to_all(terms, both, 0, 0, tiled=True)]
    pallas_call x1, Pallas kernels: 0.16 us -> 1.23 us  [spread(): pl.pallas_call(spread_kernel, out_shape=pltpu.VMEM((peers, count // 2, fu...]
  transfers between devices with their start and end apart: 4 -> 2, of which waited for: 2 -> 1; matrix products, arithmetic and copies ran while one was open for 1% -> 1% of each run, Pallas kernels for 13% -> 2%
where the time goes in v5:
time: 81.4 us; the launch traced here: 81.1 us
  blocking collectives  37.9 us (47%)
  waiting for transfers between devices  19.3 us (24%)
  Pallas kernels  13.5 us (17%)
  starting transfers between devices  8.84 us (11%)
  local copies, waits for them, and re-layouts  0.93 us (1%)
    all_to_all x1, blocking collectives, body(): parts = lax.all_to_all(mine, both, 0, 0, tiled=True)  22.7 us
    all_to_all x1, waiting for transfers between devices, body(): query = lax.all_to_all(spread(queries, peers), both, 0, 0, tiled=True)  19.3 us
    all_to_all x1, blocking collectives, body(): terms = lax.all_to_all(terms, both, 0, 0, tiled=True)  15.2 us
    pallas_call x1, Pallas kernels, attend(): pl.pallas_call(functools.partial(attend_kernel, new_count=new_count), out...  10.1 us
    all_to_all x1, starting transfers between devices, body(): query = lax.all_to_all(spread(queries, peers), both, 0, 0, tiled=True)  5.6 us
    ppermute x1, starting transfers between devices, body(): came = lax.ppermute(cache, 'core', swap)  3.24 us
  transfers between devices with their start and end apart: 2, of which 1 were waited for; matrix products, arithmetic and copies ran while one was open for 1% of the time, Pallas kernels for 2%

profile of v5, /device:TPU:1, one launch (start us, length us, event | category | flops | bytes accessed | tf_op | source)
XLA Modules:
  0.0 81.1 jit_solution(9743311001148661576)
XLA Ops:
  0.0 3.2 %collective-permute-start = (bf16[8,576,1024]{2,1,0:T(8,128)(2,1)}, bf16[8,576,1024]{2,1,0:T(8,128)(2,1)}, u32[]{:S(2)}, u32[]{:S(2)}) collective-permute-start(bf16[8,576,1024]{2,1,0:T(8,128)(2,1)} %bitcast.8), channel_id=1, source_target_pairs={{0,1},{1,0},{2,3},{3,2},{4,5},{5,4},{6,7},{7,6},{8,9},{9,8},{10,11... | collective-permute-start | bytes 28311560 | tf_op jit(solution)/shard_map/ppermute | solution.py:278
  3.2 0.0 copy-start.2
  3.2 0.9 %copy-done.2 = bf16[8,4,2,576]{3,2,1,0:T(2,128)(2,1)S(1)} copy-done((bf16[8,4,2,576]{3,2,1,0:T(2,128)(2,1)S(1)}, bf16[8,4,2,576]{3,2,1,0:T(2,128)(2,1)}, u32[]{:S(2)}) %copy-start.2) | copy-done | bytes 73752
  4.1 1.2 %spread.1 = bf16[32,32,576]{2,1,0:T(8,128)(2,1)} custom-call(bf16[8,4,2,576]{3,2,1,0:T(2,128)(2,1)S(1)} %copy-done.2), custom_call_target="tpu_custom_call" | custom-call | tf_op jit(solution)/shard_map/spread/pallas_call | solution.py:64
  5.4 0.0 copy-start.4
  5.4 0.0 copy-start.3
  5.4 5.6 %all-to-all-start = ((bf16[32,32,576]{2,1,0:T(8,128)(2,1)}), bf16[32,32,576]{2,1,0:T(8,128)(2,1)S(1)}, u32[]{:S(2)}, u32[]{:S(2)}) async-start(bf16[32,32,576]{2,1,0:T(8,128)(2,1)} %spread.1), calls=%async_computation | async-start | bytes 2621440 | tf_op jit(solution)/shard_map/all_to_all | solution.py:279
  11.0 0.1 pad_add_fusion.scalars_ref
  11.1 0.0 copy-done.4
  11.1 0.1 add_convert_fusion
  11.1 0.2 fusion
  11.3 0.1 pad_maximum_fusion
  11.4 19.3 %all-to-all-done.query_ref = bf16[32,32,576]{2,1,0:T(8,128)(2,1)S(1)} async-done(((bf16[32,32,576]{2,1,0:T(8,128)(2,1)}), bf16[32,32,576]{2,1,0:T(8,128)(2,1)S(1)}, u32[]{:S(2)}, u32[]{:S(2)}) %all-to-all-start) | async-done | bytes 1179680 | tf_op jit(solution)/shard_map/all_to_all | solution.py:279
  30.8 0.0 collective-permute-done.came_ref
  30.8 0.0 copy-done.3
  30.8 0.0 copy-start
  30.8 10.1 %attend.1 = bf16[32,144,128]{2,1,0:T(8,128)(2,1)S(1)} custom-call(s32[3]{0:T(128)S(1)} %pad_add_fusion.scalars_ref, s32[8]{0:T(128)S(1)} %copy-done.3, bf16[8,576,1024]{2,1,0:T(8,128)(2,1)} %bitcast.9, bf16[8,576,1024]{2,1,0:T(8,128)(2,1)} %collective-permute-done.came_ref, bf16[32,32,576]{2,1,0:T(8,128)(2,1)S(1)} %all-to-all-done.query_ref, ...), custom_call_target="tpu_custom_call" | custom-call | flops 4563402752 | bytes 10616832 | tf_op jit(solution)/shard_map/attend/pallas_call | solution.py:171
  40.9 0.0 copy-start.1
  40.9 22.7 %all_to_all.15.parts_ref = bf16[32,144,128]{2,1,0:T(8,128)(2,1)S(1)} all-to-all(bf16[32,144,128]{2,1,0:T(8,128)(2,1)S(1)} %attend.1), channel_id=1, replica_groups=mesh['batch'=8,'chip'=16,'core'=2] {'chip','core'}, dimensions={0} | all-to-all | bytes 2359296 | tf_op jit(solution)/shard_map/all_to_all | solution.py:283
  63.7 0.0 copy-done
  63.7 0.0 copy-done.1
  63.7 1.5 %project.1 = bf16[32,32,224]{2,1,0:T(8,128)(2,1)S(1)} custom-call(bf16[32,144,128]{2,1,0:T(8,128)(2,1)S(1)} %all_to_all.15.parts_ref, bf16[2,512,128]{2,1,0:T(8,128)(2,1)S(1)} %copy-done.1, bf16[256,7168]{1,0:T(8,128)(2,1)S(1)} %copy-done), custom_call_target="tpu_custom_call" | custom-call | tf_op jit(solution)/shard_map/project/pallas_call | solution.py:239
  65.2 15.2 %all_to_all.16.terms_ref = bf16[32,32,224]{2,1,0:T(8,128)(2,1)S(1)} all-to-all(bf16[32,32,224]{2,1,0:T(8,128)(2,1)S(1)} %project.1), channel_id=1, replica_groups=mesh['batch'=8,'chip'=16,'core'=2] {'chip','core'}, dimensions={0} | all-to-all | bytes 917504 | tf_op jit(solution)/shard_map/all_to_all | solution.py:285
  80.4 0.7 total.1
  (3 shorter events, 0.0 us)
Async XLA Ops:
  0.0 30.8 %collective-permute-start = (bf16[8,576,1024]{2,1,0:T(8,128)(2,1)}, bf16[8,576,1024]{2,1,0:T(8,128)(2,1)}, u32[]{:S(2)}, u32[]{:S(2)}) collective-permute-start(bf16[8,576,1024]{2,1,0:T(8,128)(2,1)} %bitcast.8), channel_id=1, source_target_pairs={{0,1},{1,0},{2,3},{3,2},{4,5},{5,4},{6,7},{7,6},{8,9},{9,8},{10,11... | collective-permute-start | bytes 28311560 | tf_op jit(solution)/shard_map/ppermute | solution.py:278
  3.2 0.9 %copy-start.2 = (bf16[8,4,2,576]{3,2,1,0:T(2,128)(2,1)S(1)}, bf16[8,4,2,576]{3,2,1,0:T(2,128)(2,1)}, u32[]{:S(2)}) copy-start(bf16[8,4,2,576]{3,2,1,0:T(2,128)(2,1)} %query_ref.1) | copy-start | bytes 221188
  5.4 5.7 %copy-start.4 = (s32[8]{0:T(128)S(1)}, s32[8]{0:T(128)}, u32[]{:S(2)}) copy-start(s32[8]{0:T(128)} %param.9) | copy-start | bytes 100
  5.4 25.4 %copy-start.3 = (s32[8]{0:T(128)S(1)}, s32[8]{0:T(128)}, u32[]{:S(2)}) copy-start(s32[8]{0:T(128)} %lengths_ref.1) | copy-start | bytes 100
  5.4 25.4 %all-to-all-start = ((bf16[32,32,576]{2,1,0:T(8,128)(2,1)}), bf16[32,32,576]{2,1,0:T(8,128)(2,1)S(1)}, u32[]{:S(2)}, u32[]{:S(2)}) async-start(bf16[32,32,576]{2,1,0:T(8,128)(2,1)} %spread.1), calls=%async_computation | async-start | bytes 2621440 | tf_op jit(solution)/shard_map/all_to_all | solution.py:279
  30.8 32.9 %copy-start = (bf16[256,7168]{1,0:T(8,128)(2,1)S(1)}, bf16[256,7168]{1,0:T(8,128)(2,1)}, u32[]{:S(2)}) copy-start(bf16[256,7168]{1,0:T(8,128)(2,1)} %proj_ref.1) | copy-start | bytes 11010052
  40.9 22.8 %copy-start.1 = (bf16[2,512,128]{2,1,0:T(8,128)(2,1)S(1)}, bf16[2,512,128]{2,1,0:T(8,128)(2,1)}, u32[]{:S(2)}) copy-start(bf16[2,512,128]{2,1,0:T(8,128)(2,1)} %up_ref.1) | copy-start | bytes 786436

commit v6 on v5

--- a/solution.py
+++ b/solution.py
@@ -44,39 +44,45 @@
     return tile[..., at : at + 1] + tile[..., at + 1 : at + 2] + tile[..., at + 2 : at + 3]
 
 
-def spread_kernel(query_ref, out_ref, flat_ref):
-    rows, new_count, heads, _ = query_ref.shape
+def spread_kernel(query_ref, cos_ref, sin_ref, out_ref, flat_ref):
+    rows, new_count, heads, full = query_ref.shape
+    latent = full - ROPE
     for row in range(rows):
         for token in range(new_count):
             at = (row * new_count + token) * heads
             flat_ref[at : at + heads, :] = query_ref[row, token].astype(jnp.float32)
-    flat = flat_ref[...].astype(jnp.bfloat16)
+    flat = flat_ref[...]
+    rope = flat[:, latent:]
+    swapped = jnp.concatenate([rope[:, ROPE // 2 :], rope[:, : ROPE // 2]], axis=-1)
+    turned = rope * cos_ref[...].reshape(rope.shape) + swapped * sin_ref[...].reshape(rope.shape)
+    flat = jnp.concatenate([flat[:, :latent], turned], axis=-1).astype(jnp.bfloat16)
     depth = out_ref.shape[1]
     for peer in range(out_ref.shape[0]):
         at = peer % 2 * depth
         out_ref[peer] = flat[at : at + depth]
 
 
-def spread(queries, peers):
+def spread(queries, cosines, sines, peers):
     rows, new_count, heads, full = queries.shape
     count = rows * new_count * heads
     vmem = pl.BlockSpec(memory_space=pltpu.VMEM)
     return pl.pallas_call(
         spread_kernel,
         out_shape=pltpu.VMEM((peers, count // 2, full), jnp.bfloat16),
-        in_specs=[vmem],
+        in_specs=[vmem] * 3,
         out_specs=vmem,
         scratch_shapes=[pltpu.VMEM((count, full), jnp.float32)],
         compiler_params=pltpu.CompilerParams(vmem_limit_bytes=8 * 1024 * 1024),
         name="spread",
-    )(queries)
-
-
-def attend_kernel(scalars_ref, lengths_ref, own_ref, came_ref, query_ref, cos_ref, sin_ref, out_ref, keys_ref, arrived, *, new_count):
+    )(queries, cosines, sines)
+
+
+def attend_kernel(scalars_ref, lengths_ref, own_ref, came_ref, query_ref, out_ref, keys_ref, arrived, *, new_count, mode=0):
     peers, depth, full = query_ref.shape
-    slots, wide, context = keys_ref.shape
-    rows = slots // 2
+    rows, wide, context = keys_ref.shape
+    span = context // 2
     group = depth // rows
+    heads = group // new_count
     latent = full - ROPE
     count = peers * group
     column_groups = latent // LANES
@@ -84,69 +90,56 @@
     copies = []
     for row in range(rows):
         for side, ref in enumerate((own_ref, came_ref)):
-            slot = row * 2 + side
-            copies.append(pltpu.make_async_copy(ref.at[base + row], keys_ref.at[slot, pl.ds(0, full)], arrived.at[slot]))
+            target = keys_ref.at[row, pl.ds(0, full), pl.ds(side * span, span)]
+            copies.append(pltpu.make_async_copy(ref.at[base + row], target, arrived.at[row * 2 + side]))
     for copy in copies:
         copy.start()
     spare = wide - full
-    heads = group // new_count
     column = lax.broadcasted_iota(jnp.int32, (peers, group, spare), 2)
     member = lax.broadcasted_iota(jnp.int32, (peers, group, spare), 1)
     flags = jnp.where(column == member // heads, 1.0, 0.0)
-    place = lax.broadcasted_iota(jnp.int32, (spare, context), 1)
-    token = lax.broadcasted_iota(jnp.int32, (spare, context), 0)
-    for slot in range(slots):
-        limit = lengths_ref[base + slot // 2] - new_count + 1 - scalars_ref[1 + slot % 2]
-        hidden = (token < new_count) & (place >= limit + token)
-        keys_ref[slot, full:, :] = jnp.where(hidden, HIDDEN, 0.0).astype(jnp.bfloat16)
+    place = lax.broadcasted_iota(jnp.int32, (spare, span), 1)
+    token = lax.broadcasted_iota(jnp.int32, (spare, span), 0)
     queries = []
     for row in range(rows):
+        for side in range(2):
+            limit = lengths_ref[base + row] - new_count + 1 - scalars_ref[1 + side]
+            hidden = (token < new_count) & (place >= limit + token)
+            keys_ref[row, full:, side * span : (side + 1) * span] = jnp.where(hidden, HIDDEN, 0.0).astype(jnp.bfloat16)
         query = query_ref[:, row // 2 * 2 * group : (row // 2 + 1) * 2 * group, :].astype(jnp.float32)
-        query = query[:, row % 2 * group : (row % 2 + 1) * group, :]
-        rope = query[:, :, latent:]
-        swapped = jnp.concatenate([rope[:, :, ROPE // 2 :], rope[:, :, : ROPE // 2]], axis=-1)
-        turned = rope * cos_ref[base + row][None] + swapped * sin_ref[base + row][None]
-        query = jnp.concatenate([query[:, :, :latent], turned, flags], axis=-1)
+        query = jnp.concatenate([query[:, row % 2 * group : (row % 2 + 1) * group, :], flags], axis=-1)
         queries.append(query.reshape(count, wide).astype(jnp.bfloat16))
 
-    def score(slot):
-        copies[slot].wait()
-        scores = jnp.dot(queries[slot // 2], keys_ref[slot], preferred_element_type=jnp.float32)
+    def score(row):
+        copies[2 * row].wait()
+        copies[2 * row + 1].wait()
+        scores = jnp.dot(queries[row], keys_ref[row], preferred_element_type=jnp.float32)
         return scores, jnp.maximum(jnp.max(scores, axis=-1, keepdims=True), LEAST)
-
-    def close(first, second):
-        (top_a, total_a, out_a), (top_b, total_b, out_b) = first, second
-        top = jnp.maximum(top_a, top_b)
-        scale_a, scale_b = jnp.exp2((top_a - top) * POWER), jnp.exp2((top_b - top) * POWER)
-        total = total_a * scale_a + total_b * scale_b
-        seen = total > 0.0
-        safe = jnp.where(seen, total, 1.0)
-        inverse = 1.0 / safe
-        out = out_a * (scale_a * inverse) + out_b * (scale_b * inverse)
-        stat = jnp.where(seen, top * POWER + jnp.log2(safe), HIDDEN)
-        return out.reshape(peers, group, latent), jnp.broadcast_to(stat, (count, LANES)).reshape(peers, group, LANES)
 
     sixteen = 2 * group
     at = column_groups * depth
-    terms, closed, packed = [], [], []
+    closed, packed = [], []
     ahead = score(0)
-    for slot in range(slots):
+    for row in range(rows):
         scores, top = ahead
-        if slot + 1 < slots:
-            ahead = score(slot + 1)
+        if row + 1 < rows:
+            ahead = score(row + 1)
         weights = jnp.exp2((scores - top) * POWER)
         total = jnp.sum(weights, axis=-1, keepdims=True)
         out = lax.dot_general(
             weights.astype(jnp.bfloat16),
-            keys_ref[slot, :latent],
+            keys_ref[row, :latent],
             (((1,), (1,)), ((), ())),
             preferred_element_type=jnp.float32,
         )
-        terms.append((top, total, out))
-        if slot % 2 == 1:
-            closed.append(close(*terms[-2:]))
-        if slot % 4 == 3:
-            pair = slot // 4
+        seen = total > 0.0
+        safe = jnp.where(seen, total, 1.0)
+        out = out * (1.0 / safe)
+        stat = jnp.where(seen, top * POWER + jnp.log2(safe), HIDDEN)
+        stat = jnp.broadcast_to(stat, (count, LANES)).reshape(peers, group, LANES)
+        closed.append((out.reshape(peers, group, latent), stat))
+        if row % 2 == 1:
+            pair = row // 2
             (out_a, stat_a), (out_b, stat_b) = closed[-2:]
             both = jnp.concatenate([out_a, out_b], axis=1).astype(jnp.bfloat16)
             for g in range(column_groups):
@@ -159,7 +152,7 @@
     out_ref[:, at : at + sixteen, :] = jnp.where(lane < LANES // 2, packed[0], packed[1]).astype(jnp.bfloat16)
 
 
-def attend(scalars, lengths, own, came, query, cosines, sines, new_count):
+def attend(scalars, lengths, own, came, query, new_count):
     peers, depth, full = query.shape
     rows = own.shape[0] // 2
     context = own.shape[2]
@@ -171,10 +164,10 @@
     return pl.pallas_call(
         functools.partial(attend_kernel, new_count=new_count),
         out_shape=pltpu.VMEM((peers, rows_out, LANES), jnp.bfloat16),
-        in_specs=[smem, smem, anywhere, anywhere, vmem, vmem, vmem],
+        in_specs=[smem, smem, anywhere, anywhere, vmem],
         out_specs=vmem,
         scratch_shapes=[
-            pltpu.VMEM((2 * rows, -(-full // LANES) * LANES, context), jnp.bfloat16),
+            pltpu.VMEM((rows, -(-full // LANES) * LANES, 2 * context), jnp.bfloat16),
             pltpu.SemaphoreType.DMA((2 * rows,)),
         ],
         compiler_params=pltpu.CompilerParams(vmem_limit_bytes=VMEM_LIMIT),
@@ -184,7 +177,7 @@
             transcendentals=2 * rows * count * context,
         ),
         name="attend",
-    )(scalars, lengths, own, came, query, cosines, sines)
+    )(scalars, lengths, own, came, query)
 
 
 def project_kernel(parts_ref, up_ref, proj_ref, out_ref):
@@ -276,10 +269,10 @@
     swap = [(0, 1), (1, 0)]
     cache = jnp.swapaxes(latent_cache, 1, 2)
     came = lax.ppermute(cache, "core", swap)
-    query = lax.all_to_all(spread(queries, peers), both, 0, 0, tiled=True)
     cosines, sines = angle_terms(positions, new_count, heads_dev)
+    query = lax.all_to_all(spread(queries, cosines, sines, peers), both, 0, 0, tiled=True)
     scalars = jnp.stack([core, shard * context_dev, (shard ^ 1) * context_dev]).astype(jnp.int32)
-    mine = attend(scalars, lengths, cache, came, query, cosines, sines, new_count)
+    mine = attend(scalars, lengths, cache, came, query, new_count)
     parts = lax.all_to_all(mine, both, 0, 0, tiled=True)
     terms = project(parts, value_up, out_proj)
     terms = lax.all_to_all(terms, both, 0, 0, tiled=True)

time: 81.4 us -> 82.2 us (level)
  no operation moved by 1% of the time
where the time goes in v6:
time: 82.2 us; the launch traced here: 81.9 us
  blocking collectives  37.9 us (46%)
  waiting for transfers between devices  19.7 us (24%)
  Pallas kernels  13.3 us (16%)
  starting transfers between devices  8.83 us (11%)
  other arithmetic  1.1 us (1%)
  local copies, waits for them, and re-layouts  0.92 us (1%)
    all_to_all x1, blocking collectives, body(): parts = lax.all_to_all(mine, both, 0, 0, tiled=True)  22.7 us
    all_to_all x1, waiting for transfers between devices, body(): lax.all_to_all(spread(queries, cosines, sines, peers), both, 0, 0, tiled=...  19.7 us
    all_to_all x1, blocking collectives, body(): terms = lax.all_to_all(terms, both, 0, 0, tiled=True)  15.2 us
    pallas_call x1, Pallas kernels, attend(): pl.pallas_call(functools.partial(attend_kernel, new_count=new_count), out...  9.73 us
    all_to_all x1, starting transfers between devices, body(): lax.all_to_all(spread(queries, cosines, sines, peers), both, 0, 0, tiled=...  5.59 us
    ppermute x1, starting transfers between devices, body(): came = lax.ppermute(cache, 'core', swap)  3.24 us
  transfers between devices with their start and end apart: 2, of which 1 were waited for; matrix products, arithmetic and copies ran while one was open for 1% of the time, Pallas kernels for 2%

profile of v6, /device:TPU:1, one launch (start us, length us, event | category | flops | bytes accessed | tf_op | source)
XLA Modules:
  0.0 81.9 jit_solution(10297742427130552898)
XLA Ops:
  0.0 3.2 %collective-permute-start = (bf16[8,576,1024]{2,1,0:T(8,128)(2,1)}, bf16[8,576,1024]{2,1,0:T(8,128)(2,1)}, u32[]{:S(2)}, u32[]{:S(2)}) collective-permute-start(bf16[8,576,1024]{2,1,0:T(8,128)(2,1)} %bitcast.8), channel_id=1, source_target_pairs={{0,1},{1,0},{2,3},{3,2},{4,5},{5,4},{6,7},{7,6},{8,9},{9,8},{10,11... | collective-permute-start | bytes 28311560 | tf_op jit(solution)/shard_map/ppermute | solution.py:271
  3.3 0.7 add_convert_fusion
  4.0 0.2 fusion
  4.2 0.1 pad_maximum_fusion
  4.3 0.0 copy-start.2
  4.3 0.9 %copy-done.2 = bf16[8,4,2,576]{3,2,1,0:T(2,128)(2,1)S(1)} copy-done((bf16[8,4,2,576]{3,2,1,0:T(2,128)(2,1)S(1)}, bf16[8,4,2,576]{3,2,1,0:T(2,128)(2,1)}, u32[]{:S(2)}) %copy-start.2) | copy-done | bytes 73752
  5.2 1.3 %spread.1 = bf16[32,32,576]{2,1,0:T(8,128)(2,1)} custom-call(bf16[8,4,2,576]{3,2,1,0:T(2,128)(2,1)S(1)} %copy-done.2, f32[8,8,64]{2,1,0:T(8,128)S(1)} %bitcast.6, f32[8,8,64]{2,1,0:T(8,128)S(1)} %bitcast.7), custom_call_target="tpu_custom_call" | custom-call | tf_op jit(solution)/shard_map/spread/pallas_call | solution.py:69
  6.5 0.0 copy-start.3
  6.5 5.6 %all-to-all-start = ((bf16[32,32,576]{2,1,0:T(8,128)(2,1)}), bf16[32,32,576]{2,1,0:T(8,128)(2,1)S(1)}, u32[]{:S(2)}, u32[]{:S(2)}) async-start(bf16[32,32,576]{2,1,0:T(8,128)(2,1)} %spread.1), calls=%async_computation | async-start | bytes 2621440 | tf_op jit(solution)/shard_map/all_to_all | solution.py:273
  12.2 0.1 pad_add_fusion.scalars_ref
  12.2 19.7 %all-to-all-done.query_ref = bf16[32,32,576]{2,1,0:T(8,128)(2,1)S(1)} async-done(((bf16[32,32,576]{2,1,0:T(8,128)(2,1)}), bf16[32,32,576]{2,1,0:T(8,128)(2,1)S(1)}, u32[]{:S(2)}, u32[]{:S(2)}) %all-to-all-start) | async-done | bytes 1179680 | tf_op jit(solution)/shard_map/all_to_all | solution.py:273
  31.9 0.0 collective-permute-done.came_ref
  31.9 0.0 copy-done.3
  31.9 0.0 copy-start
  32.0 9.7 %attend.1 = bf16[32,144,128]{2,1,0:T(8,128)(2,1)S(1)} custom-call(s32[3]{0:T(128)S(1)} %pad_add_fusion.scalars_ref, s32[8]{0:T(128)S(1)} %copy-done.3, bf16[8,576,1024]{2,1,0:T(8,128)(2,1)} %bitcast.9, bf16[8,576,1024]{2,1,0:T(8,128)(2,1)} %collective-permute-done.came_ref, bf16[32,32,576]{2,1,0:T(8,128)(2,1)S(1)} %all-to-all-done.query_ref), custom_call_target="tpu_custom_call" | custom-call | flops 4563402752 | bytes 10616832 | tf_op jit(solution)/shard_map/attend/pallas_call | solution.py:164
  41.7 0.0 copy-start.1
  41.7 22.7 %all_to_all.15.parts_ref = bf16[32,144,128]{2,1,0:T(8,128)(2,1)S(1)} all-to-all(bf16[32,144,128]{2,1,0:T(8,128)(2,1)S(1)} %attend.1), channel_id=1, replica_groups=mesh['batch'=8,'chip'=16,'core'=2] {'chip','core'}, dimensions={0} | all-to-all | bytes 2359296 | tf_op jit(solution)/shard_map/all_to_all | solution.py:276
  64.4 0.0 copy-done
  64.4 0.0 copy-done.1
  64.5 1.5 %project.1 = bf16[32,32,224]{2,1,0:T(8,128)(2,1)S(1)} custom-call(bf16[32,144,128]{2,1,0:T(8,128)(2,1)S(1)} %all_to_all.15.parts_ref, bf16[2,512,128]{2,1,0:T(8,128)(2,1)S(1)} %copy-done.1, bf16[256,7168]{1,0:T(8,128)(2,1)S(1)} %copy-done), custom_call_target="tpu_custom_call" | custom-call | tf_op jit(solution)/shard_map/project/pallas_call | solution.py:232
  66.0 15.2 %all_to_all.16.terms_ref = bf16[32,32,224]{2,1,0:T(8,128)(2,1)S(1)} all-to-all(bf16[32,32,224]{2,1,0:T(8,128)(2,1)S(1)} %project.1), channel_id=1, replica_groups=mesh['batch'=8,'chip'=16,'core'=2] {'chip','core'}, dimensions={0} | all-to-all | bytes 917504 | tf_op jit(solution)/shard_map/all_to_all | solution.py:278
  81.2 0.7 total.1
  (3 shorter events, 0.0 us)
Async XLA Ops:
  0.0 31.9 %collective-permute-start = (bf16[8,576,1024]{2,1,0:T(8,128)(2,1)}, bf16[8,576,1024]{2,1,0:T(8,128)(2,1)}, u32[]{:S(2)}, u32[]{:S(2)}) collective-permute-start(bf16[8,576,1024]{2,1,0:T(8,128)(2,1)} %bitcast.8), channel_id=1, source_target_pairs={{0,1},{1,0},{2,3},{3,2},{4,5},{5,4},{6,7},{7,6},{8,9},{9,8},{10,11... | collective-permute-start | bytes 28311560 | tf_op jit(solution)/shard_map/ppermute | solution.py:271
  4.3 0.9 %copy-start.2 = (bf16[8,4,2,576]{3,2,1,0:T(2,128)(2,1)S(1)}, bf16[8,4,2,576]{3,2,1,0:T(2,128)(2,1)}, u32[]{:S(2)}) copy-start(bf16[8,4,2,576]{3,2,1,0:T(2,128)(2,1)} %query_ref.1) | copy-start | bytes 221188
  6.5 25.4 %copy-start.3 = (s32[8]{0:T(128)S(1)}, s32[8]{0:T(128)}, u32[]{:S(2)}) copy-start(s32[8]{0:T(128)} %lengths_ref.1) | copy-start | bytes 100
  6.5 25.4 %all-to-all-start = ((bf16[32,32,576]{2,1,0:T(8,128)(2,1)}), bf16[32,32,576]{2,1,0:T(8,128)(2,1)S(1)}, u32[]{:S(2)}, u32[]{:S(2)}) async-start(bf16[32,32,576]{2,1,0:T(8,128)(2,1)} %spread.1), calls=%async_computation | async-start | bytes 2621440 | tf_op jit(solution)/shard_map/all_to_all | solution.py:273
  31.9 32.5 %copy-start = (bf16[256,7168]{1,0:T(8,128)(2,1)S(1)}, bf16[256,7168]{1,0:T(8,128)(2,1)}, u32[]{:S(2)}) copy-start(bf16[256,7168]{1,0:T(8,128)(2,1)} %proj_ref.1) | copy-start | bytes 11010052
  41.7 22.8 %copy-start.1 = (bf16[2,512,128]{2,1,0:T(8,128)(2,1)S(1)}, bf16[2,512,128]{2,1,0:T(8,128)(2,1)}, u32[]{:S(2)}) copy-start(bf16[2,512,128]{2,1,0:T(8,128)(2,1)} %up_ref.1) | copy-start | bytes 786436

commit v7 on v6

--- a/solution.py
+++ b/solution.py
@@ -3,6 +3,7 @@
 
 import jax
 import jax.numpy as jnp
+import numpy as np
 from jax import lax
 from jax.experimental import pallas as pl
 from jax.experimental.pallas import tpu as pltpu
@@ -18,16 +19,21 @@
 LEAST = -1e29
 
 
-def angle_terms(positions, new_count, repeats):
+def angles(positions, new_count, repeats):
     half_rope = ROPE // 2
-    exponent = jnp.arange(half_rope, dtype=jnp.float32) * (-2.0 / ROPE)
-    frequency = jnp.power(jnp.float32(50000.0), exponent)
-    token_place = positions[:, None] + jnp.arange(new_count, dtype=jnp.int32)[None, :]
-    angles = token_place.astype(jnp.float32)[:, :, None] * frequency
-    cosine, sine = jnp.cos(angles), jnp.sin(angles)
-    cosines = jnp.concatenate([cosine, cosine], axis=-1)
-    sines = jnp.concatenate([-sine, sine], axis=-1)
-    return jnp.repeat(cosines, repeats, axis=1), jnp.repeat(sines, repeats, axis=1)
+    shape = (new_count * repeats, ROPE)
+    lane = lax.broadcasted_iota(jnp.int32, shape, 1)
+    frequency = jnp.zeros(shape, jnp.float32)
+    for i in range(half_rope):
+        value = float(np.float32(50000.0 ** (-2.0 * i / ROPE)))
+        frequency = jnp.where(lane % half_rope == i, value, frequency)
+    token = lax.broadcasted_iota(jnp.int32, shape, 0) // repeats
+    terms = []
+    for position in positions:
+        angle = (position + token).astype(jnp.float32) * frequency
+        sine = jnp.sin(angle)
+        terms.append((jnp.cos(angle), jnp.where(lane < half_rope, -sine, sine)))
+    return terms
 
 
 def split_stat(value, lane):
@@ -44,40 +50,35 @@
     return tile[..., at : at + 1] + tile[..., at + 1 : at + 2] + tile[..., at + 2 : at + 3]
 
 
-def spread_kernel(query_ref, cos_ref, sin_ref, out_ref, flat_ref):
-    rows, new_count, heads, full = query_ref.shape
-    latent = full - ROPE
+def spread_kernel(query_ref, out_ref, flat_ref):
+    rows, new_count, heads, _ = query_ref.shape
     for row in range(rows):
         for token in range(new_count):
             at = (row * new_count + token) * heads
             flat_ref[at : at + heads, :] = query_ref[row, token].astype(jnp.float32)
-    flat = flat_ref[...]
-    rope = flat[:, latent:]
-    swapped = jnp.concatenate([rope[:, ROPE // 2 :], rope[:, : ROPE // 2]], axis=-1)
-    turned = rope * cos_ref[...].reshape(rope.shape) + swapped * sin_ref[...].reshape(rope.shape)
-    flat = jnp.concatenate([flat[:, :latent], turned], axis=-1).astype(jnp.bfloat16)
+    flat = flat_ref[...].astype(jnp.bfloat16)
     depth = out_ref.shape[1]
     for peer in range(out_ref.shape[0]):
         at = peer % 2 * depth
         out_ref[peer] = flat[at : at + depth]
 
 
-def spread(queries, cosines, sines, peers):
+def spread(queries, peers):
     rows, new_count, heads, full = queries.shape
     count = rows * new_count * heads
     vmem = pl.BlockSpec(memory_space=pltpu.VMEM)
     return pl.pallas_call(
         spread_kernel,
         out_shape=pltpu.VMEM((peers, count // 2, full), jnp.bfloat16),
-        in_specs=[vmem] * 3,
+        in_specs=[vmem],
         out_specs=vmem,
         scratch_shapes=[pltpu.VMEM((count, full), jnp.float32)],
         compiler_params=pltpu.CompilerParams(vmem_limit_bytes=8 * 1024 * 1024),
         name="spread",
-    )(queries, cosines, sines)
-
-
-def attend_kernel(scalars_ref, lengths_ref, own_ref, came_ref, query_ref, out_ref, keys_ref, arrived, *, new_count, mode=0):
+    )(queries)
+
+
+def attend_kernel(lengths_ref, positions_ref, own_ref, came_ref, query_ref, out_ref, keys_ref, arrived, *, new_count):
     peers, depth, full = query_ref.shape
     rows, wide, context = keys_ref.shape
     span = context // 2
@@ -86,7 +87,9 @@
     latent = full - ROPE
     count = peers * group
     column_groups = latent // LANES
-    base = scalars_ref[0] * rows
+    core = lax.axis_index("core")
+    base = core * rows
+    starts = [(lax.axis_index("chip") * 2 + place) * span for place in (core, 1 - core)]
     copies = []
     for row in range(rows):
         for side, ref in enumerate((own_ref, came_ref)):
@@ -100,20 +103,28 @@
     flags = jnp.where(column == member // heads, 1.0, 0.0)
     place = lax.broadcasted_iota(jnp.int32, (spare, span), 1)
     token = lax.broadcasted_iota(jnp.int32, (spare, span), 0)
+    turns = angles([positions_ref[base + row] for row in range(rows)], new_count, heads)
     queries = []
     for row in range(rows):
         for side in range(2):
-            limit = lengths_ref[base + row] - new_count + 1 - scalars_ref[1 + side]
+            limit = lengths_ref[base + row] - new_count + 1 - starts[side]
             hidden = (token < new_count) & (place >= limit + token)
             keys_ref[row, full:, side * span : (side + 1) * span] = jnp.where(hidden, HIDDEN, 0.0).astype(jnp.bfloat16)
         query = query_ref[:, row // 2 * 2 * group : (row // 2 + 1) * 2 * group, :].astype(jnp.float32)
-        query = jnp.concatenate([query[:, row % 2 * group : (row % 2 + 1) * group, :], flags], axis=-1)
+        query = query[:, row % 2 * group : (row % 2 + 1) * group, :]
+        rope = query[:, :, latent:]
+        swapped = jnp.concatenate([rope[:, :, ROPE // 2 :], rope[:, :, : ROPE // 2]], axis=-1)
+        turned = rope * turns[row][0][None] + swapped * turns[row][1][None]
+        query = jnp.concatenate([query[:, :, :latent], turned, flags], axis=-1)
         queries.append(query.reshape(count, wide).astype(jnp.bfloat16))
 
     def score(row):
-        copies[2 * row].wait()
-        copies[2 * row + 1].wait()
-        scores = jnp.dot(queries[row], keys_ref[row], preferred_element_type=jnp.float32)
+        halves = []
+        for side in range(2):
+            copies[2 * row + side].wait()
+            keys = keys_ref[row, :, side * span : (side + 1) * span]
+            halves.append(jnp.dot(queries[row], keys, preferred_element_type=jnp.float32))
+        scores = jnp.concatenate(halves, axis=-1)
         return scores, jnp.maximum(jnp.max(scores, axis=-1, keepdims=True), LEAST)
 
     sixteen = 2 * group
@@ -152,7 +163,7 @@
     out_ref[:, at : at + sixteen, :] = jnp.where(lane < LANES // 2, packed[0], packed[1]).astype(jnp.bfloat16)
 
 
-def attend(scalars, lengths, own, came, query, new_count):
+def attend(lengths, positions, own, came, query, new_count):
     peers, depth, full = query.shape
     rows = own.shape[0] // 2
     context = own.shape[2]
@@ -177,7 +188,7 @@
             transcendentals=2 * rows * count * context,
         ),
         name="attend",
-    )(scalars, lengths, own, came, query)
+    )(lengths, positions, own, came, query)
 
 
 def project_kernel(parts_ref, up_ref, proj_ref, out_ref):
@@ -260,19 +271,14 @@
 
 
 def body(latent_cache, queries, lengths, positions, value_up, out_proj):
-    row_count, context_dev, full = latent_cache.shape
-    new_count, heads_dev = queries.shape[1], queries.shape[2]
-    core = lax.axis_index("core")
-    shard = lax.axis_index("chip") * 2 + core
+    row_count, new_count = queries.shape[:2]
     peers = lax.axis_size("chip") * 2
     both = ("chip", "core")
     swap = [(0, 1), (1, 0)]
     cache = jnp.swapaxes(latent_cache, 1, 2)
     came = lax.ppermute(cache, "core", swap)
-    cosines, sines = angle_terms(positions, new_count, heads_dev)
-    query = lax.all_to_all(spread(queries, cosines, sines, peers), both, 0, 0, tiled=True)
-    scalars = jnp.stack([core, shard * context_dev, (shard ^ 1) * context_dev]).astype(jnp.int32)
-    mine = attend(scalars, lengths, cache, came, query, new_count)
+    query = lax.all_to_all(spread(queries, peers), both, 0, 0, tiled=True)
+    mine = attend(lengths, positions, cache, came, query, new_count)
     parts = lax.all_to_all(mine, both, 0, 0, tiled=True)
     terms = project(parts, value_up, out_proj)
     terms = lax.all_to_all(terms, both, 0, 0, tiled=True)

time: 82.2 us -> 80.3 us (0.977)
  blocking collectives: 37.9 us -> 63.2 us
  waiting for transfers between devices: 19.7 us -> 0.01 us
  starting transfers between devices: 8.83 us -> 3.24 us
  other arithmetic: 1.1 us -> 0 us
    all_to_all x0 -> x1, blocking collectives: none -> 25.5 us  [body(): query = lax.all_to_all(spread(queries, peers), both, 0, 0, tiled=True)]
    all_to_all x1 -> x0, waiting for transfers between devices: 19.7 us -> none  [body(): lax.all_to_all(spread(queries, cosines, sines, peers), both, 0, 0, tiled=...]
    all_to_all x1 -> x0, starting transfers between devices: 5.59 us -> none  [body(): lax.all_to_all(spread(queries, cosines, sines, peers), both, 0, 0, tiled=...]
    pallas_call x1, Pallas kernels: 1.33 us -> 0.16 us  [spread(): pl.pallas_call(spread_kernel, out_shape=pltpu.VMEM((peers, count // 2, fu...]
  transfers between devices with their start and end apart: 2 -> 1, of which waited for: 1 -> 0; matrix products, arithmetic and copies ran while one was open for 1% -> 0% of each run, Pallas kernels for 2% -> 0%
where the time goes in v7:
time: 80.3 us; the launch traced here: 80.1 us
  blocking collectives  63.2 us (79%)
  Pallas kernels  12.6 us (16%)
  starting transfers between devices  3.24 us (4%)
  local copies, waits for them, and re-layouts  0.91 us (1%)
    all_to_all x1, blocking collectives, body(): query = lax.all_to_all(spread(queries, peers), both, 0, 0, tiled=True)  25.5 us
    all_to_all x1, blocking collectives, body(): parts = lax.all_to_all(mine, both, 0, 0, tiled=True)  22.5 us
    all_to_all x1, blocking collectives, body(): terms = lax.all_to_all(terms, both, 0, 0, tiled=True)  15.2 us
    pallas_call x1, Pallas kernels, attend(): pl.pallas_call(functools.partial(attend_kernel, new_count=new_count), out...  10.3 us
    ppermute x1, starting transfers between devices, body(): came = lax.ppermute(cache, 'core', swap)  3.24 us
  transfers between devices with their start and end apart: 1, of which 0 were waited for; matrix products, arithmetic and copies ran while one was open for 0% of the time, Pallas kernels for 0%

profile of v7, /device:TPU:1, one launch (start us, length us, event | category | flops | bytes accessed | tf_op | source)
XLA Modules:
  0.0 80.1 jit_solution(14262124191463527683)
XLA Ops:
  0.0 3.2 %collective-permute-start = (bf16[8,576,1024]{2,1,0:T(8,128)(2,1)}, bf16[8,576,1024]{2,1,0:T(8,128)(2,1)S(1)}, u32[]{:S(2)}, u32[]{:S(2)}) collective-permute-start(bf16[8,576,1024]{2,1,0:T(8,128)(2,1)} %bitcast.1), channel_id=1, source_target_pairs={{0,1},{1,0},{2,3},{3,2},{4,5},{5,4},{6,7},{7,6},{8,9},{9,8},{10,11... | collective-permute-start | bytes 28311560 | tf_op jit(solution)/shard_map/ppermute | solution.py:279
  3.2 0.0 copy-start.2
  3.2 0.9 %copy-done.2 = bf16[8,4,2,576]{3,2,1,0:T(2,128)(2,1)S(1)} copy-done((bf16[8,4,2,576]{3,2,1,0:T(2,128)(2,1)S(1)}, bf16[8,4,2,576]{3,2,1,0:T(2,128)(2,1)}, u32[]{:S(2)}) %copy-start.2) | copy-done | bytes 73752
  4.1 0.2 spread.1
  4.3 0.0 copy-start.3
  4.3 0.0 copy-start.4
  4.3 25.5 %all_to_all.15.query_ref = bf16[32,32,576]{2,1,0:T(8,128)(2,1)S(1)} all-to-all(bf16[32,32,576]{2,1,0:T(8,128)(2,1)S(1)} %spread.1), channel_id=1, replica_groups=mesh['batch'=8,'chip'=16,'core'=2] {'chip','core'}, dimensions={0} | all-to-all | bytes 2359296 | tf_op jit(solution)/shard_map/all_to_all | solution.py:280
  29.8 0.0 collective-permute-done.came_ref
  29.8 0.0 copy-done.3
  29.8 0.0 copy-done.4
  29.8 0.0 copy-start
  29.8 10.3 %attend.1 = bf16[32,144,128]{2,1,0:T(8,128)(2,1)S(1)} custom-call(s32[8]{0:T(128)S(1)} %copy-done.3, s32[8]{0:T(128)S(1)} %copy-done.4, bf16[8,576,1024]{2,1,0:T(8,128)(2,1)} %bitcast.2, bf16[8,576,1024]{2,1,0:T(8,128)(2,1)S(1)} %collective-permute-done.came_ref, bf16[32,32,576]{2,1,0:T(8,128)(2,1)S(1)} %all_to_all.15.query_ref), custom_call_target="tpu_custom_call" | custom-call | flops 4563402752 | bytes 10616832 | tf_op jit(solution)/shard_map/attend/pallas_call | solution.py:175
  40.1 0.0 copy-start.1
  40.1 22.5 %all_to_all.16.parts_ref = bf16[32,144,128]{2,1,0:T(8,128)(2,1)S(1)} all-to-all(bf16[32,144,128]{2,1,0:T(8,128)(2,1)S(1)} %attend.1), channel_id=1, replica_groups=mesh['batch'=8,'chip'=16,'core'=2] {'chip','core'}, dimensions={0} | all-to-all | bytes 2359296 | tf_op jit(solution)/shard_map/all_to_all | solution.py:282
  62.7 0.0 copy-done
  62.7 0.0 copy-done.1
  62.7 1.5 %project.1 = bf16[32,32,224]{2,1,0:T(8,128)(2,1)S(1)} custom-call(bf16[32,144,128]{2,1,0:T(8,128)(2,1)S(1)} %all_to_all.16.parts_ref, bf16[2,512,128]{2,1,0:T(8,128)(2,1)S(1)} %copy-done.1, bf16[256,7168]{1,0:T(8,128)(2,1)S(1)} %copy-done), custom_call_target="tpu_custom_call" | custom-call | tf_op jit(solution)/shard_map/project/pallas_call | solution.py:243
  64.2 15.2 %all_to_all.17.terms_ref = bf16[32,32,224]{2,1,0:T(8,128)(2,1)S(1)} all-to-all(bf16[32,32,224]{2,1,0:T(8,128)(2,1)S(1)} %project.1), channel_id=1, replica_groups=mesh['batch'=8,'chip'=16,'core'=2] {'chip','core'}, dimensions={0} | all-to-all | bytes 917504 | tf_op jit(solution)/shard_map/all_to_all | solution.py:284
  79.4 0.7 total.1
Async XLA Ops:
  0.0 29.8 %collective-permute-start = (bf16[8,576,1024]{2,1,0:T(8,128)(2,1)}, bf16[8,576,1024]{2,1,0:T(8,128)(2,1)S(1)}, u32[]{:S(2)}, u32[]{:S(2)}) collective-permute-start(bf16[8,576,1024]{2,1,0:T(8,128)(2,1)} %bitcast.1), channel_id=1, source_target_pairs={{0,1},{1,0},{2,3},{3,2},{4,5},{5,4},{6,7},{7,6},{8,9},{9,8},{10,11... | collective-permute-start | bytes 28311560 | tf_op jit(solution)/shard_map/ppermute | solution.py:279
  3.2 0.9 %copy-start.2 = (bf16[8,4,2,576]{3,2,1,0:T(2,128)(2,1)S(1)}, bf16[8,4,2,576]{3,2,1,0:T(2,128)(2,1)}, u32[]{:S(2)}) copy-start(bf16[8,4,2,576]{3,2,1,0:T(2,128)(2,1)} %query_ref.1) | copy-start | bytes 221188
  4.3 25.5 %copy-start.3 = (s32[8]{0:T(128)S(1)}, s32[8]{0:T(128)}, u32[]{:S(2)}) copy-start(s32[8]{0:T(128)} %lengths_ref.1) | copy-start | bytes 100
  4.3 25.5 %copy-start.4 = (s32[8]{0:T(128)S(1)}, s32[8]{0:T(128)}, u32[]{:S(2)}) copy-start(s32[8]{0:T(128)} %positions_ref.1) | copy-start | bytes 100
  29.8 32.8 %copy-start = (bf16[256,7168]{1,0:T(8,128)(2,1)S(1)}, bf16[256,7168]{1,0:T(8,128)(2,1)}, u32[]{:S(2)}) copy-start(bf16[256,7168]{1,0:T(8,128)(2,1)} %proj_ref.1) | copy-start | bytes 11010052
  40.1 22.5 %copy-start.1 = (bf16[2,512,128]{2,1,0:T(8,128)(2,1)S(1)}, bf16[2,512,128]{2,1,0:T(8,128)(2,1)}, u32[]{:S(2)}) copy-start(bf16[2,512,128]{2,1,0:T(8,128)(2,1)} %up_ref.1) | copy-start | bytes 786436

commit v8 on v7

--- a/solution.py
+++ b/solution.py
@@ -15,6 +15,7 @@
 LANES = 128
 POWER = math.log2(math.e) / math.sqrt(NOPE + ROPE)
 HIDDEN = -1e30
+STRIP = 16
 VMEM_LIMIT = 24 * 1024 * 1024
 LEAST = -1e29
 
@@ -119,26 +120,29 @@
         queries.append(query.reshape(count, wide).astype(jnp.bfloat16))
 
     def score(row):
-        halves = []
-        for side in range(2):
-            copies[2 * row + side].wait()
-            keys = keys_ref[row, :, side * span : (side + 1) * span]
-            halves.append(jnp.dot(queries[row], keys, preferred_element_type=jnp.float32))
-        scores = jnp.concatenate(halves, axis=-1)
-        return scores, jnp.maximum(jnp.max(scores, axis=-1, keepdims=True), LEAST)
+        copies[2 * row].wait()
+        copies[2 * row + 1].wait()
+        scores = jnp.dot(queries[row], keys_ref[row], preferred_element_type=jnp.float32)
+        return scores
 
     sixteen = 2 * group
     at = column_groups * depth
     closed, packed = [], []
     ahead = score(0)
     for row in range(rows):
-        scores, top = ahead
+        scores = ahead
         if row + 1 < rows:
             ahead = score(row + 1)
-        weights = jnp.exp2((scores - top) * POWER)
-        total = jnp.sum(weights, axis=-1, keepdims=True)
+        tops, totals, strips = [], [], []
+        for first in range(0, count, STRIP):
+            strip = scores[first : first + STRIP]
+            tops.append(jnp.maximum(jnp.max(strip, axis=-1, keepdims=True), LEAST))
+            strip = jnp.exp2((strip - tops[-1]) * POWER)
+            totals.append(jnp.sum(strip, axis=-1, keepdims=True))
+            strips.append(strip.astype(jnp.bfloat16))
+        top, total = jnp.concatenate(tops, axis=0), jnp.concatenate(totals, axis=0)
         out = lax.dot_general(
-            weights.astype(jnp.bfloat16),
+            jnp.concatenate(strips, axis=0),
             keys_ref[row, :latent],
             (((1,), (1,)), ((), ())),
             preferred_element_type=jnp.float32,
@@ -279,6 +283,7 @@
     came = lax.ppermute(cache, "core", swap)
     query = lax.all_to_all(spread(queries, peers), both, 0, 0, tiled=True)
     mine = attend(lengths, positions, cache, came, query, new_count)
+    mine, value_up, out_proj = lax.optimization_barrier((mine, value_up, out_proj))
     parts = lax.all_to_all(mine, both, 0, 0, tiled=True)
     terms = project(parts, value_up, out_proj)
     terms = lax.all_to_all(terms, both, 0, 0, tiled=True)

time: 80.3 us -> 79.3 us (0.988)
  Pallas kernels: 12.6 us -> 11.6 us
    pallas_call x1, Pallas kernels: 10.3 us -> 9.23 us  [attend(): pl.pallas_call(functools.partial(attend_kernel, new_count=new_count), out...]
where the time goes in v8:
time: 79.3 us; the launch traced here: 79 us
  blocking collectives  63.2 us (80%)
  Pallas kernels  11.6 us (15%)
  starting transfers between devices  3.24 us (4%)
  local copies, waits for them, and re-layouts  0.91 us (1%)
    all_to_all x1, blocking collectives, body(): query = lax.all_to_all(spread(queries, peers), both, 0, 0, tiled=True)  25.5 us
    all_to_all x1, blocking collectives, body(): parts = lax.all_to_all(mine, both, 0, 0, tiled=True)  22.5 us
    all_to_all x1, blocking collectives, body(): terms = lax.all_to_all(terms, both, 0, 0, tiled=True)  15.2 us
    pallas_call x1, Pallas kernels, attend(): pl.pallas_call(functools.partial(attend_kernel, new_count=new_count), out...  9.23 us
    ppermute x1, starting transfers between devices, body(): came = lax.ppermute(cache, 'core', swap)  3.24 us
  transfers between devices with their start and end apart: 1, of which 0 were waited for; matrix products, arithmetic and copies ran while one was open for 0% of the time, Pallas kernels for 0%

profile of v8, /device:TPU:1, one launch (start us, length us, event | category | flops | bytes accessed | tf_op | source)
XLA Modules:
  0.0 79.0 jit_solution(5395287555138498025)
XLA Ops:
  0.0 3.2 %collective-permute-start = (bf16[8,576,1024]{2,1,0:T(8,128)(2,1)}, bf16[8,576,1024]{2,1,0:T(8,128)(2,1)S(1)}, u32[]{:S(2)}, u32[]{:S(2)}) collective-permute-start(bf16[8,576,1024]{2,1,0:T(8,128)(2,1)} %bitcast.1), channel_id=1, source_target_pairs={{0,1},{1,0},{2,3},{3,2},{4,5},{5,4},{6,7},{7,6},{8,9},{9,8},{10,11... | collective-permute-start | bytes 28311560 | tf_op jit(solution)/shard_map/ppermute | solution.py:283
  3.2 0.0 copy-start.2
  3.2 0.9 %copy-done.2 = bf16[8,4,2,576]{3,2,1,0:T(2,128)(2,1)S(1)} copy-done((bf16[8,4,2,576]{3,2,1,0:T(2,128)(2,1)S(1)}, bf16[8,4,2,576]{3,2,1,0:T(2,128)(2,1)}, u32[]{:S(2)}) %copy-start.2) | copy-done | bytes 73752
  4.1 0.2 spread.1
  4.3 0.0 copy-start.3
  4.3 0.0 copy-start.4
  4.3 25.5 %all_to_all.15.query_ref = bf16[32,32,576]{2,1,0:T(8,128)(2,1)S(1)} all-to-all(bf16[32,32,576]{2,1,0:T(8,128)(2,1)S(1)} %spread.1), channel_id=1, replica_groups=mesh['batch'=8,'chip'=16,'core'=2] {'chip','core'}, dimensions={0} | all-to-all | bytes 2359296 | tf_op jit(solution)/shard_map/all_to_all | solution.py:284
  29.8 0.0 collective-permute-done.came_ref
  29.8 0.0 copy-done.3
  29.8 0.0 copy-done.4
  29.8 0.0 copy-start
  29.8 9.2 %attend.1 = bf16[32,144,128]{2,1,0:T(8,128)(2,1)S(1)} custom-call(s32[8]{0:T(128)S(1)} %copy-done.3, s32[8]{0:T(128)S(1)} %copy-done.4, bf16[8,576,1024]{2,1,0:T(8,128)(2,1)} %bitcast.2, bf16[8,576,1024]{2,1,0:T(8,128)(2,1)S(1)} %collective-permute-done.came_ref, bf16[32,32,576]{2,1,0:T(8,128)(2,1)S(1)} %all_to_all.15.query_ref), custom_call_target="tpu_custom_call" | custom-call | flops 4563402752 | bytes 10616832 | tf_op jit(solution)/shard_map/attend/pallas_call | solution.py:179
  39.1 0.0 copy-start.1
  39.1 22.5 %all_to_all.16.parts_ref = bf16[32,144,128]{2,1,0:T(8,128)(2,1)S(1)} all-to-all(bf16[32,144,128]{2,1,0:T(8,128)(2,1)S(1)} %attend.1), channel_id=1, replica_groups=mesh['batch'=8,'chip'=16,'core'=2] {'chip','core'}, dimensions={0} | all-to-all | bytes 2359296 | tf_op jit(solution)/shard_map/all_to_all | solution.py:287
  61.6 0.0 copy-done
  61.6 0.0 copy-done.1
  61.6 1.5 %project.1 = bf16[32,32,224]{2,1,0:T(8,128)(2,1)S(1)} custom-call(bf16[32,144,128]{2,1,0:T(8,128)(2,1)S(1)} %all_to_all.16.parts_ref, bf16[2,512,128]{2,1,0:T(8,128)(2,1)S(1)} %copy-done.1, bf16[256,7168]{1,0:T(8,128)(2,1)S(1)} %copy-done), custom_call_target="tpu_custom_call" | custom-call | tf_op jit(solution)/shard_map/project/pallas_call | solution.py:247
  63.2 15.2 %all_to_all.17.terms_ref = bf16[32,32,224]{2,1,0:T(8,128)(2,1)S(1)} all-to-all(bf16[32,32,224]{2,1,0:T(8,128)(2,1)S(1)} %project.1), channel_id=1, replica_groups=mesh['batch'=8,'chip'=16,'core'=2] {'chip','core'}, dimensions={0} | all-to-all | bytes 917504 | tf_op jit(solution)/shard_map/all_to_all | solution.py:289
  78.3 0.7 total.1
Async XLA Ops:
  0.0 29.8 %collective-permute-start = (bf16[8,576,1024]{2,1,0:T(8,128)(2,1)}, bf16[8,576,1024]{2,1,0:T(8,128)(2,1)S(1)}, u32[]{:S(2)}, u32[]{:S(2)}) collective-permute-start(bf16[8,576,1024]{2,1,0:T(8,128)(2,1)} %bitcast.1), channel_id=1, source_target_pairs={{0,1},{1,0},{2,3},{3,2},{4,5},{5,4},{6,7},{7,6},{8,9},{9,8},{10,11... | collective-permute-start | bytes 28311560 | tf_op jit(solution)/shard_map/ppermute | solution.py:283
  3.2 0.9 %copy-start.2 = (bf16[8,4,2,576]{3,2,1,0:T(2,128)(2,1)S(1)}, bf16[8,4,2,576]{3,2,1,0:T(2,128)(2,1)}, u32[]{:S(2)}) copy-start(bf16[8,4,2,576]{3,2,1,0:T(2,128)(2,1)} %query_ref.1) | copy-start | bytes 221188
  4.3 25.5 %copy-start.3 = (s32[8]{0:T(128)S(1)}, s32[8]{0:T(128)}, u32[]{:S(2)}) copy-start(s32[8]{0:T(128)} %lengths_ref.1) | copy-start | bytes 100
  4.3 25.5 %copy-start.4 = (s32[8]{0:T(128)S(1)}, s32[8]{0:T(128)}, u32[]{:S(2)}) copy-start(s32[8]{0:T(128)} %positions_ref.1) | copy-start | bytes 100
  29.8 31.8 %copy-start = (bf16[256,7168]{1,0:T(8,128)(2,1)S(1)}, bf16[256,7168]{1,0:T(8,128)(2,1)}, u32[]{:S(2)}) copy-start(bf16[256,7168]{1,0:T(8,128)(2,1)} %proj_ref) | copy-start | bytes 11010052
  39.1 22.6 %copy-start.1 = (bf16[2,512,128]{2,1,0:T(8,128)(2,1)S(1)}, bf16[2,512,128]{2,1,0:T(8,128)(2,1)}, u32[]{:S(2)}) copy-start(bf16[2,512,128]{2,1,0:T(8,128)(2,1)} %up_ref) | copy-start | bytes 786436

commit v9 on v8

--- a/solution.py
+++ b/solution.py
@@ -13,6 +13,7 @@
 ROPE = 64
 NOPE = 128
 LANES = 128
+STAT_LANES = 32
 POWER = math.log2(math.e) / math.sqrt(NOPE + ROPE)
 HIDDEN = -1e30
 STRIP = 16
@@ -42,26 +43,31 @@
     rest = value - high
     middle = rest.astype(jnp.bfloat16).astype(jnp.float32)
     low = rest - middle
-    spot = lane % (LANES // 2)
+    spot = lane % STAT_LANES
     return jnp.where(spot == 0, high, jnp.where(spot == 1, middle, low))
 
 
-def join_stat(tile, pair):
-    at = pair * (LANES // 2)
+def join_stat(tile, row):
+    at = row * STAT_LANES
     return tile[..., at : at + 1] + tile[..., at + 1 : at + 2] + tile[..., at + 2 : at + 3]
 
 
 def spread_kernel(query_ref, out_ref, flat_ref):
-    rows, new_count, heads, _ = query_ref.shape
+    rows, new_count, heads, full = query_ref.shape
+    latent = full - ROPE
     for row in range(rows):
         for token in range(new_count):
             at = (row * new_count + token) * heads
             flat_ref[at : at + heads, :] = query_ref[row, token].astype(jnp.float32)
-    flat = flat_ref[...].astype(jnp.bfloat16)
-    depth = out_ref.shape[1]
-    for peer in range(out_ref.shape[0]):
-        at = peer % 2 * depth
-        out_ref[peer] = flat[at : at + depth]
+    flat = flat_ref[...]
+    depth = flat.shape[0] // 2
+    for half in range(2):
+        mine = flat[half * depth : (half + 1) * depth]
+        pieces = [mine[:, g : g + LANES] for g in range(0, latent, LANES)]
+        pieces.append(jnp.concatenate([mine[: depth // 2, latent:], mine[depth // 2 :, latent:]], axis=-1))
+        block = jnp.concatenate(pieces, axis=0).astype(jnp.bfloat16)
+        for peer in range(half, out_ref.shape[0], 2):
+            out_ref[peer] = block
 
 
 def spread(queries, peers):
@@ -70,7 +76,7 @@
     vmem = pl.BlockSpec(memory_space=pltpu.VMEM)
     return pl.pallas_call(
         spread_kernel,
-        out_shape=pltpu.VMEM((peers, count // 2, full), jnp.bfloat16),
+        out_shape=pltpu.VMEM((peers, count // 2 * full // LANES, LANES), jnp.bfloat16),
         in_specs=[vmem],
         out_specs=vmem,
         scratch_shapes=[pltpu.VMEM((count, full), jnp.float32)],
@@ -80,14 +86,16 @@
 
 
 def attend_kernel(lengths_ref, positions_ref, own_ref, came_ref, query_ref, out_ref, keys_ref, arrived, *, new_count):
-    peers, depth, full = query_ref.shape
+    peers = query_ref.shape[0]
+    full = own_ref.shape[1]
     rows, wide, context = keys_ref.shape
     span = context // 2
+    latent = full - ROPE
+    column_groups = latent // LANES
+    depth = query_ref.shape[1] * LANES // full
     group = depth // rows
     heads = group // new_count
-    latent = full - ROPE
     count = peers * group
-    column_groups = latent // LANES
     core = lax.axis_index("core")
     base = core * rows
     starts = [(lax.axis_index("chip") * 2 + place) * span for place in (core, 1 - core)]
@@ -111,12 +119,16 @@
             limit = lengths_ref[base + row] - new_count + 1 - starts[side]
             hidden = (token < new_count) & (place >= limit + token)
             keys_ref[row, full:, side * span : (side + 1) * span] = jnp.where(hidden, HIDDEN, 0.0).astype(jnp.bfloat16)
-        query = query_ref[:, row // 2 * 2 * group : (row // 2 + 1) * 2 * group, :].astype(jnp.float32)
-        query = query[:, row % 2 * group : (row % 2 + 1) * group, :]
-        rope = query[:, :, latent:]
+        tile, upper = row // 2 * 2 * group, slice(row % 2 * group, (row % 2 + 1) * group)
+        pieces = []
+        for g in range(column_groups):
+            piece = query_ref[:, g * depth + tile : g * depth + tile + 2 * group, :].astype(jnp.float32)
+            pieces.append(piece[:, upper])
+        rope = query_ref[:, column_groups * depth :, :].astype(jnp.float32)
+        rope = rope[:, upper, row // 2 * ROPE : (row // 2 + 1) * ROPE]
         swapped = jnp.concatenate([rope[:, :, ROPE // 2 :], rope[:, :, : ROPE // 2]], axis=-1)
         turned = rope * turns[row][0][None] + swapped * turns[row][1][None]
-        query = jnp.concatenate([query[:, :, :latent], turned, flags], axis=-1)
+        query = jnp.concatenate([*pieces, turned, flags], axis=-1)
         queries.append(query.reshape(count, wide).astype(jnp.bfloat16))
 
     def score(row):
@@ -127,7 +139,8 @@
 
     sixteen = 2 * group
     at = column_groups * depth
-    closed, packed = [], []
+    closed, packed = [], None
+    lane = lax.broadcasted_iota(jnp.int32, (peers, group, LANES), 2)
     ahead = score(0)
     for row in range(rows):
         scores = ahead
@@ -152,28 +165,26 @@
         out = out * (1.0 / safe)
         stat = jnp.where(seen, top * POWER + jnp.log2(safe), HIDDEN)
         stat = jnp.broadcast_to(stat, (count, LANES)).reshape(peers, group, LANES)
-        closed.append((out.reshape(peers, group, latent), stat))
+        closed.append(out.reshape(peers, group, latent))
+        stat = split_stat(stat, lane)
+        packed = stat if packed is None else jnp.where(lane < row * STAT_LANES, packed, stat)
         if row % 2 == 1:
-            pair = row // 2
-            (out_a, stat_a), (out_b, stat_b) = closed[-2:]
-            both = jnp.concatenate([out_a, out_b], axis=1).astype(jnp.bfloat16)
+            both = jnp.concatenate(closed[-2:], axis=1).astype(jnp.bfloat16)
             for g in range(column_groups):
-                start = g * depth + pair * sixteen
+                start = g * depth + row // 2 * sixteen
                 out_ref[:, start : start + sixteen, :] = both[:, :, g * LANES : (g + 1) * LANES]
-            stats = jnp.concatenate([stat_a, stat_b], axis=1)
-            lane = lax.broadcasted_iota(jnp.int32, stats.shape, 2)
-            packed.append(split_stat(stats, lane))
-    lane = lax.broadcasted_iota(jnp.int32, packed[0].shape, 2)
-    out_ref[:, at : at + sixteen, :] = jnp.where(lane < LANES // 2, packed[0], packed[1]).astype(jnp.bfloat16)
+    out_ref[:, at:, :] = packed.astype(jnp.bfloat16)
 
 
 def attend(lengths, positions, own, came, query, new_count):
-    peers, depth, full = query.shape
+    peers = query.shape[0]
     rows = own.shape[0] // 2
-    context = own.shape[2]
+    full, context = own.shape[1:]
     latent = full - ROPE
-    rows_out = latent // LANES * depth + depth // rows * 2
-    count = peers * depth // rows
+    depth = query.shape[1] * LANES // full
+    group = depth // rows
+    rows_out = latent // LANES * depth + group
+    count = peers * group
     smem, vmem, anywhere = (pl.BlockSpec(memory_space=s) for s in (pltpu.SMEM, pltpu.VMEM, pl.ANY))
     own = pltpu.with_memory_space_constraint(own, pltpu.HBM)
     return pl.pallas_call(
@@ -198,21 +209,25 @@
 def project_kernel(parts_ref, up_ref, proj_ref, out_ref):
     sixteen = 16
     peers, rows_out, _ = parts_ref.shape
-    at = rows_out - sixteen
-    groups = at // (2 * sixteen)
-    heads = up_ref.shape[0]
+    heads, wide, _ = up_ref.shape
+    groups = wide // LANES
+    at = rows_out - rows_out % sixteen
+    depth = at // groups
     blocks = []
     for half in range(2):
         chosen = range(half, peers, 2)
         stat_tiles = [parts_ref[k, at:, :].astype(jnp.float32) for k in chosen]
         for pair in range(2):
-            stats = [join_stat(tile, pair) for tile in stat_tiles]
+            stats = [
+                jnp.concatenate([join_stat(tile, 2 * pair), join_stat(tile, 2 * pair + 1)], axis=0)
+                for tile in stat_tiles
+            ]
             top = functools.reduce(jnp.maximum, stats)
             weights = [jnp.exp2(stat - top) for stat in stats]
             scale = 1.0 / functools.reduce(jnp.add, weights)
             sums = []
             for g in range(groups):
-                start = g * 2 * sixteen + pair * sixteen
+                start = g * depth + pair * sixteen
                 terms = [
                     parts_ref[k, start : start + sixteen, :].astype(jnp.float32) * weight
                     for k, weight in zip(chosen, weights)
@@ -229,24 +244,48 @@
         own = jnp.dot(pick, latent, preferred_element_type=jnp.float32).astype(jnp.bfloat16)
         values.append(jnp.dot(own, up_ref[head], preferred_element_type=jnp.float32).astype(jnp.bfloat16))
     flat = jnp.concatenate(values, axis=-1)
-    width = out_ref.shape[2]
+    width = proj_ref.shape[1] // peers
     step = 4
-    for first in range(0, out_ref.shape[0], step):
+    for first in range(0, peers, step):
         columns = slice(first * width, (first + step) * width)
         terms = jnp.dot(flat, proj_ref[:, columns], preferred_element_type=jnp.float32)
         for k in range(step):
-            out_ref[first + k] = terms[:, k * width : (k + 1) * width].astype(jnp.bfloat16)
+            out_ref[first + k] = fold(terms[:, k * width : (k + 1) * width]).astype(jnp.bfloat16)
+
+
+def fold(block):
+    lines, width = block.shape
+    part = lines // 4
+    thin = LANES // 4
+    pieces = [block[:, :LANES]]
+    for at in range(LANES, width, thin):
+        pieces.append(
+            jnp.concatenate([block[m * part : (m + 1) * part, at : at + thin] for m in range(4)], axis=-1)
+        )
+    return jnp.concatenate(pieces, axis=0)
+
+
+def unfold(block, lines):
+    part = lines // 4
+    thin = LANES // 4
+    pieces = [block[:lines]]
+    for at in range(lines, block.shape[0], part):
+        pieces.append(
+            jnp.concatenate([block[at : at + part, m * thin : (m + 1) * thin] for m in range(4)], axis=0)
+        )
+    return jnp.concatenate(pieces, axis=-1)
 
 
 def project(parts, value_up, out_proj):
-    peers, rows_out, lanes = parts.shape
+    peers, rows_out, _ = parts.shape
     heads, latent, _ = value_up.shape
     columns = out_proj.shape[1]
-    tokens = (rows_out - 16) // (latent // lanes) * 2 // heads
+    tokens = rows_out // 16 * 16 // (latent // LANES) * 2 // heads
+    lines = tokens * (columns // peers) // LANES
     vmem = pl.BlockSpec(memory_space=pltpu.VMEM)
     return pl.pallas_call(
         project_kernel,
-        out_shape=pltpu.VMEM((peers, tokens, columns // peers), jnp.bfloat16),
+        out_shape=pltpu.VMEM((peers, lines, LANES), jnp.bfloat16),
         in_specs=[vmem] * 3,
         out_specs=vmem,
         compiler_params=pltpu.CompilerParams(vmem_limit_bytes=16 * 1024 * 1024),
@@ -257,16 +296,17 @@
 def total_kernel(terms_ref, out_ref):
     rows, new_count, _ = out_ref.shape
     terms = [terms_ref[k].astype(jnp.float32) for k in range(terms_ref.shape[0])]
-    result = functools.reduce(jnp.add, terms).astype(jnp.bfloat16)
+    result = unfold(functools.reduce(jnp.add, terms), rows * new_count).astype(jnp.bfloat16)
     for row in range(rows):
         out_ref[row] = result[row * new_count : (row + 1) * new_count]
 
 
 def total(terms, rows, new_count):
+    peers, lines, _ = terms.shape
     vmem = pl.BlockSpec(memory_space=pltpu.VMEM)
     return pl.pallas_call(
         total_kernel,
-        out_shape=jax.ShapeDtypeStruct((rows, new_count, terms.shape[2]), jnp.bfloat16),
+        out_shape=jax.ShapeDtypeStruct((rows, new_count, lines * LANES // (rows * new_count)), jnp.bfloat16),
         in_specs=[vmem],
         out_specs=vmem,
         compiler_params=pltpu.CompilerParams(vmem_limit_bytes=8 * 1024 * 1024),

time: 79.3 us -> 77.7 us (0.980)
  blocking collectives: 63.2 us -> 60.8 us
  Pallas kernels: 11.6 us -> 12.5 us
    all_to_all x1, blocking collectives: 25.5 us -> 24.2 us  [body(): query = lax.all_to_all(spread(queries, peers), both, 0, 0, tiled=True)]
    pallas_call x2, Pallas kernels: 1.68 us -> 2.49 us  [the longest x1 2.35 us: project(): pl.pallas_call(project_kernel, out_shape=pltpu.VMEM((peers, lines, LANES)...]
where the time goes in v9:
time: 77.7 us; the launch traced here: 77.5 us
  blocking collectives  60.8 us (78%)
  Pallas kernels  12.5 us (16%)
  starting transfers between devices  3.24 us (4%)
  local copies, waits for them, and re-layouts  0.91 us (1%)
    all_to_all x1, blocking collectives, body(): query = lax.all_to_all(spread(queries, peers), both, 0, 0, tiled=True)  24.2 us
    all_to_all x1, blocking collectives, body(): parts = lax.all_to_all(mine, both, 0, 0, tiled=True)  22.1 us
    all_to_all x1, blocking collectives, body(): terms = lax.all_to_all(terms, both, 0, 0, tiled=True)  14.5 us
    pallas_call x1, Pallas kernels, attend(): pl.pallas_call(functools.partial(attend_kernel, new_count=new_count), out...  9.21 us
    ppermute x1, starting transfers between devices, body(): came = lax.ppermute(cache, 'core', swap)  3.24 us
    pallas_call x1, Pallas kernels, project(): pl.pallas_call(project_kernel, out_shape=pltpu.VMEM((peers, lines, LANES)...  2.35 us
  transfers between devices with their start and end apart: 1, of which 0 were waited for; matrix products, arithmetic and copies ran while one was open for 0% of the time, Pallas kernels for 0%

profile of v9, /device:TPU:1, one launch (start us, length us, event | category | flops | bytes accessed | tf_op | source)
XLA Modules:
  0.0 77.5 jit_solution(9909841513599017367)
XLA Ops:
  0.0 3.2 %collective-permute-start = (bf16[8,576,1024]{2,1,0:T(8,128)(2,1)}, bf16[8,576,1024]{2,1,0:T(8,128)(2,1)S(1)}, u32[]{:S(2)}, u32[]{:S(2)}) collective-permute-start(bf16[8,576,1024]{2,1,0:T(8,128)(2,1)} %bitcast.1), channel_id=1, source_target_pairs={{0,1},{1,0},{2,3},{3,2},{4,5},{5,4},{6,7},{7,6},{8,9},{9,8},{10,11... | collective-permute-start | bytes 28311560 | tf_op jit(solution)/shard_map/ppermute | solution.py:323
  3.2 0.0 copy-start.2
  3.2 0.9 %copy-done.2 = bf16[8,4,2,576]{3,2,1,0:T(2,128)(2,1)S(1)} copy-done((bf16[8,4,2,576]{3,2,1,0:T(2,128)(2,1)S(1)}, bf16[8,4,2,576]{3,2,1,0:T(2,128)(2,1)}, u32[]{:S(2)}) %copy-start.2) | copy-done | bytes 73752
  4.1 0.1 spread.1
  4.3 0.0 copy-start.3
  4.3 0.0 copy-start.4
  4.3 24.2 %all_to_all.15.query_ref = bf16[32,144,128]{2,1,0:T(8,128)(2,1)S(1)} all-to-all(bf16[32,144,128]{2,1,0:T(8,128)(2,1)S(1)} %spread.1), channel_id=1, replica_groups=mesh['batch'=8,'chip'=16,'core'=2] {'chip','core'}, dimensions={0} | all-to-all | bytes 2359296 | tf_op jit(solution)/shard_map/all_to_all | solution.py:324
  28.5 0.0 collective-permute-done.came_ref
  28.5 0.0 copy-done.3
  28.5 0.0 copy-done.4
  28.5 0.0 copy-start
  28.5 9.2 %attend.1 = bf16[32,136,128]{2,1,0:T(8,128)(2,1)S(1)} custom-call(s32[8]{0:T(128)S(1)} %copy-done.3, s32[8]{0:T(128)S(1)} %copy-done.4, bf16[8,576,1024]{2,1,0:T(8,128)(2,1)} %bitcast.2, bf16[8,576,1024]{2,1,0:T(8,128)(2,1)S(1)} %collective-permute-done.came_ref, bf16[32,144,128]{2,1,0:T(8,128)(2,1)S(1)} %all_to_all.15.query_ref), custom_call_target="tpu_custom_call" | custom-call | flops 4563402752 | bytes 10551296 | tf_op jit(solution)/shard_map/attend/pallas_call | solution.py:190
  37.7 0.0 copy-start.1
  37.7 22.1 %all_to_all.16.parts_ref = bf16[32,136,128]{2,1,0:T(8,128)(2,1)S(1)} all-to-all(bf16[32,136,128]{2,1,0:T(8,128)(2,1)S(1)} %attend.1), channel_id=1, replica_groups=mesh['batch'=8,'chip'=16,'core'=2] {'chip','core'}, dimensions={0} | all-to-all | bytes 2228224 | tf_op jit(solution)/shard_map/all_to_all | solution.py:327
  59.9 0.0 copy-done
  59.9 0.0 copy-done.1
  59.9 2.3 %project.1 = bf16[32,56,128]{2,1,0:T(8,128)(2,1)S(1)} custom-call(bf16[32,136,128]{2,1,0:T(8,128)(2,1)S(1)} %all_to_all.16.parts_ref, bf16[2,512,128]{2,1,0:T(8,128)(2,1)S(1)} %copy-done.1, bf16[256,7168]{1,0:T(8,128)(2,1)S(1)} %copy-done), custom_call_target="tpu_custom_call" | custom-call | tf_op jit(solution)/shard_map/project/pallas_call | solution.py:286
  62.2 14.5 %all_to_all.17.terms_ref = bf16[32,56,128]{2,1,0:T(8,128)(2,1)S(1)} all-to-all(bf16[32,56,128]{2,1,0:T(8,128)(2,1)S(1)} %project.1), channel_id=1, replica_groups=mesh['batch'=8,'chip'=16,'core'=2] {'chip','core'}, dimensions={0} | all-to-all | bytes 917504 | tf_op jit(solution)/shard_map/all_to_all | solution.py:329
  76.7 0.8 %total.1 = bf16[8,4,224]{2,1,0:T(4,128)(2,1)} custom-call(bf16[32,56,128]{2,1,0:T(8,128)(2,1)S(1)} %all_to_all.17.terms_ref), custom_call_target="tpu_custom_call" | custom-call | tf_op jit(solution)/shard_map/total/pallas_call | solution.py:307
Async XLA Ops:
  0.0 28.5 %collective-permute-start = (bf16[8,576,1024]{2,1,0:T(8,128)(2,1)}, bf16[8,576,1024]{2,1,0:T(8,128)(2,1)S(1)}, u32[]{:S(2)}, u32[]{:S(2)}) collective-permute-start(bf16[8,576,1024]{2,1,0:T(8,128)(2,1)} %bitcast.1), channel_id=1, source_target_pairs={{0,1},{1,0},{2,3},{3,2},{4,5},{5,4},{6,7},{7,6},{8,9},{9,8},{10,11... | collective-permute-start | bytes 28311560 | tf_op jit(solution)/shard_map/ppermute | solution.py:323
  3.2 0.9 %copy-start.2 = (bf16[8,4,2,576]{3,2,1,0:T(2,128)(2,1)S(1)}, bf16[8,4,2,576]{3,2,1,0:T(2,128)(2,1)}, u32[]{:S(2)}) copy-start(bf16[8,4,2,576]{3,2,1,0:T(2,128)(2,1)} %query_ref.1) | copy-start | bytes 221188
  4.3 24.2 %copy-start.3 = (s32[8]{0:T(128)S(1)}, s32[8]{0:T(128)}, u32[]{:S(2)}) copy-start(s32[8]{0:T(128)} %lengths_ref.1) | copy-start | bytes 100
  4.3 24.2 %copy-start.4 = (s32[8]{0:T(128)S(1)}, s32[8]{0:T(128)}, u32[]{:S(2)}) copy-start(s32[8]{0:T(128)} %positions_ref.1) | copy-start | bytes 100
  28.5 31.4 %copy-start = (bf16[256,7168]{1,0:T(8,128)(2,1)S(1)}, bf16[256,7168]{1,0:T(8,128)(2,1)}, u32[]{:S(2)}) copy-start(bf16[256,7168]{1,0:T(8,128)(2,1)} %proj_ref) | copy-start | bytes 11010052
  37.7 22.1 %copy-start.1 = (bf16[2,512,128]{2,1,0:T(8,128)(2,1)S(1)}, bf16[2,512,128]{2,1,0:T(8,128)(2,1)}, u32[]{:S(2)}) copy-start(bf16[2,512,128]{2,1,0:T(8,128)(2,1)} %up_ref) | copy-start | bytes 786436

commit v10 on v9

--- a/solution.py
+++ b/solution.py
@@ -52,37 +52,38 @@
     return tile[..., at : at + 1] + tile[..., at + 1 : at + 2] + tile[..., at + 2 : at + 3]
 
 
-def spread_kernel(query_ref, out_ref, flat_ref):
-    rows, new_count, heads, full = query_ref.shape
+def spread_kernel(own_ref, came_ref, out_ref, flat_ref):
+    rows, new_count, heads, full = own_ref.shape
     latent = full - ROPE
-    for row in range(rows):
-        for token in range(new_count):
-            at = (row * new_count + token) * heads
-            flat_ref[at : at + heads, :] = query_ref[row, token].astype(jnp.float32)
-    flat = flat_ref[...]
-    depth = flat.shape[0] // 2
-    for half in range(2):
-        mine = flat[half * depth : (half + 1) * depth]
+    depth = flat_ref.shape[1] // 2
+    core = lax.axis_index("core")
+    for side, ref in enumerate((own_ref, came_ref)):
+        for row in range(rows):
+            for token in range(new_count):
+                at = (row * new_count + token) * heads
+                flat_ref[side, at : at + heads, :] = ref[row, token].astype(jnp.float32)
+        mine = flat_ref[side, pl.ds(pl.multiple_of(core * depth, depth), depth), :]
         pieces = [mine[:, g : g + LANES] for g in range(0, latent, LANES)]
         pieces.append(jnp.concatenate([mine[: depth // 2, latent:], mine[depth // 2 :, latent:]], axis=-1))
         block = jnp.concatenate(pieces, axis=0).astype(jnp.bfloat16)
-        for peer in range(half, out_ref.shape[0], 2):
-            out_ref[peer] = block
-
-
-def spread(queries, peers):
-    rows, new_count, heads, full = queries.shape
+        member = core if side == 0 else 1 - core
+        for chip in range(out_ref.shape[0] // 2):
+            out_ref[2 * chip + member] = block
+
+
+def spread(own, came, peers):
+    rows, new_count, heads, full = own.shape
     count = rows * new_count * heads
     vmem = pl.BlockSpec(memory_space=pltpu.VMEM)
     return pl.pallas_call(
         spread_kernel,
         out_shape=pltpu.VMEM((peers, count // 2 * full // LANES, LANES), jnp.bfloat16),
-        in_specs=[vmem],
+        in_specs=[vmem] * 2,
         out_specs=vmem,
-        scratch_shapes=[pltpu.VMEM((count, full), jnp.float32)],
+        scratch_shapes=[pltpu.VMEM((2, count, full), jnp.float32)],
         compiler_params=pltpu.CompilerParams(vmem_limit_bytes=8 * 1024 * 1024),
         name="spread",
-    )(queries)
+    )(own, came)
 
 
 def attend_kernel(lengths_ref, positions_ref, own_ref, came_ref, query_ref, out_ref, keys_ref, arrived, *, new_count):
@@ -206,17 +207,29 @@
     )(lengths, positions, own, came, query)
 
 
-def project_kernel(parts_ref, up_ref, proj_ref, out_ref):
+def project_kernel(parts_ref, own_up_ref, came_up_ref, own_proj_ref, came_proj_ref, out_ref, proj_ref, arrived):
     sixteen = 16
     peers, rows_out, _ = parts_ref.shape
-    heads, wide, _ = up_ref.shape
+    heads, wide, _ = own_up_ref.shape
     groups = wide // LANES
     at = rows_out - rows_out % sixteen
     depth = at // groups
-    blocks = []
-    for half in range(2):
-        chosen = range(half, peers, 2)
-        stat_tiles = [parts_ref[k, at:, :].astype(jnp.float32) for k in chosen]
+    width = out_ref.shape[2]
+    step = 4
+    copies = []
+    for piece, first in enumerate(range(0, peers, step)):
+        columns = pl.ds(first * width, step * width)
+        for side, ref in enumerate((own_proj_ref, came_proj_ref)):
+            target = proj_ref.at[side, :, columns]
+            copies.append(pltpu.make_async_copy(ref.at[:, columns], target, arrived.at[piece, side]))
+    for copy in copies:
+        copy.start()
+    core = lax.axis_index("core")
+    flats = []
+    for side, up_ref in enumerate((own_up_ref, came_up_ref)):
+        member = core if side == 0 else 1 - core
+        blocks = []
+        stat_tiles = [parts_ref[2 * k + member, at:, :].astype(jnp.float32) for k in range(peers // 2)]
         for pair in range(2):
             stats = [
                 jnp.concatenate([join_stat(tile, 2 * pair), join_stat(tile, 2 * pair + 1)], axis=0)
@@ -229,84 +242,67 @@
             for g in range(groups):
                 start = g * depth + pair * sixteen
                 terms = [
-                    parts_ref[k, start : start + sixteen, :].astype(jnp.float32) * weight
-                    for k, weight in zip(chosen, weights)
+                    parts_ref[2 * k + member, start : start + sixteen, :].astype(jnp.float32) * weight
+                    for k, weight in enumerate(weights)
                 ]
                 sums.append(functools.reduce(jnp.add, terms) * scale)
             blocks.append(jnp.concatenate(sums, axis=-1))
-    latent = jnp.concatenate(blocks, axis=0).astype(jnp.bfloat16)
-    count = latent.shape[0]
-    out_row = lax.broadcasted_iota(jnp.int32, (count // heads, count), 0)
-    in_row = lax.broadcasted_iota(jnp.int32, (count // heads, count), 1)
-    values = []
-    for head in range(heads):
-        pick = jnp.where(in_row == out_row * heads + head, 1.0, 0.0).astype(jnp.bfloat16)
-        own = jnp.dot(pick, latent, preferred_element_type=jnp.float32).astype(jnp.bfloat16)
-        values.append(jnp.dot(own, up_ref[head], preferred_element_type=jnp.float32).astype(jnp.bfloat16))
-    flat = jnp.concatenate(values, axis=-1)
-    width = proj_ref.shape[1] // peers
-    step = 4
-    for first in range(0, peers, step):
+        latent = jnp.concatenate(blocks, axis=0).astype(jnp.bfloat16)
+        count = latent.shape[0]
+        out_row = lax.broadcasted_iota(jnp.int32, (count // heads, count), 0)
+        in_row = lax.broadcasted_iota(jnp.int32, (count // heads, count), 1)
+        values = []
+        for head in range(heads):
+            pick = jnp.where(in_row == out_row * heads + head, 1.0, 0.0).astype(jnp.bfloat16)
+            chosen = jnp.dot(pick, latent, preferred_element_type=jnp.float32).astype(jnp.bfloat16)
+            values.append(jnp.dot(chosen, up_ref[head], preferred_element_type=jnp.float32).astype(jnp.bfloat16))
+        flats.append(jnp.concatenate(values, axis=-1))
+    for piece, first in enumerate(range(0, peers, step)):
         columns = slice(first * width, (first + step) * width)
-        terms = jnp.dot(flat, proj_ref[:, columns], preferred_element_type=jnp.float32)
+        terms = None
+        for side in range(2):
+            copies[2 * piece + side].wait()
+            term = jnp.dot(flats[side], proj_ref[side, :, columns], preferred_element_type=jnp.float32)
+            terms = term if terms is None else terms + term
         for k in range(step):
-            out_ref[first + k] = fold(terms[:, k * width : (k + 1) * width]).astype(jnp.bfloat16)
-
-
-def fold(block):
-    lines, width = block.shape
-    part = lines // 4
-    thin = LANES // 4
-    pieces = [block[:, :LANES]]
-    for at in range(LANES, width, thin):
-        pieces.append(
-            jnp.concatenate([block[m * part : (m + 1) * part, at : at + thin] for m in range(4)], axis=-1)
-        )
-    return jnp.concatenate(pieces, axis=0)
-
-
-def unfold(block, lines):
-    part = lines // 4
-    thin = LANES // 4
-    pieces = [block[:lines]]
-    for at in range(lines, block.shape[0], part):
-        pieces.append(
-            jnp.concatenate([block[at : at + part, m * thin : (m + 1) * thin] for m in range(4)], axis=0)
-        )
-    return jnp.concatenate(pieces, axis=-1)
-
-
-def project(parts, value_up, out_proj):
+            out_ref[first + k] = terms[:, k * width : (k + 1) * width].astype(jnp.bfloat16)
+
+
+def project(parts, own_up, came_up, own_proj, came_proj):
     peers, rows_out, _ = parts.shape
-    heads, latent, _ = value_up.shape
-    columns = out_proj.shape[1]
-    tokens = rows_out // 16 * 16 // (latent // LANES) * 2 // heads
-    lines = tokens * (columns // peers) // LANES
-    vmem = pl.BlockSpec(memory_space=pltpu.VMEM)
+    heads, latent, _ = own_up.shape
+    depth, columns = own_proj.shape
+    tokens = rows_out // 16 * 16 // (latent // LANES) // heads
+    vmem, anywhere = pl.BlockSpec(memory_space=pltpu.VMEM), pl.BlockSpec(memory_space=pl.ANY)
     return pl.pallas_call(
         project_kernel,
-        out_shape=pltpu.VMEM((peers, lines, LANES), jnp.bfloat16),
-        in_specs=[vmem] * 3,
+        out_shape=pltpu.VMEM((peers, tokens, columns // peers), jnp.bfloat16),
+        in_specs=[vmem] * 3 + [anywhere] * 2,
         out_specs=vmem,
-        compiler_params=pltpu.CompilerParams(vmem_limit_bytes=16 * 1024 * 1024),
+        scratch_shapes=[
+            pltpu.VMEM((2, depth, columns), jnp.bfloat16),
+            pltpu.SemaphoreType.DMA((peers // 4, 2)),
+        ],
+        compiler_params=pltpu.CompilerParams(vmem_limit_bytes=24 * 1024 * 1024),
         name="project",
-    )(parts, value_up, out_proj)
+    )(parts, own_up, came_up, own_proj, came_proj)
 
 
 def total_kernel(terms_ref, out_ref):
     rows, new_count, _ = out_ref.shape
-    terms = [terms_ref[k].astype(jnp.float32) for k in range(terms_ref.shape[0])]
-    result = unfold(functools.reduce(jnp.add, terms), rows * new_count).astype(jnp.bfloat16)
-    for row in range(rows):
-        out_ref[row] = result[row * new_count : (row + 1) * new_count]
+    half = rows // 2
+    for core in range(2):
+        terms = [terms_ref[k].astype(jnp.float32) for k in range(core, terms_ref.shape[0], 2)]
+        result = functools.reduce(jnp.add, terms).astype(jnp.bfloat16)
+        for row in range(half):
+            out_ref[core * half + row] = result[row * new_count : (row + 1) * new_count]
 
 
 def total(terms, rows, new_count):
-    peers, lines, _ = terms.shape
     vmem = pl.BlockSpec(memory_space=pltpu.VMEM)
     return pl.pallas_call(
         total_kernel,
-        out_shape=jax.ShapeDtypeStruct((rows, new_count, lines * LANES // (rows * new_count)), jnp.bfloat16),
+        out_shape=jax.ShapeDtypeStruct((rows, new_count, terms.shape[2]), jnp.bfloat16),
         in_specs=[vmem],
         out_specs=vmem,
         compiler_params=pltpu.CompilerParams(vmem_limit_bytes=8 * 1024 * 1024),
@@ -317,16 +313,20 @@
 def body(latent_cache, queries, lengths, positions, value_up, out_proj):
     row_count, new_count = queries.shape[:2]
     peers = lax.axis_size("chip") * 2
-    both = ("chip", "core")
     swap = [(0, 1), (1, 0)]
+    came_queries = lax.ppermute(queries, "core", swap)
+    came_queries, latent_cache = lax.optimization_barrier((came_queries, latent_cache))
     cache = jnp.swapaxes(latent_cache, 1, 2)
     came = lax.ppermute(cache, "core", swap)
-    query = lax.all_to_all(spread(queries, peers), both, 0, 0, tiled=True)
+    query = lax.all_to_all(spread(queries, came_queries, peers), "chip", 0, 0, tiled=True)
+    query, value_up, out_proj = lax.optimization_barrier((query, value_up, out_proj))
+    came_up = lax.ppermute(value_up, "core", swap)
+    came_proj = lax.ppermute(out_proj, "core", swap)
     mine = attend(lengths, positions, cache, came, query, new_count)
-    mine, value_up, out_proj = lax.optimization_barrier((mine, value_up, out_proj))
-    parts = lax.all_to_all(mine, both, 0, 0, tiled=True)
-    terms = project(parts, value_up, out_proj)
-    terms = lax.all_to_all(terms, both, 0, 0, tiled=True)
+    mine, came_up, came_proj = lax.optimization_barrier((mine, came_up, came_proj))
+    parts = lax.all_to_all(mine, "chip", 0, 0, tiled=True)
+    terms = project(parts, value_up, came_up, out_proj, came_proj)
+    terms = lax.all_to_all(terms, ("chip", "core"), 0, 0, tiled=True)
     return total(terms, row_count, new_count)
 
 

time: 77.7 us -> 79 us (1.017)
  blocking collectives: 60.8 us -> 56.9 us
  Pallas kernels: 12.5 us -> 14.6 us
  starting transfers between devices: 3.24 us -> 5.17 us
  waiting for transfers between devices: 0.01 us -> 1.14 us
    ppermute x0 -> x3, starting transfers between devices: none -> 4.82 us  [the longest x1 3.24 us: body(): came_queries = lax.ppermute(queries, 'core', swap)]
    all_to_all x3, blocking collectives: 60.8 us -> 56.9 us  [the longest x1 22.7 us: body(): lax.all_to_all(spread(queries, came_queries, peers), 'chip', 0, 0, tiled=...]
    ppermute x1, starting transfers between devices: 3.24 us -> 0.35 us  [body(): came = lax.ppermute(cache, 'core', swap)]
    pallas_call x1, Pallas kernels: 2.35 us -> 4.8 us  [project(): pl.pallas_call(project_kernel, out_shape=pltpu.VMEM((peers, tokens, colum...]
    ppermute x0 -> x3, waiting for transfers between devices: none -> 1.14 us  [the longest x1 1.13 us: body(): came_queries = lax.ppermute(queries, 'core', swap)]
  transfers between devices with their start and end apart: 1 -> 4, of which waited for: 0 -> 1; matrix products, arithmetic and copies ran while one was open for 0% -> 0% of each run, Pallas kernels for 0% -> 12%
where the time goes in v10:
time: 79 us; the launch traced here: 78.8 us
  blocking collectives  56.9 us (72%)
  Pallas kernels  14.6 us (18%)
  starting transfers between devices  5.17 us (7%)
  waiting for transfers between devices  1.14 us (1%)
  local copies, waits for them, and re-layouts  0.9 us (1%)
    all_to_all x1, blocking collectives, body(): lax.all_to_all(spread(queries, came_queries, peers), 'chip', 0, 0, tiled=...  22.7 us
    all_to_all x1, blocking collectives, body(): parts = lax.all_to_all(mine, 'chip', 0, 0, tiled=True)  20.2 us
    all_to_all x1, blocking collectives, body(): terms = lax.all_to_all(terms, ('chip', 'core'), 0, 0, tiled=True)  14.1 us
    pallas_call x1, Pallas kernels, attend(): pl.pallas_call(functools.partial(attend_kernel, new_count=new_count), out...  8.93 us
    pallas_call x1, Pallas kernels, project(): pl.pallas_call(project_kernel, out_shape=pltpu.VMEM((peers, tokens, colum...  4.8 us
    ppermute x1, starting transfers between devices, body(): came_queries = lax.ppermute(queries, 'core', swap)  3.24 us
  transfers between devices with their start and end apart: 4, of which 1 were waited for; matrix products, arithmetic and copies ran while one was open for 0% of the time, Pallas kernels for 12%

profile of v10, /device:TPU:1, one launch (start us, length us, event | category | flops | bytes accessed | tf_op | source)
XLA Modules:
  0.0 78.8 jit_solution(5790885916968911907)
XLA Ops:
  0.0 0.0 copy-start
  0.0 3.2 %collective-permute-start = (bf16[8,4,2,576]{3,2,1,0:T(2,128)(2,1)}, bf16[8,4,2,576]{3,2,1,0:T(2,128)(2,1)S(1)}, u32[]{:S(2)}, u32[]{:S(2)}) collective-permute-start(bf16[8,4,2,576]{3,2,1,0:T(2,128)(2,1)} %own_ref.1), channel_id=1, source_target_pairs={{0,1},{1,0},{2,3},{3,2},{4,5},{5,4},{6,7},{7,6},{8,9},{9,8},{10,11... | collective-permute-start | bytes 221192 | tf_op jit(solution)/shard_map/ppermute | solution.py:317
  3.2 1.1 %collective-permute-done.came_ref = bf16[8,4,2,576]{3,2,1,0:T(2,128)(2,1)S(1)} collective-permute-done((bf16[8,4,2,576]{3,2,1,0:T(2,128)(2,1)}, bf16[8,4,2,576]{3,2,1,0:T(2,128)(2,1)S(1)}, u32[]{:S(2)}, u32[]{:S(2)}) %collective-permute-start) | collective-permute-done | bytes 73760 | tf_op jit(solution)/shard_map/ppermute | solution.py:317
  4.4 0.4 collective-permute-start.1
  4.7 0.0 copy-start.2
  4.7 0.9 %copy-done.2 = bf16[8,4,2,576]{3,2,1,0:T(2,128)(2,1)S(1)} copy-done((bf16[8,4,2,576]{3,2,1,0:T(2,128)(2,1)S(1)}, bf16[8,4,2,576]{3,2,1,0:T(2,128)(2,1)}, u32[]{:S(2)}) %copy-start.2) | copy-done | bytes 73752
  5.6 0.0 copy-start.3
  5.6 0.0 copy-start.4
  5.6 0.2 spread.1
  5.8 22.7 %all_to_all.15.query_ref = bf16[32,144,128]{2,1,0:T(8,128)(2,1)S(1)} all-to-all(bf16[32,144,128]{2,1,0:T(8,128)(2,1)S(1)} %spread.1), channel_id=1, replica_groups=mesh['batch'=8,'chip'=16,'core'=2] {'chip'}, dimensions={0} | all-to-all | bytes 2359296 | tf_op jit(solution)/shard_map/all_to_all | solution.py:321
  28.5 0.0 copy-done
  28.5 1.5 %collective-permute-start.3 = (bf16[256,7168]{1,0:T(8,128)(2,1)S(1)}, bf16[256,7168]{1,0:T(8,128)(2,1)S(1)}, u32[]{:S(2)}, u32[]{:S(2)}) collective-permute-start(bf16[256,7168]{1,0:T(8,128)(2,1)S(1)} %copy-done), channel_id=1, source_target_pairs={{0,1},{1,0},{2,3},{3,2},{4,5},{5,4},{6,7},{7,6},{8,9},{9,8},{10,11... | collective-permute-start | bytes 11010056 | tf_op jit(solution)/shard_map/ppermute | solution.py:324
  30.0 0.1 collective-permute-start.2
  30.1 0.0 collective-permute-done.1.came_ref
  30.1 0.0 copy-done.3
  30.1 0.0 copy-done.4
  30.1 8.9 %attend.1 = bf16[32,136,128]{2,1,0:T(8,128)(2,1)S(1)} custom-call(s32[8]{0:T(128)S(1)} %copy-done.3, s32[8]{0:T(128)S(1)} %copy-done.4, bf16[8,576,1024]{2,1,0:T(8,128)(2,1)} %bitcast.2, bf16[8,576,1024]{2,1,0:T(8,128)(2,1)S(1)} %collective-permute-done.1.came_ref, bf16[32,144,128]{2,1,0:T(8,128)(2,1)S(1)} %all_to_all.15.query_ref), custom_call_target="tpu_custom_call" | custom-call | flops 4563402752 | bytes 10551296 | tf_op jit(solution)/shard_map/attend/pallas_call | solution.py:191
  39.0 0.0 collective-permute-done.2.came_up_ref
  39.0 0.0 collective-permute-done.3.came_proj_ref
  39.1 20.2 %all_to_all.16.parts_ref = bf16[32,136,128]{2,1,0:T(8,128)(2,1)S(1)} all-to-all(bf16[32,136,128]{2,1,0:T(8,128)(2,1)S(1)} %attend.1), channel_id=1, replica_groups=mesh['batch'=8,'chip'=16,'core'=2] {'chip'}, dimensions={0} | all-to-all | bytes 2228224 | tf_op jit(solution)/shard_map/all_to_all | solution.py:327
  59.2 0.0 copy-done.1
  59.2 4.8 %project.1 = bf16[32,16,224]{2,1,0:T(8,128)(2,1)S(1)} custom-call(bf16[32,136,128]{2,1,0:T(8,128)(2,1)S(1)} %all_to_all.16.parts_ref, bf16[2,512,128]{2,1,0:T(8,128)(2,1)S(1)} %copy-done.1, bf16[2,512,128]{2,1,0:T(8,128)(2,1)S(1)} %collective-permute-done.2.came_up_ref, bf16[256,7168]{1,0:T(8,128)(2,1)S(1)} %copy-done, ...), custom_call_target="tpu_custom_call" | custom-call | tf_op jit(solution)/shard_map/project/pallas_call | solution.py:277
  64.0 14.1 %all_to_all.17.terms_ref = bf16[32,16,224]{2,1,0:T(8,128)(2,1)S(1)} all-to-all(bf16[32,16,224]{2,1,0:T(8,128)(2,1)S(1)} %project.1), channel_id=1, replica_groups=mesh['batch'=8,'chip'=16,'core'=2] {'chip','core'}, dimensions={0} | all-to-all | bytes 458752 | tf_op jit(solution)/shard_map/all_to_all | solution.py:329
  78.1 0.7 total.1
  (1 shorter events, 0.0 us)
Async XLA Ops:
  0.0 28.5 %copy-start = (bf16[256,7168]{1,0:T(8,128)(2,1)S(1)}, bf16[256,7168]{1,0:T(8,128)(2,1)}, u32[]{:S(2)}) copy-start(bf16[256,7168]{1,0:T(8,128)(2,1)} %own_proj_ref) | copy-start | bytes 11010052
  0.0 4.4 %collective-permute-start = (bf16[8,4,2,576]{3,2,1,0:T(2,128)(2,1)}, bf16[8,4,2,576]{3,2,1,0:T(2,128)(2,1)S(1)}, u32[]{:S(2)}, u32[]{:S(2)}) collective-permute-start(bf16[8,4,2,576]{3,2,1,0:T(2,128)(2,1)} %own_ref.1), channel_id=1, source_target_pairs={{0,1},{1,0},{2,3},{3,2},{4,5},{5,4},{6,7},{7,6},{8,9},{9,8},{10,11... | collective-permute-start | bytes 221192 | tf_op jit(solution)/shard_map/ppermute | solution.py:317
  4.4 25.7 %collective-permute-start.1 = (bf16[8,576,1024]{2,1,0:T(8,128)(2,1)}, bf16[8,576,1024]{2,1,0:T(8,128)(2,1)S(1)}, u32[]{:S(2)}, u32[]{:S(2)}) collective-permute-start(bf16[8,576,1024]{2,1,0:T(8,128)(2,1)} %bitcast.1), channel_id=1, source_target_pairs={{0,1},{1,0},{2,3},{3,2},{4,5},{5,4},{6,7},{7,6},{8,9},{9,8},{10,11... | collective-permute-start | bytes 28311560 | tf_op jit(solution)/shard_map/ppermute | solution.py:320
  4.7 0.9 %copy-start.2 = (bf16[8,4,2,576]{3,2,1,0:T(2,128)(2,1)S(1)}, bf16[8,4,2,576]{3,2,1,0:T(2,128)(2,1)}, u32[]{:S(2)}) copy-start(bf16[8,4,2,576]{3,2,1,0:T(2,128)(2,1)} %own_ref.1) | copy-start | bytes 221188
  5.6 24.5 %copy-start.3 = (s32[8]{0:T(128)S(1)}, s32[8]{0:T(128)}, u32[]{:S(2)}) copy-start(s32[8]{0:T(128)} %lengths_ref.1) | copy-start | bytes 100
  5.6 24.5 %copy-start.4 = (s32[8]{0:T(128)S(1)}, s32[8]{0:T(128)}, u32[]{:S(2)}) copy-start(s32[8]{0:T(128)} %positions_ref.1) | copy-start | bytes 100
  28.5 30.7 %copy-start.1 = (bf16[2,512,128]{2,1,0:T(8,128)(2,1)S(1)}, bf16[2,512,128]{2,1,0:T(8,128)(2,1)}, u32[]{:S(2)}) copy-start(bf16[2,512,128]{2,1,0:T(8,128)(2,1)} %own_up_ref) | copy-start | bytes 786436
  28.5 10.5 %collective-permute-start.3 = (bf16[256,7168]{1,0:T(8,128)(2,1)S(1)}, bf16[256,7168]{1,0:T(8,128)(2,1)S(1)}, u32[]{:S(2)}, u32[]{:S(2)}) collective-permute-start(bf16[256,7168]{1,0:T(8,128)(2,1)S(1)} %copy-done), channel_id=1, source_target_pairs={{0,1},{1,0},{2,3},{3,2},{4,5},{5,4},{6,7},{7,6},{8,9},{9,8},{10,11... | collective-permute-start | bytes 11010056 | tf_op jit(solution)/shard_map/ppermute | solution.py:324
  30.0 9.0 %collective-permute-start.2 = (bf16[2,512,128]{2,1,0:T(8,128)(2,1)}, bf16[2,512,128]{2,1,0:T(8,128)(2,1)S(1)}, u32[]{:S(2)}, u32[]{:S(2)}) collective-permute-start(bf16[2,512,128]{2,1,0:T(8,128)(2,1)} %own_up_ref), channel_id=1, source_target_pairs={{0,1},{1,0},{2,3},{3,2},{4,5},{5,4},{6,7},{7,6},{8,9},{9,8},{10,11... | collective-permute-start | bytes 786440 | tf_op jit(solution)/shard_map/ppermute | solution.py:323

commit v11 on v10

--- a/solution.py
+++ b/solution.py
@@ -52,38 +52,37 @@
     return tile[..., at : at + 1] + tile[..., at + 1 : at + 2] + tile[..., at + 2 : at + 3]
 
 
-def spread_kernel(own_ref, came_ref, out_ref, flat_ref):
-    rows, new_count, heads, full = own_ref.shape
+def spread_kernel(query_ref, out_ref, flat_ref):
+    rows, new_count, heads, full = query_ref.shape
     latent = full - ROPE
-    depth = flat_ref.shape[1] // 2
-    core = lax.axis_index("core")
-    for side, ref in enumerate((own_ref, came_ref)):
-        for row in range(rows):
-            for token in range(new_count):
-                at = (row * new_count + token) * heads
-                flat_ref[side, at : at + heads, :] = ref[row, token].astype(jnp.float32)
-        mine = flat_ref[side, pl.ds(pl.multiple_of(core * depth, depth), depth), :]
+    for row in range(rows):
+        for token in range(new_count):
+            at = (row * new_count + token) * heads
+            flat_ref[at : at + heads, :] = query_ref[row, token].astype(jnp.float32)
+    flat = flat_ref[...]
+    depth = flat.shape[0] // 2
+    for half in range(2):
+        mine = flat[half * depth : (half + 1) * depth]
         pieces = [mine[:, g : g + LANES] for g in range(0, latent, LANES)]
         pieces.append(jnp.concatenate([mine[: depth // 2, latent:], mine[depth // 2 :, latent:]], axis=-1))
         block = jnp.concatenate(pieces, axis=0).astype(jnp.bfloat16)
-        member = core if side == 0 else 1 - core
-        for chip in range(out_ref.shape[0] // 2):
-            out_ref[2 * chip + member] = block
-
-
-def spread(own, came, peers):
-    rows, new_count, heads, full = own.shape
+        for peer in range(half, out_ref.shape[0], 2):
+            out_ref[peer] = block
+
+
+def spread(queries, peers):
+    rows, new_count, heads, full = queries.shape
     count = rows * new_count * heads
     vmem = pl.BlockSpec(memory_space=pltpu.VMEM)
     return pl.pallas_call(
         spread_kernel,
         out_shape=pltpu.VMEM((peers, count // 2 * full // LANES, LANES), jnp.bfloat16),
-        in_specs=[vmem] * 2,
+        in_specs=[vmem],
         out_specs=vmem,
-        scratch_shapes=[pltpu.VMEM((2, count, full), jnp.float32)],
+        scratch_shapes=[pltpu.VMEM((count, full), jnp.float32)],
         compiler_params=pltpu.CompilerParams(vmem_limit_bytes=8 * 1024 * 1024),
         name="spread",
-    )(own, came)
+    )(queries)
 
 
 def attend_kernel(lengths_ref, positions_ref, own_ref, came_ref, query_ref, out_ref, keys_ref, arrived, *, new_count):
@@ -207,7 +206,7 @@
     )(lengths, positions, own, came, query)
 
 
-def project_kernel(parts_ref, own_up_ref, came_up_ref, own_proj_ref, came_proj_ref, out_ref, proj_ref, arrived):
+def project_kernel(parts_ref, own_up_ref, came_up_ref, own_proj_ref, came_proj_ref, out_ref):
     sixteen = 16
     peers, rows_out, _ = parts_ref.shape
     heads, wide, _ = own_up_ref.shape
@@ -216,14 +215,6 @@
     depth = at // groups
     width = out_ref.shape[2]
     step = 4
-    copies = []
-    for piece, first in enumerate(range(0, peers, step)):
-        columns = pl.ds(first * width, step * width)
-        for side, ref in enumerate((own_proj_ref, came_proj_ref)):
-            target = proj_ref.at[side, :, columns]
-            copies.append(pltpu.make_async_copy(ref.at[:, columns], target, arrived.at[piece, side]))
-    for copy in copies:
-        copy.start()
     core = lax.axis_index("core")
     flats = []
     for side, up_ref in enumerate((own_up_ref, came_up_ref)):
@@ -257,13 +248,10 @@
             chosen = jnp.dot(pick, latent, preferred_element_type=jnp.float32).astype(jnp.bfloat16)
             values.append(jnp.dot(chosen, up_ref[head], preferred_element_type=jnp.float32).astype(jnp.bfloat16))
         flats.append(jnp.concatenate(values, axis=-1))
-    for piece, first in enumerate(range(0, peers, step)):
+    for first in range(0, peers, step):
         columns = slice(first * width, (first + step) * width)
-        terms = None
-        for side in range(2):
-            copies[2 * piece + side].wait()
-            term = jnp.dot(flats[side], proj_ref[side, :, columns], preferred_element_type=jnp.float32)
-            terms = term if terms is None else terms + term
+        terms = jnp.dot(flats[0], own_proj_ref[:, columns], preferred_element_type=jnp.float32)
+        terms += jnp.dot(flats[1], came_proj_ref[:, columns], preferred_element_type=jnp.float32)
         for k in range(step):
             out_ref[first + k] = terms[:, k * width : (k + 1) * width].astype(jnp.bfloat16)
 
@@ -271,19 +259,15 @@
 def project(parts, own_up, came_up, own_proj, came_proj):
     peers, rows_out, _ = parts.shape
     heads, latent, _ = own_up.shape
-    depth, columns = own_proj.shape
+    columns = own_proj.shape[1]
     tokens = rows_out // 16 * 16 // (latent // LANES) // heads
-    vmem, anywhere = pl.BlockSpec(memory_space=pltpu.VMEM), pl.BlockSpec(memory_space=pl.ANY)
+    vmem = pl.BlockSpec(memory_space=pltpu.VMEM)
     return pl.pallas_call(
         project_kernel,
         out_shape=pltpu.VMEM((peers, tokens, columns // peers), jnp.bfloat16),
-        in_specs=[vmem] * 3 + [anywhere] * 2,
+        in_specs=[vmem] * 5,
         out_specs=vmem,
-        scratch_shapes=[
-            pltpu.VMEM((2, depth, columns), jnp.bfloat16),
-            pltpu.SemaphoreType.DMA((peers // 4, 2)),
-        ],
-        compiler_params=pltpu.CompilerParams(vmem_limit_bytes=24 * 1024 * 1024),
+        compiler_params=pltpu.CompilerParams(vmem_limit_bytes=16 * 1024 * 1024),
         name="project",
     )(parts, own_up, came_up, own_proj, came_proj)
 
@@ -314,11 +298,9 @@
     row_count, new_count = queries.shape[:2]
     peers = lax.axis_size("chip") * 2
     swap = [(0, 1), (1, 0)]
-    came_queries = lax.ppermute(queries, "core", swap)
-    came_queries, latent_cache = lax.optimization_barrier((came_queries, latent_cache))
     cache = jnp.swapaxes(latent_cache, 1, 2)
     came = lax.ppermute(cache, "core", swap)
-    query = lax.all_to_all(spread(queries, came_queries, peers), "chip", 0, 0, tiled=True)
+    query = lax.all_to_all(spread(queries, peers), ("chip", "core"), 0, 0, tiled=True)
     query, value_up, out_proj = lax.optimization_barrier((query, value_up, out_proj))
     came_up = lax.ppermute(value_up, "core", swap)
     came_proj = lax.ppermute(out_proj, "core", swap)

time: 79 us -> 76.5 us (0.968)
  Pallas kernels: 14.6 us -> 12.1 us
  starting transfers between devices: 5.17 us -> 3.75 us
  local copies, waits for them, and re-layouts: 0.9 us -> 2.2 us
  blocking collectives: 56.9 us -> 58.1 us
  waiting for transfers between devices: 1.14 us -> 0.01 us
    ppermute x1 -> x0, starting transfers between devices: 3.24 us -> none  [body(): came_queries = lax.ppermute(queries, 'core', swap)]
    ppermute x1, starting transfers between devices: 0.35 us -> 3.24 us  [body(): came = lax.ppermute(cache, 'core', swap)]
    pallas_call x1, Pallas kernels: 4.8 us -> 2.1 us  [project(): pl.pallas_call(project_kernel, out_shape=pltpu.VMEM((peers, tokens, colum...]
    all_to_all x1, blocking collectives: 22.7 us -> 24.2 us  [body(): lax.all_to_all(spread(queries, peers), ('chip', 'core'), 0, 0, tiled=True)]
    unnamed x10, local copies, waits for them, and re-layouts: 0.9 us -> 2.2 us
    ppermute x1 -> x0, waiting for transfers between devices: 1.13 us -> none  [body(): came_queries = lax.ppermute(queries, 'core', swap)]
    ppermute x1, starting transfers between devices: 1.48 us -> 0.39 us  [body(): came_proj = lax.ppermute(out_proj, 'core', swap)]
  transfers between devices with their start and end apart: 4 -> 3, of which waited for: 1 -> 0; matrix products, arithmetic and copies ran while one was open for 0% -> 0% of each run, Pallas kernels for 12% -> 12%
where the time goes in v11:
time: 76.5 us; the launch traced here: 76.2 us
  blocking collectives  58.1 us (76%)
  Pallas kernels  12.1 us (16%)
  starting transfers between devices  3.75 us (5%)
  local copies, waits for them, and re-layouts  2.2 us (3%)
    all_to_all x1, blocking collectives, body(): lax.all_to_all(spread(queries, peers), ('chip', 'core'), 0, 0, tiled=True)  24.2 us
    all_to_all x1, blocking collectives, body(): parts = lax.all_to_all(mine, 'chip', 0, 0, tiled=True)  19.7 us
    all_to_all x1, blocking collectives, body(): terms = lax.all_to_all(terms, ('chip', 'core'), 0, 0, tiled=True)  14.2 us
    pallas_call x1, Pallas kernels, attend(): pl.pallas_call(functools.partial(attend_kernel, new_count=new_count), out...  9.21 us
    ppermute x1, starting transfers between devices, body(): came = lax.ppermute(cache, 'core', swap)  3.24 us
    unnamed x10, local copies, waits for them, and re-layouts  2.2 us
    pallas_call x1, Pallas kernels, project(): pl.pallas_call(project_kernel, out_shape=pltpu.VMEM((peers, tokens, colum...  2.1 us
  transfers between devices with their start and end apart: 3, of which 0 were waited for; matrix products, arithmetic and copies ran while one was open for 0% of the time, Pallas kernels for 12%

profile of v11, /device:TPU:1, one launch (start us, length us, event | category | flops | bytes accessed | tf_op | source)
XLA Modules:
  0.0 76.2 jit_solution(13403328846427738360)
XLA Ops:
  0.0 3.2 %collective-permute-start = (bf16[8,576,1024]{2,1,0:T(8,128)(2,1)}, bf16[8,576,1024]{2,1,0:T(8,128)(2,1)S(1)}, u32[]{:S(2)}, u32[]{:S(2)}) collective-permute-start(bf16[8,576,1024]{2,1,0:T(8,128)(2,1)} %bitcast.1), channel_id=1, source_target_pairs={{0,1},{1,0},{2,3},{3,2},{4,5},{5,4},{6,7},{7,6},{8,9},{9,8},{10,11... | collective-permute-start | bytes 28311560 | tf_op jit(solution)/shard_map/ppermute | solution.py:302
  3.2 0.0 copy-start.2
  3.2 0.9 %copy-done.2 = bf16[8,4,2,576]{3,2,1,0:T(2,128)(2,1)S(1)} copy-done((bf16[8,4,2,576]{3,2,1,0:T(2,128)(2,1)S(1)}, bf16[8,4,2,576]{3,2,1,0:T(2,128)(2,1)}, u32[]{:S(2)}) %copy-start.2) | copy-done | bytes 73752
  4.1 0.1 spread.1
  4.3 24.2 %all_to_all.15.query_ref = bf16[32,144,128]{2,1,0:T(8,128)(2,1)S(1)} all-to-all(bf16[32,144,128]{2,1,0:T(8,128)(2,1)S(1)} %spread.1), channel_id=1, replica_groups=mesh['batch'=8,'chip'=16,'core'=2] {'chip','core'}, dimensions={0} | all-to-all | bytes 2359296 | tf_op jit(solution)/shard_map/all_to_all | solution.py:303
  28.5 0.0 copy-start.1
  28.5 0.4 collective-permute-start.2
  28.9 0.1 collective-permute-start.1
  29.0 0.0 collective-permute-done.came_ref
  29.0 0.0 copy-start.3
  29.0 0.7 copy-done.3
  29.6 0.0 copy-start.4
  29.6 0.7 copy-done.4
  30.3 0.0 copy-start
  30.3 9.2 %attend.1 = bf16[32,136,128]{2,1,0:T(8,128)(2,1)S(1)} custom-call(s32[8]{0:T(128)S(1)} %copy-done.3, s32[8]{0:T(128)S(1)} %copy-done.4, bf16[8,576,1024]{2,1,0:T(8,128)(2,1)} %bitcast.2, bf16[8,576,1024]{2,1,0:T(8,128)(2,1)S(1)} %collective-permute-done.came_ref, bf16[32,144,128]{2,1,0:T(8,128)(2,1)S(1)} %all_to_all.15.query_ref), custom_call_target="tpu_custom_call" | custom-call | flops 4563402752 | bytes 10551296 | tf_op jit(solution)/shard_map/attend/pallas_call | solution.py:190
  39.5 0.0 collective-permute-done.1.came_up_ref
  39.5 0.0 collective-permute-done.2.came_proj_ref
  39.5 19.7 %all_to_all.16.parts_ref = bf16[32,136,128]{2,1,0:T(8,128)(2,1)S(1)} all-to-all(bf16[32,136,128]{2,1,0:T(8,128)(2,1)S(1)} %attend.1), channel_id=1, replica_groups=mesh['batch'=8,'chip'=16,'core'=2] {'chip'}, dimensions={0} | all-to-all | bytes 2228224 | tf_op jit(solution)/shard_map/all_to_all | solution.py:309
  59.3 0.0 copy-done.1
  59.3 0.0 copy-done
  59.3 2.1 %project.1 = bf16[32,16,224]{2,1,0:T(8,128)(2,1)S(1)} custom-call(bf16[32,136,128]{2,1,0:T(8,128)(2,1)S(1)} %all_to_all.16.parts_ref, bf16[2,512,128]{2,1,0:T(8,128)(2,1)S(1)} %copy-done.1, bf16[2,512,128]{2,1,0:T(8,128)(2,1)S(1)} %collective-permute-done.1.came_up_ref, bf16[256,7168]{1,0:T(8,128)(2,1)S(1)} %copy-done, ...), custom_call_target="tpu_custom_call" | custom-call | tf_op jit(solution)/shard_map/project/pallas_call | solution.py:265
  61.4 14.2 %all_to_all.17.terms_ref = bf16[32,16,224]{2,1,0:T(8,128)(2,1)S(1)} all-to-all(bf16[32,16,224]{2,1,0:T(8,128)(2,1)S(1)} %project.1), channel_id=1, replica_groups=mesh['batch'=8,'chip'=16,'core'=2] {'chip','core'}, dimensions={0} | all-to-all | bytes 458752 | tf_op jit(solution)/shard_map/all_to_all | solution.py:311
  75.6 0.7 total.1
Async XLA Ops:
  0.0 29.0 %collective-permute-start = (bf16[8,576,1024]{2,1,0:T(8,128)(2,1)}, bf16[8,576,1024]{2,1,0:T(8,128)(2,1)S(1)}, u32[]{:S(2)}, u32[]{:S(2)}) collective-permute-start(bf16[8,576,1024]{2,1,0:T(8,128)(2,1)} %bitcast.1), channel_id=1, source_target_pairs={{0,1},{1,0},{2,3},{3,2},{4,5},{5,4},{6,7},{7,6},{8,9},{9,8},{10,11... | collective-permute-start | bytes 28311560 | tf_op jit(solution)/shard_map/ppermute | solution.py:302
  3.2 0.9 %copy-start.2 = (bf16[8,4,2,576]{3,2,1,0:T(2,128)(2,1)S(1)}, bf16[8,4,2,576]{3,2,1,0:T(2,128)(2,1)}, u32[]{:S(2)}) copy-start(bf16[8,4,2,576]{3,2,1,0:T(2,128)(2,1)} %query_ref.1) | copy-start | bytes 221188
  28.5 30.8 %copy-start.1 = (bf16[2,512,128]{2,1,0:T(8,128)(2,1)S(1)}, bf16[2,512,128]{2,1,0:T(8,128)(2,1)}, u32[]{:S(2)}) copy-start(bf16[2,512,128]{2,1,0:T(8,128)(2,1)} %own_up_ref) | copy-start | bytes 786436
  28.5 11.1 %collective-permute-start.2 = (bf16[256,7168]{1,0:T(8,128)(2,1)}, bf16[256,7168]{1,0:T(8,128)(2,1)S(1)}, u32[]{:S(2)}, u32[]{:S(2)}) collective-permute-start(bf16[256,7168]{1,0:T(8,128)(2,1)} %own_proj_ref), channel_id=1, source_target_pairs={{0,1},{1,0},{2,3},{3,2},{4,5},{5,4},{6,7},{7,6},{8,9},{9,8},{10,11... | collective-permute-start | bytes 11010056 | tf_op jit(solution)/shard_map/ppermute | solution.py:306
  28.9 10.7 %collective-permute-start.1 = (bf16[2,512,128]{2,1,0:T(8,128)(2,1)}, bf16[2,512,128]{2,1,0:T(8,128)(2,1)S(1)}, u32[]{:S(2)}, u32[]{:S(2)}) collective-permute-start(bf16[2,512,128]{2,1,0:T(8,128)(2,1)} %own_up_ref), channel_id=1, source_target_pairs={{0,1},{1,0},{2,3},{3,2},{4,5},{5,4},{6,7},{7,6},{8,9},{9,8},{10,11... | collective-permute-start | bytes 786440 | tf_op jit(solution)/shard_map/ppermute | solution.py:305
  29.0 0.7 copy-start.3
  29.6 0.7 copy-start.4
  30.3 29.0 %copy-start = (bf16[256,7168]{1,0:T(8,128)(2,1)S(1)}, bf16[256,7168]{1,0:T(8,128)(2,1)}, u32[]{:S(2)}) copy-start(bf16[256,7168]{1,0:T(8,128)(2,1)} %own_proj_ref) | copy-start | bytes 11010052

commit v12 on v11

--- a/solution.py
+++ b/solution.py
@@ -85,7 +85,9 @@
     )(queries)
 
 
-def attend_kernel(lengths_ref, positions_ref, own_ref, came_ref, query_ref, out_ref, keys_ref, arrived, *, new_count):
+def attend_kernel(
+    far_lengths_ref, far_positions_ref, own_ref, came_ref, query_ref, out_ref, keys_ref, lengths_ref, positions_ref, arrived, told, *, new_count
+):
     peers = query_ref.shape[0]
     full = own_ref.shape[1]
     rows, wide, context = keys_ref.shape
@@ -99,6 +101,12 @@
     core = lax.axis_index("core")
     base = core * rows
     starts = [(lax.axis_index("chip") * 2 + place) * span for place in (core, 1 - core)]
+    scalars = [
+        pltpu.make_async_copy(far_lengths_ref, lengths_ref, told.at[0]),
+        pltpu.make_async_copy(far_positions_ref, positions_ref, told.at[1]),
+    ]
+    for copy in scalars:
+        copy.start()
     copies = []
     for row in range(rows):
         for side, ref in enumerate((own_ref, came_ref)):
@@ -112,6 +120,16 @@
     flags = jnp.where(column == member // heads, 1.0, 0.0)
     place = lax.broadcasted_iota(jnp.int32, (spare, span), 1)
     token = lax.broadcasted_iota(jnp.int32, (spare, span), 0)
+    latents, ropes = [], []
+    for row in range(rows):
+        tile, upper = row // 2 * 2 * group, slice(row % 2 * group, (row % 2 + 1) * group)
+        for g in range(column_groups):
+            piece = query_ref[:, g * depth + tile : g * depth + tile + 2 * group, :].astype(jnp.float32)
+            latents.append(piece[:, upper])
+        rope = query_ref[:, column_groups * depth :, :].astype(jnp.float32)
+        ropes.append(rope[:, upper, row // 2 * ROPE : (row // 2 + 1) * ROPE])
+    for copy in scalars:
+        copy.wait()
     turns = angles([positions_ref[base + row] for row in range(rows)], new_count, heads)
     queries = []
     for row in range(rows):
@@ -119,15 +137,10 @@
             limit = lengths_ref[base + row] - new_count + 1 - starts[side]
             hidden = (token < new_count) & (place >= limit + token)
             keys_ref[row, full:, side * span : (side + 1) * span] = jnp.where(hidden, HIDDEN, 0.0).astype(jnp.bfloat16)
-        tile, upper = row // 2 * 2 * group, slice(row % 2 * group, (row % 2 + 1) * group)
-        pieces = []
-        for g in range(column_groups):
-            piece = query_ref[:, g * depth + tile : g * depth + tile + 2 * group, :].astype(jnp.float32)
-            pieces.append(piece[:, upper])
-        rope = query_ref[:, column_groups * depth :, :].astype(jnp.float32)
-        rope = rope[:, upper, row // 2 * ROPE : (row // 2 + 1) * ROPE]
+        rope = ropes[row]
         swapped = jnp.concatenate([rope[:, :, ROPE // 2 :], rope[:, :, : ROPE // 2]], axis=-1)
         turned = rope * turns[row][0][None] + swapped * turns[row][1][None]
+        pieces = latents[row * column_groups : (row + 1) * column_groups]
         query = jnp.concatenate([*pieces, turned, flags], axis=-1)
         queries.append(query.reshape(count, wide).astype(jnp.bfloat16))
 
@@ -185,16 +198,21 @@
     group = depth // rows
     rows_out = latent // LANES * depth + group
     count = peers * group
-    smem, vmem, anywhere = (pl.BlockSpec(memory_space=s) for s in (pltpu.SMEM, pltpu.VMEM, pl.ANY))
-    own = pltpu.with_memory_space_constraint(own, pltpu.HBM)
+    vmem, anywhere = (pl.BlockSpec(memory_space=space) for space in (pltpu.VMEM, pl.ANY))
+    own, lengths, positions = (
+        pltpu.with_memory_space_constraint(array, pltpu.HBM) for array in (own, lengths, positions)
+    )
     return pl.pallas_call(
         functools.partial(attend_kernel, new_count=new_count),
         out_shape=pltpu.VMEM((peers, rows_out, LANES), jnp.bfloat16),
-        in_specs=[smem, smem, anywhere, anywhere, vmem],
+        in_specs=[anywhere] * 4 + [vmem],
         out_specs=vmem,
         scratch_shapes=[
             pltpu.VMEM((rows, -(-full // LANES) * LANES, 2 * context), jnp.bfloat16),
+            pltpu.SMEM(lengths.shape, jnp.int32),
+            pltpu.SMEM(positions.shape, jnp.int32),
             pltpu.SemaphoreType.DMA((2 * rows,)),
+            pltpu.SemaphoreType.DMA((2,)),
         ],
         compiler_params=pltpu.CompilerParams(vmem_limit_bytes=VMEM_LIMIT),
         cost_estimate=pl.CostEstimate(

time: 76.5 us -> 74.6 us (0.975)
  local copies, waits for them, and re-layouts: 2.2 us -> 0.89 us
    unnamed x10 -> x6, local copies, waits for them, and re-layouts: 2.2 us -> 0.89 us
where the time goes in v12:
time: 74.6 us; the launch traced here: 74.4 us
  blocking collectives  58.1 us (78%)
  Pallas kernels  11.5 us (15%)
  starting transfers between devices  3.75 us (5%)
  local copies, waits for them, and re-layouts  0.89 us (1%)
    all_to_all x1, blocking collectives, body(): lax.all_to_all(spread(queries, peers), ('chip', 'core'), 0, 0, tiled=True)  24.2 us
    all_to_all x1, blocking collectives, body(): parts = lax.all_to_all(mine, 'chip', 0, 0, tiled=True)  19.8 us
    all_to_all x1, blocking collectives, body(): terms = lax.all_to_all(terms, ('chip', 'core'), 0, 0, tiled=True)  14.2 us
    pallas_call x1, Pallas kernels, attend(): pl.pallas_call(functools.partial(attend_kernel, new_count=new_count), out...  8.66 us
    ppermute x1, starting transfers between devices, body(): came = lax.ppermute(cache, 'core', swap)  3.24 us
    pallas_call x1, Pallas kernels, project(): pl.pallas_call(project_kernel, out_shape=pltpu.VMEM((peers, tokens, colum...  2.09 us
  transfers between devices with their start and end apart: 3, of which 0 were waited for; matrix products, arithmetic and copies ran while one was open for 0% of the time, Pallas kernels for 12%

profile of v12, /device:TPU:1, one launch (start us, length us, event | category | flops | bytes accessed | tf_op | source)
XLA Modules:
  0.0 74.4 jit_solution(17980196962826399255)
XLA Ops:
  0.0 3.2 %collective-permute-start = (bf16[8,576,1024]{2,1,0:T(8,128)(2,1)}, bf16[8,576,1024]{2,1,0:T(8,128)(2,1)S(1)}, u32[]{:S(2)}, u32[]{:S(2)}) collective-permute-start(bf16[8,576,1024]{2,1,0:T(8,128)(2,1)} %bitcast.1), channel_id=1, source_target_pairs={{0,1},{1,0},{2,3},{3,2},{4,5},{5,4},{6,7},{7,6},{8,9},{9,8},{10,11... | collective-permute-start | bytes 28311560 | tf_op jit(solution)/shard_map/ppermute | solution.py:320
  3.2 0.0 copy-start.2
  3.2 0.9 %copy-done.2 = bf16[8,4,2,576]{3,2,1,0:T(2,128)(2,1)S(1)} copy-done((bf16[8,4,2,576]{3,2,1,0:T(2,128)(2,1)S(1)}, bf16[8,4,2,576]{3,2,1,0:T(2,128)(2,1)}, u32[]{:S(2)}) %copy-start.2) | copy-done | bytes 73752
  4.1 0.1 spread.1
  4.3 24.2 %all_to_all.15.query_ref = bf16[32,144,128]{2,1,0:T(8,128)(2,1)S(1)} all-to-all(bf16[32,144,128]{2,1,0:T(8,128)(2,1)S(1)} %spread.1), channel_id=1, replica_groups=mesh['batch'=8,'chip'=16,'core'=2] {'chip','core'}, dimensions={0} | all-to-all | bytes 2359296 | tf_op jit(solution)/shard_map/all_to_all | solution.py:321
  28.5 0.0 copy-start.1
  28.5 0.4 collective-permute-start.2
  28.9 0.1 collective-permute-start.1
  29.0 0.0 collective-permute-done.came_ref
  29.0 0.0 copy-start
  29.0 8.7 %attend.1 = bf16[32,136,128]{2,1,0:T(8,128)(2,1)S(1)} custom-call(s32[8]{0:T(128)} %far_lengths_ref.1, s32[8]{0:T(128)} %far_positions_ref.1, bf16[8,576,1024]{2,1,0:T(8,128)(2,1)} %bitcast.2, bf16[8,576,1024]{2,1,0:T(8,128)(2,1)S(1)} %collective-permute-done.came_ref, bf16[32,144,128]{2,1,0:T(8,128)(2,1)S(1)} %all_to_all.15.query_ref), custom_call_target="tpu_custom_call" | custom-call | flops 4563402752 | bytes 10551296 | tf_op jit(solution)/shard_map/attend/pallas_call | solution.py:205
  37.7 0.0 collective-permute-done.1.came_up_ref
  37.7 0.0 collective-permute-done.2.came_proj_ref
  37.7 19.8 %all_to_all.16.parts_ref = bf16[32,136,128]{2,1,0:T(8,128)(2,1)S(1)} all-to-all(bf16[32,136,128]{2,1,0:T(8,128)(2,1)S(1)} %attend.1), channel_id=1, replica_groups=mesh['batch'=8,'chip'=16,'core'=2] {'chip'}, dimensions={0} | all-to-all | bytes 2228224 | tf_op jit(solution)/shard_map/all_to_all | solution.py:327
  57.5 0.0 copy-done.1
  57.5 0.0 copy-done
  57.5 2.1 %project.1 = bf16[32,16,224]{2,1,0:T(8,128)(2,1)S(1)} custom-call(bf16[32,136,128]{2,1,0:T(8,128)(2,1)S(1)} %all_to_all.16.parts_ref, bf16[2,512,128]{2,1,0:T(8,128)(2,1)S(1)} %copy-done.1, bf16[2,512,128]{2,1,0:T(8,128)(2,1)S(1)} %collective-permute-done.1.came_up_ref, bf16[256,7168]{1,0:T(8,128)(2,1)S(1)} %copy-done, ...), custom_call_target="tpu_custom_call" | custom-call | tf_op jit(solution)/shard_map/project/pallas_call | solution.py:283
  59.6 14.2 %all_to_all.17.terms_ref = bf16[32,16,224]{2,1,0:T(8,128)(2,1)S(1)} all-to-all(bf16[32,16,224]{2,1,0:T(8,128)(2,1)S(1)} %project.1), channel_id=1, replica_groups=mesh['batch'=8,'chip'=16,'core'=2] {'chip','core'}, dimensions={0} | all-to-all | bytes 458752 | tf_op jit(solution)/shard_map/all_to_all | solution.py:329
  73.7 0.7 total.1
Async XLA Ops:
  0.0 29.0 %collective-permute-start = (bf16[8,576,1024]{2,1,0:T(8,128)(2,1)}, bf16[8,576,1024]{2,1,0:T(8,128)(2,1)S(1)}, u32[]{:S(2)}, u32[]{:S(2)}) collective-permute-start(bf16[8,576,1024]{2,1,0:T(8,128)(2,1)} %bitcast.1), channel_id=1, source_target_pairs={{0,1},{1,0},{2,3},{3,2},{4,5},{5,4},{6,7},{7,6},{8,9},{9,8},{10,11... | collective-permute-start | bytes 28311560 | tf_op jit(solution)/shard_map/ppermute | solution.py:320
  3.2 0.9 %copy-start.2 = (bf16[8,4,2,576]{3,2,1,0:T(2,128)(2,1)S(1)}, bf16[8,4,2,576]{3,2,1,0:T(2,128)(2,1)}, u32[]{:S(2)}) copy-start(bf16[8,4,2,576]{3,2,1,0:T(2,128)(2,1)} %query_ref.1) | copy-start | bytes 221188
  28.5 29.0 %copy-start.1 = (bf16[2,512,128]{2,1,0:T(8,128)(2,1)S(1)}, bf16[2,512,128]{2,1,0:T(8,128)(2,1)}, u32[]{:S(2)}) copy-start(bf16[2,512,128]{2,1,0:T(8,128)(2,1)} %own_up_ref) | copy-start | bytes 786436
  28.5 9.2 %collective-permute-start.2 = (bf16[256,7168]{1,0:T(8,128)(2,1)}, bf16[256,7168]{1,0:T(8,128)(2,1)S(1)}, u32[]{:S(2)}, u32[]{:S(2)}) collective-permute-start(bf16[256,7168]{1,0:T(8,128)(2,1)} %own_proj_ref), channel_id=1, source_target_pairs={{0,1},{1,0},{2,3},{3,2},{4,5},{5,4},{6,7},{7,6},{8,9},{9,8},{10,11... | collective-permute-start | bytes 11010056 | tf_op jit(solution)/shard_map/ppermute | solution.py:324
  28.9 8.8 %collective-permute-start.1 = (bf16[2,512,128]{2,1,0:T(8,128)(2,1)}, bf16[2,512,128]{2,1,0:T(8,128)(2,1)S(1)}, u32[]{:S(2)}, u32[]{:S(2)}) collective-permute-start(bf16[2,512,128]{2,1,0:T(8,128)(2,1)} %own_up_ref), channel_id=1, source_target_pairs={{0,1},{1,0},{2,3},{3,2},{4,5},{5,4},{6,7},{7,6},{8,9},{9,8},{10,11... | collective-permute-start | bytes 786440 | tf_op jit(solution)/shard_map/ppermute | solution.py:323
  29.0 28.5 %copy-start = (bf16[256,7168]{1,0:T(8,128)(2,1)S(1)}, bf16[256,7168]{1,0:T(8,128)(2,1)}, u32[]{:S(2)}) copy-start(bf16[256,7168]{1,0:T(8,128)(2,1)} %own_proj_ref) | copy-start | bytes 11010052

commit v13 on v12

--- a/solution.py
+++ b/solution.py
@@ -182,11 +182,12 @@
         stat = split_stat(stat, lane)
         packed = stat if packed is None else jnp.where(lane < row * STAT_LANES, packed, stat)
         if row % 2 == 1:
-            both = jnp.concatenate(closed[-2:], axis=1).astype(jnp.bfloat16)
-            for g in range(column_groups):
-                start = g * depth + row // 2 * sixteen
-                out_ref[:, start : start + sixteen, :] = both[:, :, g * LANES : (g + 1) * LANES]
-    out_ref[:, at:, :] = packed.astype(jnp.bfloat16)
+            both = jnp.concatenate(closed[-2:], axis=1).reshape(peers // 2, 2, sixteen, latent).astype(jnp.bfloat16)
+            for member in range(2):
+                for g in range(column_groups):
+                    start = member * at + g * depth + row // 2 * sixteen
+                    out_ref[:, start : start + sixteen, :] = both[:, member, :, g * LANES : (g + 1) * LANES]
+    out_ref[:, 2 * at :, :] = packed.reshape(peers // 2, 2 * group, LANES).astype(jnp.bfloat16)
 
 
 def attend(lengths, positions, own, came, query, new_count):
@@ -196,7 +197,7 @@
     latent = full - ROPE
     depth = query.shape[1] * LANES // full
     group = depth // rows
-    rows_out = latent // LANES * depth + group
+    rows_out = 2 * (latent // LANES * depth + group)
     count = peers * group
     vmem, anywhere = (pl.BlockSpec(memory_space=space) for space in (pltpu.VMEM, pl.ANY))
     own, lengths, positions = (
@@ -204,7 +205,7 @@
     )
     return pl.pallas_call(
         functools.partial(attend_kernel, new_count=new_count),
-        out_shape=pltpu.VMEM((peers, rows_out, LANES), jnp.bfloat16),
+        out_shape=pltpu.VMEM((peers // 2, rows_out, LANES), jnp.bfloat16),
         in_specs=[anywhere] * 4 + [vmem],
         out_specs=vmem,
         scratch_shapes=[
@@ -217,7 +218,7 @@
         compiler_params=pltpu.CompilerParams(vmem_limit_bytes=VMEM_LIMIT),
         cost_estimate=pl.CostEstimate(
             flops=4 * count * context * (full + latent) * rows,
-            bytes_accessed=2 * rows * context * full * 2 + 2 * peers * rows_out * LANES,
+            bytes_accessed=2 * rows * context * full * 2 + peers * rows_out * LANES,
             transcendentals=2 * rows * count * context,
         ),
         name="attend",
@@ -226,11 +227,12 @@
 
 def project_kernel(parts_ref, own_up_ref, came_up_ref, own_proj_ref, came_proj_ref, out_ref):
     sixteen = 16
-    peers, rows_out, _ = parts_ref.shape
+    chips, rows_out, _ = parts_ref.shape
+    peers = out_ref.shape[0]
     heads, wide, _ = own_up_ref.shape
     groups = wide // LANES
-    at = rows_out - rows_out % sixteen
-    depth = at // groups
+    at = rows_out - sixteen
+    depth = at // 2 // groups
     width = out_ref.shape[2]
     step = 4
     core = lax.axis_index("core")
@@ -238,7 +240,8 @@
     for side, up_ref in enumerate((own_up_ref, came_up_ref)):
         member = core if side == 0 else 1 - core
         blocks = []
-        stat_tiles = [parts_ref[2 * k + member, at:, :].astype(jnp.float32) for k in range(peers // 2)]
+        stat_tiles = [parts_ref[k, at:, :].astype(jnp.float32) for k in range(chips)]
+        stat_tiles = [jnp.where(member == 0, tile[: sixteen // 2], tile[sixteen // 2 :]) for tile in stat_tiles]
         for pair in range(2):
             stats = [
                 jnp.concatenate([join_stat(tile, 2 * pair), join_stat(tile, 2 * pair + 1)], axis=0)
@@ -249,9 +252,9 @@
             scale = 1.0 / functools.reduce(jnp.add, weights)
             sums = []
             for g in range(groups):
-                start = g * depth + pair * sixteen
+                start = pl.multiple_of(member * (at // 2) + g * depth + pair * sixteen, sixteen)
                 terms = [
-                    parts_ref[2 * k + member, start : start + sixteen, :].astype(jnp.float32) * weight
+                    parts_ref[k, pl.ds(start, sixteen), :].astype(jnp.float32) * weight
                     for k, weight in enumerate(weights)
                 ]
                 sums.append(functools.reduce(jnp.add, terms) * scale)
@@ -275,10 +278,11 @@
 
 
 def project(parts, own_up, came_up, own_proj, came_proj):
-    peers, rows_out, _ = parts.shape
+    chips, rows_out, _ = parts.shape
+    peers = chips * 2
     heads, latent, _ = own_up.shape
     columns = own_proj.shape[1]
-    tokens = rows_out // 16 * 16 // (latent // LANES) // heads
+    tokens = (rows_out - 16) // 2 // (latent // LANES) // heads
     vmem = pl.BlockSpec(memory_space=pltpu.VMEM)
     return pl.pallas_call(
         project_kernel,

time: 74.6 us -> 74.6 us (level)
  no operation moved by 1% of the time
where the time goes in v13:
time: 74.6 us; the launch traced here: 74.4 us
  blocking collectives  58.1 us (78%)
  Pallas kernels  11.5 us (15%)
  starting transfers between devices  3.75 us (5%)
  local copies, waits for them, and re-layouts  0.89 us (1%)
    all_to_all x1, blocking collectives, body(): lax.all_to_all(spread(queries, peers), ('chip', 'core'), 0, 0, tiled=True)  24.2 us
    all_to_all x1, blocking collectives, body(): parts = lax.all_to_all(mine, 'chip', 0, 0, tiled=True)  19.8 us
    all_to_all x1, blocking collectives, body(): terms = lax.all_to_all(terms, ('chip', 'core'), 0, 0, tiled=True)  14.2 us
    pallas_call x1, Pallas kernels, attend(): pl.pallas_call(functools.partial(attend_kernel, new_count=new_count), out...  8.64 us
    ppermute x1, starting transfers between devices, body(): came = lax.ppermute(cache, 'core', swap)  3.24 us
    pallas_call x1, Pallas kernels, project(): pl.pallas_call(project_kernel, out_shape=pltpu.VMEM((peers, tokens, colum...  2.11 us
  transfers between devices with their start and end apart: 3, of which 0 were waited for; matrix products, arithmetic and copies ran while one was open for 0% of the time, Pallas kernels for 12%

profile of v13, /device:TPU:1, one launch (start us, length us, event | category | flops | bytes accessed | tf_op | source)
XLA Modules:
  0.0 74.4 jit_solution(17653544432280443218)
XLA Ops:
  0.0 3.2 %collective-permute-start = (bf16[8,576,1024]{2,1,0:T(8,128)(2,1)}, bf16[8,576,1024]{2,1,0:T(8,128)(2,1)S(1)}, u32[]{:S(2)}, u32[]{:S(2)}) collective-permute-start(bf16[8,576,1024]{2,1,0:T(8,128)(2,1)} %bitcast.1), channel_id=1, source_target_pairs={{0,1},{1,0},{2,3},{3,2},{4,5},{5,4},{6,7},{7,6},{8,9},{9,8},{10,11... | collective-permute-start | bytes 28311560 | tf_op jit(solution)/shard_map/ppermute | solution.py:324
  3.2 0.0 copy-start.2
  3.2 0.9 %copy-done.2 = bf16[8,4,2,576]{3,2,1,0:T(2,128)(2,1)S(1)} copy-done((bf16[8,4,2,576]{3,2,1,0:T(2,128)(2,1)S(1)}, bf16[8,4,2,576]{3,2,1,0:T(2,128)(2,1)}, u32[]{:S(2)}) %copy-start.2) | copy-done | bytes 73752
  4.1 0.1 spread.1
  4.3 24.2 %all_to_all.15.query_ref = bf16[32,144,128]{2,1,0:T(8,128)(2,1)S(1)} all-to-all(bf16[32,144,128]{2,1,0:T(8,128)(2,1)S(1)} %spread.1), channel_id=1, replica_groups=mesh['batch'=8,'chip'=16,'core'=2] {'chip','core'}, dimensions={0} | all-to-all | bytes 2359296 | tf_op jit(solution)/shard_map/all_to_all | solution.py:325
  28.5 0.0 copy-start.1
  28.5 0.4 collective-permute-start.2
  28.9 0.1 collective-permute-start.1
  29.0 0.0 collective-permute-done.came_ref
  29.0 0.0 copy-start
  29.0 8.6 %attend.1 = bf16[16,272,128]{2,1,0:T(8,128)(2,1)S(1)} custom-call(s32[8]{0:T(128)} %far_lengths_ref.1, s32[8]{0:T(128)} %far_positions_ref.1, bf16[8,576,1024]{2,1,0:T(8,128)(2,1)} %bitcast.2, bf16[8,576,1024]{2,1,0:T(8,128)(2,1)S(1)} %collective-permute-done.came_ref, bf16[32,144,128]{2,1,0:T(8,128)(2,1)S(1)} %all_to_all.15.query_ref), custom_call_target="tpu_custom_call" | custom-call | flops 4563402752 | bytes 10551296 | tf_op jit(solution)/shard_map/attend/pallas_call | solution.py:206
  37.6 0.0 collective-permute-done.1.came_up_ref
  37.6 0.0 collective-permute-done.2.came_proj_ref
  37.7 19.8 %all_to_all.16.parts_ref = bf16[16,272,128]{2,1,0:T(8,128)(2,1)S(1)} all-to-all(bf16[16,272,128]{2,1,0:T(8,128)(2,1)S(1)} %attend.1), channel_id=1, replica_groups=mesh['batch'=8,'chip'=16,'core'=2] {'chip'}, dimensions={0} | all-to-all | bytes 2228224 | tf_op jit(solution)/shard_map/all_to_all | solution.py:331
  57.4 0.0 copy-done.1
  57.4 0.0 copy-done
  57.4 2.1 %project.1 = bf16[32,16,224]{2,1,0:T(8,128)(2,1)S(1)} custom-call(bf16[16,272,128]{2,1,0:T(8,128)(2,1)S(1)} %all_to_all.16.parts_ref, bf16[2,512,128]{2,1,0:T(8,128)(2,1)S(1)} %copy-done.1, bf16[2,512,128]{2,1,0:T(8,128)(2,1)S(1)} %collective-permute-done.1.came_up_ref, bf16[256,7168]{1,0:T(8,128)(2,1)S(1)} %copy-done, ...), custom_call_target="tpu_custom_call" | custom-call | tf_op jit(solution)/shard_map/project/pallas_call | solution.py:287
  59.5 14.2 %all_to_all.17.terms_ref = bf16[32,16,224]{2,1,0:T(8,128)(2,1)S(1)} all-to-all(bf16[32,16,224]{2,1,0:T(8,128)(2,1)S(1)} %project.1), channel_id=1, replica_groups=mesh['batch'=8,'chip'=16,'core'=2] {'chip','core'}, dimensions={0} | all-to-all | bytes 458752 | tf_op jit(solution)/shard_map/all_to_all | solution.py:333
  73.7 0.7 total.1
Async XLA Ops:
  0.0 29.0 %collective-permute-start = (bf16[8,576,1024]{2,1,0:T(8,128)(2,1)}, bf16[8,576,1024]{2,1,0:T(8,128)(2,1)S(1)}, u32[]{:S(2)}, u32[]{:S(2)}) collective-permute-start(bf16[8,576,1024]{2,1,0:T(8,128)(2,1)} %bitcast.1), channel_id=1, source_target_pairs={{0,1},{1,0},{2,3},{3,2},{4,5},{5,4},{6,7},{7,6},{8,9},{9,8},{10,11... | collective-permute-start | bytes 28311560 | tf_op jit(solution)/shard_map/ppermute | solution.py:324
  3.2 0.9 %copy-start.2 = (bf16[8,4,2,576]{3,2,1,0:T(2,128)(2,1)S(1)}, bf16[8,4,2,576]{3,2,1,0:T(2,128)(2,1)}, u32[]{:S(2)}) copy-start(bf16[8,4,2,576]{3,2,1,0:T(2,128)(2,1)} %query_ref.1) | copy-start | bytes 221188
  28.5 29.0 %copy-start.1 = (bf16[2,512,128]{2,1,0:T(8,128)(2,1)S(1)}, bf16[2,512,128]{2,1,0:T(8,128)(2,1)}, u32[]{:S(2)}) copy-start(bf16[2,512,128]{2,1,0:T(8,128)(2,1)} %own_up_ref) | copy-start | bytes 786436
  28.5 9.2 %collective-permute-start.2 = (bf16[256,7168]{1,0:T(8,128)(2,1)}, bf16[256,7168]{1,0:T(8,128)(2,1)S(1)}, u32[]{:S(2)}, u32[]{:S(2)}) collective-permute-start(bf16[256,7168]{1,0:T(8,128)(2,1)} %own_proj_ref), channel_id=1, source_target_pairs={{0,1},{1,0},{2,3},{3,2},{4,5},{5,4},{6,7},{7,6},{8,9},{9,8},{10,11... | collective-permute-start | bytes 11010056 | tf_op jit(solution)/shard_map/ppermute | solution.py:328
  28.9 8.8 %collective-permute-start.1 = (bf16[2,512,128]{2,1,0:T(8,128)(2,1)}, bf16[2,512,128]{2,1,0:T(8,128)(2,1)S(1)}, u32[]{:S(2)}, u32[]{:S(2)}) collective-permute-start(bf16[2,512,128]{2,1,0:T(8,128)(2,1)} %own_up_ref), channel_id=1, source_target_pairs={{0,1},{1,0},{2,3},{3,2},{4,5},{5,4},{6,7},{7,6},{8,9},{9,8},{10,11... | collective-permute-start | bytes 786440 | tf_op jit(solution)/shard_map/ppermute | solution.py:327
  29.0 28.4 %copy-start = (bf16[256,7168]{1,0:T(8,128)(2,1)S(1)}, bf16[256,7168]{1,0:T(8,128)(2,1)}, u32[]{:S(2)}) copy-start(bf16[256,7168]{1,0:T(8,128)(2,1)} %own_proj_ref) | copy-start | bytes 11010052

commit v14 on v13

--- a/solution.py
+++ b/solution.py
@@ -145,10 +145,16 @@
         queries.append(query.reshape(count, wide).astype(jnp.bfloat16))
 
     def score(row):
-        copies[2 * row].wait()
-        copies[2 * row + 1].wait()
-        scores = jnp.dot(queries[row], keys_ref[row], preferred_element_type=jnp.float32)
-        return scores
+        if row > 0:
+            copies[2 * row].wait()
+            copies[2 * row + 1].wait()
+            return jnp.dot(queries[row], keys_ref[row], preferred_element_type=jnp.float32)
+        halves = []
+        for side in range(2):
+            copies[side].wait()
+            keys = keys_ref[row, :, side * span : (side + 1) * span]
+            halves.append(jnp.dot(queries[row], keys, preferred_element_type=jnp.float32))
+        return jnp.concatenate(halves, axis=-1)
 
     sixteen = 2 * group
     at = column_groups * depth

time: 74.6 us -> 74.7 us (level)
  no operation moved by 1% of the time
where the time goes in v14:
time: 74.7 us; the launch traced here: 74.5 us
  blocking collectives  58.1 us (78%)
  Pallas kernels  11.7 us (16%)
  starting transfers between devices  3.75 us (5%)
  local copies, waits for them, and re-layouts  0.89 us (1%)
    all_to_all x1, blocking collectives, body(): lax.all_to_all(spread(queries, peers), ('chip', 'core'), 0, 0, tiled=True)  24.2 us
    all_to_all x1, blocking collectives, body(): parts = lax.all_to_all(mine, 'chip', 0, 0, tiled=True)  19.8 us
    all_to_all x1, blocking collectives, body(): terms = lax.all_to_all(terms, ('chip', 'core'), 0, 0, tiled=True)  14.1 us
    pallas_call x1, Pallas kernels, attend(): pl.pallas_call(functools.partial(attend_kernel, new_count=new_count), out...  8.8 us
    ppermute x1, starting transfers between devices, body(): came = lax.ppermute(cache, 'core', swap)  3.24 us
    pallas_call x1, Pallas kernels, project(): pl.pallas_call(project_kernel, out_shape=pltpu.VMEM((peers, tokens, colum...  2.11 us
  transfers between devices with their start and end apart: 3, of which 0 were waited for; matrix products, arithmetic and copies ran while one was open for 0% of the time, Pallas kernels for 12%

profile of v14, /device:TPU:1, one launch (start us, length us, event | category | flops | bytes accessed | tf_op | source)
XLA Modules:
  0.0 74.5 jit_solution(14026257442744453893)
XLA Ops:
  0.0 3.2 %collective-permute-start = (bf16[8,576,1024]{2,1,0:T(8,128)(2,1)}, bf16[8,576,1024]{2,1,0:T(8,128)(2,1)S(1)}, u32[]{:S(2)}, u32[]{:S(2)}) collective-permute-start(bf16[8,576,1024]{2,1,0:T(8,128)(2,1)} %bitcast.1), channel_id=1, source_target_pairs={{0,1},{1,0},{2,3},{3,2},{4,5},{5,4},{6,7},{7,6},{8,9},{9,8},{10,11... | collective-permute-start | bytes 28311560 | tf_op jit(solution)/shard_map/ppermute | solution.py:330
  3.2 0.0 copy-start.2
  3.2 0.9 %copy-done.2 = bf16[8,4,2,576]{3,2,1,0:T(2,128)(2,1)S(1)} copy-done((bf16[8,4,2,576]{3,2,1,0:T(2,128)(2,1)S(1)}, bf16[8,4,2,576]{3,2,1,0:T(2,128)(2,1)}, u32[]{:S(2)}) %copy-start.2) | copy-done | bytes 73752
  4.1 0.1 spread.1
  4.3 24.2 %all_to_all.15.query_ref = bf16[32,144,128]{2,1,0:T(8,128)(2,1)S(1)} all-to-all(bf16[32,144,128]{2,1,0:T(8,128)(2,1)S(1)} %spread.1), channel_id=1, replica_groups=mesh['batch'=8,'chip'=16,'core'=2] {'chip','core'}, dimensions={0} | all-to-all | bytes 2359296 | tf_op jit(solution)/shard_map/all_to_all | solution.py:331
  28.5 0.0 copy-start.1
  28.5 0.4 collective-permute-start.2
  28.9 0.1 collective-permute-start.1
  29.0 0.0 collective-permute-done.came_ref
  29.0 0.0 copy-start
  29.0 8.8 %attend.1 = bf16[16,272,128]{2,1,0:T(8,128)(2,1)S(1)} custom-call(s32[8]{0:T(128)} %far_lengths_ref.1, s32[8]{0:T(128)} %far_positions_ref.1, bf16[8,576,1024]{2,1,0:T(8,128)(2,1)} %bitcast.2, bf16[8,576,1024]{2,1,0:T(8,128)(2,1)S(1)} %collective-permute-done.came_ref, bf16[32,144,128]{2,1,0:T(8,128)(2,1)S(1)} %all_to_all.15.query_ref), custom_call_target="tpu_custom_call" | custom-call | flops 4563402752 | bytes 10551296 | tf_op jit(solution)/shard_map/attend/pallas_call | solution.py:212
  37.8 0.0 collective-permute-done.1.came_up_ref
  37.8 0.0 collective-permute-done.2.came_proj_ref
  37.8 19.8 %all_to_all.16.parts_ref = bf16[16,272,128]{2,1,0:T(8,128)(2,1)S(1)} all-to-all(bf16[16,272,128]{2,1,0:T(8,128)(2,1)S(1)} %attend.1), channel_id=1, replica_groups=mesh['batch'=8,'chip'=16,'core'=2] {'chip'}, dimensions={0} | all-to-all | bytes 2228224 | tf_op jit(solution)/shard_map/all_to_all | solution.py:337
  57.6 0.0 copy-done.1
  57.6 0.0 copy-done
  57.6 2.1 %project.1 = bf16[32,16,224]{2,1,0:T(8,128)(2,1)S(1)} custom-call(bf16[16,272,128]{2,1,0:T(8,128)(2,1)S(1)} %all_to_all.16.parts_ref, bf16[2,512,128]{2,1,0:T(8,128)(2,1)S(1)} %copy-done.1, bf16[2,512,128]{2,1,0:T(8,128)(2,1)S(1)} %collective-permute-done.1.came_up_ref, bf16[256,7168]{1,0:T(8,128)(2,1)S(1)} %copy-done, ...), custom_call_target="tpu_custom_call" | custom-call | tf_op jit(solution)/shard_map/project/pallas_call | solution.py:293
  59.7 14.1 %all_to_all.17.terms_ref = bf16[32,16,224]{2,1,0:T(8,128)(2,1)S(1)} all-to-all(bf16[32,16,224]{2,1,0:T(8,128)(2,1)S(1)} %project.1), channel_id=1, replica_groups=mesh['batch'=8,'chip'=16,'core'=2] {'chip','core'}, dimensions={0} | all-to-all | bytes 458752 | tf_op jit(solution)/shard_map/all_to_all | solution.py:339
  73.8 0.7 total.1
Async XLA Ops:
  0.0 29.0 %collective-permute-start = (bf16[8,576,1024]{2,1,0:T(8,128)(2,1)}, bf16[8,576,1024]{2,1,0:T(8,128)(2,1)S(1)}, u32[]{:S(2)}, u32[]{:S(2)}) collective-permute-start(bf16[8,576,1024]{2,1,0:T(8,128)(2,1)} %bitcast.1), channel_id=1, source_target_pairs={{0,1},{1,0},{2,3},{3,2},{4,5},{5,4},{6,7},{7,6},{8,9},{9,8},{10,11... | collective-permute-start | bytes 28311560 | tf_op jit(solution)/shard_map/ppermute | solution.py:330
  3.2 0.9 %copy-start.2 = (bf16[8,4,2,576]{3,2,1,0:T(2,128)(2,1)S(1)}, bf16[8,4,2,576]{3,2,1,0:T(2,128)(2,1)}, u32[]{:S(2)}) copy-start(bf16[8,4,2,576]{3,2,1,0:T(2,128)(2,1)} %query_ref.1) | copy-start | bytes 221188
  28.5 29.1 %copy-start.1 = (bf16[2,512,128]{2,1,0:T(8,128)(2,1)S(1)}, bf16[2,512,128]{2,1,0:T(8,128)(2,1)}, u32[]{:S(2)}) copy-start(bf16[2,512,128]{2,1,0:T(8,128)(2,1)} %own_up_ref) | copy-start | bytes 786436
  28.5 9.3 %collective-permute-start.2 = (bf16[256,7168]{1,0:T(8,128)(2,1)}, bf16[256,7168]{1,0:T(8,128)(2,1)S(1)}, u32[]{:S(2)}, u32[]{:S(2)}) collective-permute-start(bf16[256,7168]{1,0:T(8,128)(2,1)} %own_proj_ref), channel_id=1, source_target_pairs={{0,1},{1,0},{2,3},{3,2},{4,5},{5,4},{6,7},{7,6},{8,9},{9,8},{10,11... | collective-permute-start | bytes 11010056 | tf_op jit(solution)/shard_map/ppermute | solution.py:334
  28.9 8.9 %collective-permute-start.1 = (bf16[2,512,128]{2,1,0:T(8,128)(2,1)}, bf16[2,512,128]{2,1,0:T(8,128)(2,1)S(1)}, u32[]{:S(2)}, u32[]{:S(2)}) collective-permute-start(bf16[2,512,128]{2,1,0:T(8,128)(2,1)} %own_up_ref), channel_id=1, source_target_pairs={{0,1},{1,0},{2,3},{3,2},{4,5},{5,4},{6,7},{7,6},{8,9},{9,8},{10,11... | collective-permute-start | bytes 786440 | tf_op jit(solution)/shard_map/ppermute | solution.py:333
  29.0 28.6 %copy-start = (bf16[256,7168]{1,0:T(8,128)(2,1)S(1)}, bf16[256,7168]{1,0:T(8,128)(2,1)}, u32[]{:S(2)}) copy-start(bf16[256,7168]{1,0:T(8,128)(2,1)} %own_proj_ref) | copy-start | bytes 11010052

commit v15 on v13

--- a/solution.py
+++ b/solution.py
@@ -323,11 +323,10 @@
     cache = jnp.swapaxes(latent_cache, 1, 2)
     came = lax.ppermute(cache, "core", swap)
     query = lax.all_to_all(spread(queries, peers), ("chip", "core"), 0, 0, tiled=True)
-    query, value_up, out_proj = lax.optimization_barrier((query, value_up, out_proj))
+    mine = attend(lengths, positions, cache, came, query, new_count)
+    mine, value_up, out_proj = lax.optimization_barrier((mine, value_up, out_proj))
     came_up = lax.ppermute(value_up, "core", swap)
     came_proj = lax.ppermute(out_proj, "core", swap)
-    mine = attend(lengths, positions, cache, came, query, new_count)
-    mine, came_up, came_proj = lax.optimization_barrier((mine, came_up, came_proj))
     parts = lax.all_to_all(mine, "chip", 0, 0, tiled=True)
     terms = project(parts, value_up, came_up, out_proj, came_proj)
     terms = lax.all_to_all(terms, ("chip", "core"), 0, 0, tiled=True)

time: 74.6 us -> 80.4 us (1.078)
  blocking collectives: 58.1 us -> 37.5 us
  waiting for transfers between devices: 0.01 us -> 18.4 us
  Pallas kernels: 11.5 us -> 15.7 us
  starting transfers between devices: 3.75 us -> 7.62 us
    all_to_all x1 -> x0, blocking collectives: 19.8 us -> none  [body(): parts = lax.all_to_all(mine, 'chip', 0, 0, tiled=True)]
    all_to_all x0 -> x1, waiting for transfers between devices: none -> 15.9 us  [body(): parts = lax.all_to_all(mine, 'chip', 0, 0, tiled=True)]
    all_to_all x0 -> x1, starting transfers between devices: none -> 3.7 us  [body(): parts = lax.all_to_all(mine, 'chip', 0, 0, tiled=True)]
    pallas_call x1, Pallas kernels: 2.11 us -> 5.26 us  [project(): pl.pallas_call(project_kernel, out_shape=pltpu.VMEM((peers, tokens, colum...]
    ppermute x1, waiting for transfers between devices: 0.01 us -> 2.5 us  [body(): came_up = lax.ppermute(value_up, 'core', swap)]
    pallas_call x1, Pallas kernels: 8.64 us -> 9.65 us  [attend(): pl.pallas_call(functools.partial(attend_kernel, new_count=new_count), out...]
    all_to_all x1, blocking collectives: 14.2 us -> 13.3 us  [body(): terms = lax.all_to_all(terms, ('chip', 'core'), 0, 0, tiled=True)]
  transfers between devices with their start and end apart: 3 -> 4, of which waited for: 0 -> 2; matrix products, arithmetic and copies ran while one was open for 0% -> 0% of each run, Pallas kernels for 12% -> 0%
where the time goes in v15:
time: 80.4 us; the launch traced here: 80.1 us
  blocking collectives  37.5 us (47%)
  waiting for transfers between devices  18.4 us (23%)
  Pallas kernels  15.7 us (20%)
  starting transfers between devices  7.62 us (9%)
  local copies, waits for them, and re-layouts  0.89 us (1%)
    all_to_all x1, blocking collectives, body(): lax.all_to_all(spread(queries, peers), ('chip', 'core'), 0, 0, tiled=True)  24.2 us
    all_to_all x1, waiting for transfers between devices, body(): parts = lax.all_to_all(mine, 'chip', 0, 0, tiled=True)  15.9 us
    all_to_all x1, blocking collectives, body(): terms = lax.all_to_all(terms, ('chip', 'core'), 0, 0, tiled=True)  13.3 us
    pallas_call x1, Pallas kernels, attend(): pl.pallas_call(functools.partial(attend_kernel, new_count=new_count), out...  9.65 us
    pallas_call x1, Pallas kernels, project(): pl.pallas_call(project_kernel, out_shape=pltpu.VMEM((peers, tokens, colum...  5.26 us
    all_to_all x1, starting transfers between devices, body(): parts = lax.all_to_all(mine, 'chip', 0, 0, tiled=True)  3.7 us
    ppermute x1, starting transfers between devices, body(): came = lax.ppermute(cache, 'core', swap)  3.24 us
    ppermute x1, waiting for transfers between devices, body(): came_up = lax.ppermute(value_up, 'core', swap)  2.5 us
  transfers between devices with their start and end apart: 4, of which 2 were waited for; matrix products, arithmetic and copies ran while one was open for 0% of the time, Pallas kernels for 0%

profile of v15, /device:TPU:1, one launch (start us, length us, event | category | flops | bytes accessed | tf_op | source)
XLA Modules:
  0.0 80.1 jit_solution(1590952238976454509)
XLA Ops:
  0.0 3.2 %collective-permute-start = (bf16[8,576,1024]{2,1,0:T(8,128)(2,1)}, bf16[8,576,1024]{2,1,0:T(8,128)(2,1)S(1)}, u32[]{:S(2)}, u32[]{:S(2)}) collective-permute-start(bf16[8,576,1024]{2,1,0:T(8,128)(2,1)} %bitcast.1), channel_id=1, source_target_pairs={{0,1},{1,0},{2,3},{3,2},{4,5},{5,4},{6,7},{7,6},{8,9},{9,8},{10,11... | collective-permute-start | bytes 28311560 | tf_op jit(solution)/shard_map/ppermute | solution.py:324
  3.2 0.0 copy-start.1
  3.2 0.9 %copy-done.1 = bf16[8,4,2,576]{3,2,1,0:T(2,128)(2,1)S(1)} copy-done((bf16[8,4,2,576]{3,2,1,0:T(2,128)(2,1)S(1)}, bf16[8,4,2,576]{3,2,1,0:T(2,128)(2,1)}, u32[]{:S(2)}) %copy-start.1) | copy-done | bytes 73752
  4.1 0.1 spread.1
  4.3 24.2 %all_to_all.15.query_ref = bf16[32,144,128]{2,1,0:T(8,128)(2,1)S(1)} all-to-all(bf16[32,144,128]{2,1,0:T(8,128)(2,1)S(1)} %spread.1), channel_id=1, replica_groups=mesh['batch'=8,'chip'=16,'core'=2] {'chip','core'}, dimensions={0} | all-to-all | bytes 2359296 | tf_op jit(solution)/shard_map/all_to_all | solution.py:325
  28.5 0.0 copy-start
  28.5 0.0 collective-permute-done.came_ref
  28.5 9.6 %attend.1 = bf16[16,272,128]{2,1,0:T(8,128)(2,1)} custom-call(s32[8]{0:T(128)} %far_lengths_ref.1, s32[8]{0:T(128)} %far_positions_ref.1, bf16[8,576,1024]{2,1,0:T(8,128)(2,1)} %bitcast.2, bf16[8,576,1024]{2,1,0:T(8,128)(2,1)S(1)} %collective-permute-done.came_ref, bf16[32,144,128]{2,1,0:T(8,128)(2,1)S(1)} %all_to_all.15.query_ref), custom_call_target="tpu_custom_call" | custom-call | flops 4563402752 | bytes 10551296 | tf_op jit(solution)/shard_map/attend/pallas_call | solution.py:206
  38.1 0.5 collective-permute-start.2
  38.6 3.7 %all-to-all-start.1 = ((bf16[16,272,128]{2,1,0:T(8,128)(2,1)}), bf16[16,272,128]{2,1,0:T(8,128)(2,1)S(1)}, u32[]{:S(2)}, u32[]{:S(2)}) async-start(bf16[16,272,128]{2,1,0:T(8,128)(2,1)} %attend.1), calls=%async_computation.1 | async-start | bytes 2228224 | tf_op jit(solution)/shard_map/all_to_all | solution.py:330
  42.3 0.0 copy-done
  42.3 0.2 collective-permute-start.1
  42.5 2.5 %collective-permute-done.1.came_up_ref = bf16[2,512,128]{2,1,0:T(8,128)(2,1)S(1)} collective-permute-done((bf16[2,512,128]{2,1,0:T(8,128)(2,1)S(1)}, bf16[2,512,128]{2,1,0:T(8,128)(2,1)S(1)}, u32[]{:S(2)}, u32[]{:S(2)}) %collective-permute-start.1) | collective-permute-done | bytes 262176 | tf_op jit(solution)/shard_map/ppermute | solution.py:328
  45.0 15.9 %all-to-all-done.1.parts_ref = bf16[16,272,128]{2,1,0:T(8,128)(2,1)S(1)} async-done(((bf16[16,272,128]{2,1,0:T(8,128)(2,1)}), bf16[16,272,128]{2,1,0:T(8,128)(2,1)S(1)}, u32[]{:S(2)}, u32[]{:S(2)}) %all-to-all-start.1) | async-done | bytes 1114144 | tf_op jit(solution)/shard_map/all_to_all | solution.py:330
  60.9 0.0 collective-permute-done.2.came_proj_ref
  60.9 5.3 %project.1 = bf16[32,16,224]{2,1,0:T(8,128)(2,1)S(1)} custom-call(bf16[16,272,128]{2,1,0:T(8,128)(2,1)S(1)} %all-to-all-done.1.parts_ref, bf16[2,512,128]{2,1,0:T(8,128)(2,1)S(1)} %copy-done, bf16[2,512,128]{2,1,0:T(8,128)(2,1)S(1)} %collective-permute-done.1.came_up_ref, bf16[256,7168]{1,0:T(8,128)(2,1)} %own_proj_ref, ...), custom_call_target="tpu_custom_call" | custom-call | tf_op jit(solution)/shard_map/project/pallas_call | solution.py:287
  66.2 13.3 %all_to_all.16.terms_ref = bf16[32,16,224]{2,1,0:T(8,128)(2,1)S(1)} all-to-all(bf16[32,16,224]{2,1,0:T(8,128)(2,1)S(1)} %project.1), channel_id=1, replica_groups=mesh['batch'=8,'chip'=16,'core'=2] {'chip','core'}, dimensions={0} | all-to-all | bytes 458752 | tf_op jit(solution)/shard_map/all_to_all | solution.py:332
  79.5 0.7 total.1
Async XLA Ops:
  0.0 28.5 %collective-permute-start = (bf16[8,576,1024]{2,1,0:T(8,128)(2,1)}, bf16[8,576,1024]{2,1,0:T(8,128)(2,1)S(1)}, u32[]{:S(2)}, u32[]{:S(2)}) collective-permute-start(bf16[8,576,1024]{2,1,0:T(8,128)(2,1)} %bitcast.1), channel_id=1, source_target_pairs={{0,1},{1,0},{2,3},{3,2},{4,5},{5,4},{6,7},{7,6},{8,9},{9,8},{10,11... | collective-permute-start | bytes 28311560 | tf_op jit(solution)/shard_map/ppermute | solution.py:324
  3.2 0.9 %copy-start.1 = (bf16[8,4,2,576]{3,2,1,0:T(2,128)(2,1)S(1)}, bf16[8,4,2,576]{3,2,1,0:T(2,128)(2,1)}, u32[]{:S(2)}) copy-start(bf16[8,4,2,576]{3,2,1,0:T(2,128)(2,1)} %query_ref.1) | copy-start | bytes 221188
  28.5 13.9 %copy-start = (bf16[2,512,128]{2,1,0:T(8,128)(2,1)S(1)}, bf16[2,512,128]{2,1,0:T(8,128)(2,1)}, u32[]{:S(2)}) copy-start(bf16[2,512,128]{2,1,0:T(8,128)(2,1)} %own_up_ref) | copy-start | bytes 786436
  38.1 22.8 %collective-permute-start.2 = (bf16[256,7168]{1,0:T(8,128)(2,1)}, bf16[256,7168]{1,0:T(8,128)(2,1)}, u32[]{:S(2)}, u32[]{:S(2)}) collective-permute-start(bf16[256,7168]{1,0:T(8,128)(2,1)} %own_proj_ref), channel_id=1, source_target_pairs={{0,1},{1,0},{2,3},{3,2},{4,5},{5,4},{6,7},{7,6},{8,9},{9,8},{10,11... | collective-permute-start | bytes 11010056 | tf_op jit(solution)/shard_map/ppermute | solution.py:329
  38.6 22.3 %all-to-all-start.1 = ((bf16[16,272,128]{2,1,0:T(8,128)(2,1)}), bf16[16,272,128]{2,1,0:T(8,128)(2,1)S(1)}, u32[]{:S(2)}, u32[]{:S(2)}) async-start(bf16[16,272,128]{2,1,0:T(8,128)(2,1)} %attend.1), calls=%async_computation.1 | async-start | bytes 2228224 | tf_op jit(solution)/shard_map/all_to_all | solution.py:330
  42.3 2.7 %collective-permute-start.1 = (bf16[2,512,128]{2,1,0:T(8,128)(2,1)S(1)}, bf16[2,512,128]{2,1,0:T(8,128)(2,1)S(1)}, u32[]{:S(2)}, u32[]{:S(2)}) collective-permute-start(bf16[2,512,128]{2,1,0:T(8,128)(2,1)S(1)} %copy-done), channel_id=1, source_target_pairs={{0,1},{1,0},{2,3},{3,2},{4,5},{5,4},{6,7},{7,6},{8,9},{9,8},{10,11... | collective-permute-start | bytes 786440 | tf_op jit(solution)/shard_map/ppermute | solution.py:328
